TPU v7x, 32 devices: a whole 2x2x4 slice. The times are simulated.
32 devices in a mesh: rec: 4 (over z), tm: 8 (over y, x, core).
Axes of the slice: x: 2, y: 2, z: 4, core: 2. Of those that a mesh axis runs over, the one named last changes fastest.
Arguments:
- mel_frames: bfloat16 [4, 16384, 80], P('rec', 'tm'), may hold values from -6 to 6
- lengths: int32 [4, 4], P('rec'), may hold values from 1 to 8192, 16384 in all within a row
- w_first: float32 [3, 3, 256], replicated, may hold values from -2 to 2
- w_second: bfloat16 [2304, 256], P(('rec', 'tm')), may hold values from -0.125 to 0.125
- w_proj: bfloat16 [5120, 1024], P(('rec', 'tm')), may hold values from -0.078125 to 0.078125
- gain_attn: float32 [1024], replicated, may hold values from 0.5 to 1.5
- w_qkv: bfloat16 [1024, 3072], P(('rec', 'tm')), may hold values from -2 to 2
- w_out: bfloat16 [1024, 1024], P(('rec', 'tm')), may hold values from -0.1875 to 0.1875
- gain_conv: float32 [1024], replicated, may hold values from 0.5 to 1.5
- w_point_in: bfloat16 [1024, 2048], P(('rec', 'tm')), may hold values from -0.1875 to 0.1875
- w_depth: float32 [9, 1024], replicated, may hold values from -6 to 6
- w_point_out: bfloat16 [1024, 1024], P(('rec', 'tm')), may hold values from -0.375 to 0.375
- gain_out: float32 [1024], replicated, may hold values from 0.5 to 1.5
Outputs:
- encoded: bfloat16 [4, 4096, 1024], P('rec', 'tm')
Inputs may be any that keep to these rules, and one draw needn't show every extreme that they name: Each group's 4 lengths sum to 16384, and the largest of them is 8192.
All inputs are finite; a program needn't handle non-finite values.
Results may differ from a plain program's by a relative error of at most 0.024.
The roundings to bfloat16 on the way count: a program that leaves them out, or rounds other values in their place, can miss the bound.
Values may be sent and summed in bfloat16 or wider, within the bound.
No kernel may reach another device: no remote copies, remote signals or barrier semaphores. Data moves between devices by JAX's collectives and lax.ppermute only.
A program may use at most 128 MiB of HBM per device.

v0:
```python
import jax
import jax.numpy as jnp
from jax import lax
from jax.sharding import PartitionSpec as P

WIDTH = 1024
HEADS = 8
KERNEL = 9
WINDOW = 128
CONV_BLOCK = 64
HEAD_DIM = 128


NORM_EPSILON = 1e-05


def passed_along(block, axis, distance):
    devices = range(lax.axis_size(axis))
    route = [(i - distance, i) for i in devices if i - distance in devices]
    return lax.ppermute(block, axis, route)


def with_halo(block, sides, width):
    for axis, dim in sides:
        count = lax.axis_size(axis)
        forward = [(i, i + 1) for i in range(count - 1)]
        backward = [(target, source) for source, target in forward]
        low = lax.ppermute(
            lax.slice_in_dim(block, block.shape[dim] - width, None, axis=dim), axis, forward
        )
        high = lax.ppermute(lax.slice_in_dim(block, 0, width, axis=dim), axis, backward)
        block = jnp.concatenate([low, block, high], axis=dim)
    return block


def layer_norm(values, gain):
    row_mean = jnp.mean(values, axis=-1, keepdims=True)
    centred = values - row_mean
    variance = jnp.mean(centred * centred, axis=-1, keepdims=True)
    return centred * lax.rsqrt(variance + NORM_EPSILON) * gain


def segment_ids(positions, bounds, limit):
    counted = jnp.sum((positions[:, None] >= bounds[None, :-1]).astype(jnp.int32), axis=1)
    inside = (positions >= 0) & (positions < limit)
    return jnp.where(inside, counted, -1)


def conv_first(window, seg_rows, w_first):
    frame_count = (window.shape[0] - 1) // 2
    bins = window.shape[1]
    padded = jnp.pad(window.astype(jnp.float32), ((0, 0), (1, 1)))
    centre = seg_rows[1 : 2 * frame_count : 2]
    total = jnp.zeros((frame_count, bins // 2, w_first.shape[-1]), jnp.float32)
    for step_t in range(3):
        taken = padded[step_t : step_t + 2 * frame_count - 1 : 2]
        same_seg = (seg_rows[step_t : step_t + 2 * frame_count - 1 : 2] == centre).astype(
            jnp.float32
        )
        taken = taken * same_seg[:, None]
        for step_f in range(3):
            columns = taken[:, step_f : step_f + bins - 1 : 2]
            total = total + columns[:, :, None] * w_first[step_t, step_f][None, None, :]
    return jnp.maximum(total, 0.0).astype(jnp.bfloat16)


def conv_second(first, seg_first, w_second):
    frame_count = (first.shape[0] - 1) // 2
    channels = first.shape[2]
    quarter = first.shape[1] // 2
    padded = jnp.pad(first, ((0, 0), (1, 1), (0, 0)))
    centre = seg_first[1 : 2 * frame_count : 2]
    total = jnp.zeros((frame_count * quarter, w_second.shape[1]), jnp.float32)
    for step_t in range(3):
        taken = padded[step_t : step_t + 2 * frame_count - 1 : 2]
        same_seg = (seg_first[step_t : step_t + 2 * frame_count - 1 : 2] == centre).astype(
            jnp.bfloat16
        )
        taken = taken * same_seg[:, None, None]
        for step_f in range(3):
            columns = taken[:, step_f : step_f + 2 * quarter - 1 : 2].reshape(
                frame_count * quarter, channels
            )
            offset = (step_t * 3 + step_f) * channels
            total = total + jnp.dot(
                columns, w_second[offset : offset + channels], preferred_element_type=jnp.float32
            )
    return jnp.maximum(total, 0.0).astype(jnp.bfloat16).reshape(frame_count, quarter * channels)


def attend_block(q_block, kv_block, q_seg, k_seg):
    row_count = q_block.shape[0]
    span = kv_block.shape[0]
    reach = (span - row_count) // 2
    offsets = (
        jnp.arange(span, dtype=jnp.int32)[None, :]
        - jnp.arange(row_count, dtype=jnp.int32)[:, None]
        - reach
    )
    allowed = (jnp.abs(offsets) <= reach) & (k_seg[None, :] == q_seg[:, None])

    def one_head(head):
        start = head * HEAD_DIM
        q_head = lax.dynamic_slice_in_dim(q_block, start, HEAD_DIM, 1)
        k_head = lax.dynamic_slice_in_dim(kv_block, start, HEAD_DIM, 1)
        v_head = lax.dynamic_slice_in_dim(kv_block, WIDTH + start, HEAD_DIM, 1)
        scores = lax.dot_general(
            q_head, k_head, (((1,), (1,)), ((), ())), preferred_element_type=jnp.float32
        ) * HEAD_DIM ** (-0.5)
        scores = jnp.where(allowed, scores, -1e30)
        row_max = jnp.max(scores, axis=-1, keepdims=True)
        exped = jnp.where(allowed, jnp.exp(scores - row_max), 0.0)
        probabilities = (exped / jnp.sum(exped, axis=-1, keepdims=True)).astype(jnp.bfloat16)
        return jnp.dot(probabilities, v_head, preferred_element_type=jnp.float32).astype(
            jnp.bfloat16
        )

    per_head = lax.map(one_head, jnp.arange(HEADS, dtype=jnp.int32))
    return jnp.transpose(per_head, (1, 0, 2)).reshape(row_count, WIDTH)


def depthwise(gated_ext, seg_ext, seg_mid, w_depth):
    length = seg_mid.shape[0]
    total = jnp.zeros((length, gated_ext.shape[1]), jnp.float32)
    for tap_index in range(w_depth.shape[0]):
        same_seg = (seg_ext[tap_index : tap_index + length] == seg_mid).astype(jnp.float32)
        total = (
            total
            + gated_ext[tap_index : tap_index + length].astype(jnp.float32)
            * w_depth[tap_index][None, :]
            * same_seg[:, None]
        )
    return jax.nn.silu(total).astype(jnp.bfloat16)


def add_product(inputs, piece):
    return jnp.dot(inputs, piece, preferred_element_type=jnp.float32)


def on_device(
    mel_frames,
    lengths,
    w_first,
    w_second,
    w_proj,
    gain_attn,
    w_qkv,
    w_out,
    gain_conv,
    w_point_in,
    w_depth,
    w_point_out,
    gain_out,
):
    frames_dev = mel_frames.shape[1]
    tokens_dev = frames_dev // 4
    shards = lax.axis_size("tm")
    index = lax.axis_index("tm")
    frames_all = frames_dev * shards
    bounds = jnp.cumsum(lengths[0])
    local_mel = mel_frames[0]
    first_base = index * frames_dev
    second_full = lax.all_gather(w_second, ("rec", "tm"), axis=0, tiled=True)
    block_count = tokens_dev // CONV_BLOCK
    mel_edge = passed_along(local_mel[frames_dev - 3 :], "tm", 1)
    extended = jnp.concatenate([mel_edge, local_mel], axis=0)

    def sub_block(block):
        start = block * CONV_BLOCK
        window = lax.dynamic_slice_in_dim(extended, 4 * start, 4 * CONV_BLOCK + 3, 0)
        positions = first_base + 4 * start - 3 + jnp.arange(4 * CONV_BLOCK + 3, dtype=jnp.int32)
        seg_rows = segment_ids(positions, bounds, frames_all)
        first = conv_first(window, seg_rows, w_first)
        return conv_second(first, seg_rows[1::2], second_full)

    sub = lax.map(sub_block, jnp.arange(block_count, dtype=jnp.int32))
    sub = sub.reshape(tokens_dev, sub.shape[-1])
    hidden = add_product(sub, lax.all_gather(w_proj, ("rec", "tm"), axis=0, tiled=True))
    token_pos = index * tokens_dev + jnp.arange(tokens_dev, dtype=jnp.int32)
    token_seg = segment_ids(4 * token_pos, bounds, frames_all)
    key_pos = index * tokens_dev - WINDOW + jnp.arange(tokens_dev + 2 * WINDOW, dtype=jnp.int32)
    key_seg = segment_ids(4 * key_pos, bounds, frames_all)
    normed = layer_norm(hidden, gain_attn).astype(jnp.bfloat16)
    mixed = add_product(normed, lax.all_gather(w_qkv, ("rec", "tm"), axis=0, tiled=True)).astype(
        jnp.bfloat16
    )
    query = mixed[:, :WIDTH]
    keyval = with_halo(mixed[:, WIDTH:], (("tm", 0),), WINDOW)
    block_rows = min(512, tokens_dev)
    block = 0
    start = block * block_rows
    pieces = attend_block(query, keyval, token_seg, key_seg)
    attn_out = add_product(pieces, lax.all_gather(w_out, ("rec", "tm"), axis=0, tiled=True))
    attended = hidden + attn_out
    normed_conv = layer_norm(attended, gain_conv).astype(jnp.bfloat16)
    upward = add_product(normed_conv, lax.all_gather(w_point_in, ("rec", "tm"), axis=0, tiled=True))
    gated = (upward[:, :WIDTH] * jax.nn.sigmoid(upward[:, WIDTH:])).astype(jnp.bfloat16)
    reach = KERNEL // 2
    gated_ext = with_halo(gated, (("tm", 0),), KERNEL // 2)
    depth_pos = index * tokens_dev - reach + jnp.arange(tokens_dev + 2 * reach, dtype=jnp.int32)
    seg_ext = segment_ids(4 * depth_pos, bounds, frames_all)
    acted = depthwise(gated_ext, seg_ext, token_seg, w_depth)
    conv_out = add_product(acted, lax.all_gather(w_point_out, ("rec", "tm"), axis=0, tiled=True))
    combined = attended + conv_out
    return layer_norm(combined, gain_out).astype(jnp.bfloat16)[None]


def solution(mesh):
    placed = (
        P("rec", "tm", None),
        P("rec", None),
        P(),
        P(("rec", "tm"), None),
        P(("rec", "tm"), None),
        P(),
        P(("rec", "tm"), None),
        P(("rec", "tm"), None),
        P(),
        P(("rec", "tm"), None),
        P(),
        P(("rec", "tm"), None),
        P(),
    )
    return jax.shard_map(
        on_device, mesh=mesh, in_specs=placed, out_specs=P("rec", "tm", None), check_vma=False
    )
```

profile of v0, /device:TPU:1, one launch (start us, length us, event | category | flops | bytes accessed | tf_op | source)
XLA Modules:
  0.0 867.0 jit_solution(4612300970806927037)
XLA Ops:
  20.1 46.7 %all-gather.7.cloned.1.call-done = bf16[2304,256]{1,0:T(8,128)(2,1)} async-done(((bf16[72,256]{1,0:T(8,128)(2,1)}), bf16[2304,256]{1,0:T(8,128)(2,1)}) %all-gather.7.cloned.1.call-update) | async-done | bytes 1179664 | tf_op jit(solution)/shard_map/all_gather | solution.py:163
  67.4 684.3 %while.25 = (s32[]{:T(128)}, bf16[8,64,5120]{2,1,0:T(8,128)(2,1)}, s32[8]{0:T(128)}, bf16[2051,80]{1,0:T(8,128)(2,1)}, s32[]{:T(128)}, /*index=5*/s32[4]{0:T(128...) while((s32[]{:T(128)}, bf16[8,64,5120]{2,1,0:T(8,128)(2,1)}, ...), condition=%wide.region_3.4_spmd, body=%wide.region_1.3_spmd.sunk | while | flops 1543876352 | bytes 92566552 | solution.py:176
  79.2 7.7 maximum_convert_fusion.2
  90.6 6.9 slice.735
  103.3 4.9 slice.737
  111.9 4.8 slice.738
  123.6 4.9 slice.740
  132.3 4.8 slice.741
  144.0 4.9 slice.743
  164.7 7.7 maximum_convert_fusion.2
  176.1 6.9 slice.735
  188.9 4.9 slice.737
  197.5 4.8 slice.738
  209.2 4.9 slice.740
  217.8 4.8 slice.741
  229.5 4.9 slice.743
  250.3 7.7 maximum_convert_fusion.2
  261.6 6.9 slice.735
  274.4 4.9 slice.737
  283.0 4.8 slice.738
  294.8 4.9 slice.740
  303.4 4.8 slice.741
  315.1 4.9 slice.743
  335.9 7.7 maximum_convert_fusion.2
  347.2 6.9 slice.735
  360.0 4.9 slice.737
  368.6 4.8 slice.738
  380.3 4.9 slice.740
  388.9 4.8 slice.741
  400.6 4.9 slice.743
  421.4 7.7 maximum_convert_fusion.2
  432.8 6.9 slice.735
  445.5 4.9 slice.737
  454.1 4.8 slice.738
  465.8 4.9 slice.740
  474.5 4.8 slice.741
  486.1 4.9 slice.743
  506.9 7.7 maximum_convert_fusion.2
  518.3 6.9 slice.735
  531.1 4.9 slice.737
  539.6 4.8 slice.738
  551.4 4.9 slice.740
  560.0 4.8 slice.741
  571.7 4.9 slice.743
  592.4 7.7 maximum_convert_fusion.2
  603.8 6.9 slice.735
  616.5 4.9 slice.737
  625.1 4.8 slice.738
  636.8 4.9 slice.740
  645.5 4.8 slice.741
  657.2 4.9 slice.743
  677.9 7.7 maximum_convert_fusion.2
  689.3 6.9 slice.735
  702.1 4.9 slice.737
  710.6 4.8 slice.738
  722.4 4.9 slice.740
  731.0 4.8 slice.741
  742.7 4.9 slice.743
  751.7 10.0 %fusion.62 = (f32[512]{0:T(512)S(1)}, f32[512,1024]{1,0:T(8,128)S(1)}) fusion(bf16[512,5120]{1,0:T(8,128)(2,1)} %bitcast.115, bf16[5120,1024]{1,0:T(8,128)(2,1)} %all-gather.9.cloned.1.call-done), kind=kOutput, calls=%fused_computation.140 | convolution fusion | flops 5369232896 | bytes 17827840 | tf_op jit(solution)/shard_map/dot_general | solution.py:137
  762.4 6.6 convolution_convert_fusion.1
  778.8 7.2 collective-permute-done.2
  787.8 47.7 %while.26 = (s32[]{:T(128)}, bf16[8,512,128]{1,2,0:T(8,128)(2,1)}, s32[8]{0:T(128)S(1)}, bf16[512,1024]{1,0:T(8,128)(2,1)S(1)}, bf16[768,2048]{1,0:T(8,128)(2,1)...) while((s32[]{:T(128)}, bf16[8,512,128]{1,2,0:T(8,128)(2,1)}, ...), condition=%wide.region_11.12_spmd.clone, body=%wide.region_8.11_spmd.clone.sunk | while | flops 212401152 | bytes 5925630 | solution.py:118
  840.1 4.6 fusion.38
  852.2 6.0 fusion.64
  (638 shorter events, 449.2 us)
Async XLA Ops:
  6.5 60.9 %copy-start.7 = (f32[3,3,256]{2,1,0:T(4,128)S(1)}, f32[3,3,256]{2,1,0:T(4,128)}, u32[]{:S(2)}) copy-start(f32[3,3,256]{2,1,0:T(4,128)} %param.19) | copy-start | bytes 27652
  6.5 60.3 %all-gather.7.cloned.1.call-start = ((), (), s32[]{:S(2)}) async-start(), calls=%async_computation | async-start | bytes 1216512 | tf_op jit(solution)/shard_map/all_gather | solution.py:163
  7.3 744.4 %all-gather.9.cloned.1.call-start = ((), (), s32[]{:S(2)}) async-start(), calls=%async_computation.1 | async-start | bytes 10813440 | tf_op jit(solution)/shard_map/all_gather | solution.py:178
  8.0 754.1 %all-gather.11.cloned.1.call-start = ((), (), s32[]{:S(2)}) async-start(), calls=%async_computation.2 | async-start | bytes 6488064 | tf_op jit(solution)/shard_map/all_gather | solution.py:184
  8.7 826.8 %all-gather.13.cloned.1.call-start = ((), (), s32[]{:S(2)}) async-start(), calls=%async_computation.3 | async-start | bytes 2162688 | tf_op jit(solution)/shard_map/all_gather | solution.py:193
  9.3 830.5 %all-gather.15.cloned.1.call-start = ((), (), s32[]{:S(2)}) async-start(), calls=%async_computation.4 | async-start | bytes 4325376 | tf_op jit(solution)/shard_map/all_gather | solution.py:196
  9.9 840.1 %all-gather.17.cloned.1.call-start = ((), (), s32[]{:S(2)}) async-start(), calls=%async_computation.5 | async-start | bytes 2162688 | tf_op jit(solution)/shard_map/all_gather | solution.py:203
  11.2 7.9 collective-permute-start
  17.7 49.7 %copy-start.11 = (s32[3]{0:T(128)}, s32[3]{0:T(128)S(1)}, u32[]{:S(2)}) copy-start(s32[3]{0:T(128)S(1)} %slice_bitcast_fusion.1) | copy-start | bytes 40
  97.5 2.5 copy-start.2
  108.2 3.7 copy-start.1
  111.9 6.0 copy-start.4
  128.6 3.7 copy-start
  132.3 6.0 copy-start.3
  183.0 2.5 copy-start.2
  193.8 3.7 copy-start.1
  197.5 6.0 copy-start.4
  214.1 3.7 copy-start
  217.8 6.0 copy-start.3
  268.5 2.5 copy-start.2
  279.3 3.7 copy-start.1
  283.0 6.0 copy-start.4
  299.7 3.7 copy-start
  303.4 6.0 copy-start.3
  354.1 2.5 copy-start.2
  364.9 3.7 copy-start.1
  368.6 6.0 copy-start.4
  385.2 3.7 copy-start
  388.9 6.0 copy-start.3
  439.6 2.5 copy-start.2
  450.4 3.7 copy-start.1
  454.1 6.0 copy-start.4
  470.8 3.7 copy-start
  474.5 6.0 copy-start.3
  525.2 2.5 copy-start.2
  535.9 3.7 copy-start.1
  539.6 6.0 copy-start.4
  556.3 3.7 copy-start
  560.0 6.0 copy-start.3
  610.7 2.5 copy-start.2
  621.4 3.7 copy-start.1
  625.1 6.0 copy-start.4
  641.8 3.7 copy-start
  645.5 6.0 copy-start.3
  696.2 2.5 copy-start.2
  707.0 3.7 copy-start.1
  710.6 6.0 copy-start.4
  727.3 3.7 copy-start
  731.0 6.0 copy-start.3
  761.7 7.3 copy-start.6
  761.7 0.7 copy-start.14
  769.0 6.0 copy-start.5
  769.0 5.6 copy-start.10
  769.0 5.6 copy-start.12
  769.1 5.7 copy-start.8
  769.1 5.7 copy-start.9
  769.2 9.6 %collective-permute-start.1 = (bf16[128,2048]{1,0:T(8,128)(2,1)S(1)}, bf16[128,2048]{1,0:T(8,128)(2,1)S(1)}, u32[]{:S(2)}, u32[]{:S(2)}) collective-permute-start(bf16[128,2048]{1,0:T(8,128)(2,1)S(1)} %get-tuple-element.258), channel_id=1, source_target_pairs={{0,1},{1,2},{2,3},{3,4},{4,5},{5,6},{6,7},{8,9},{9,10},{10,11},{11... | collective-permute-start | bytes 1572872 | tf_op jit(solution)/shard_map/ppermute | solution.py:28
  772.7 13.3 %collective-permute-start.2 = (bf16[128,2048]{1,0:T(8,128)(2,1)S(1)}, bf16[128,2048]{1,0:T(8,128)(2,1)S(1)}, u32[]{:S(2)}, u32[]{:S(2)}) collective-permute-start(bf16[128,2048]{1,0:T(8,128)(2,1)S(1)} %get-tuple-element.259), channel_id=1, source_target_pairs={{1,0},{2,1},{3,2},{4,3},{5,4},{6,5},{7,6},{9,8},{10,9},{11,10},{12... | collective-permute-start | bytes 1572872 | tf_op jit(solution)/shard_map/ppermute | solution.py:31
  775.0 12.8 %slice-start = ((bf16[512,3072]{1,0:T(8,128)(2,1)}), bf16[512,1024]{1,0:T(8,128)(2,1)S(1)}, s32[]{:S(2)}) async-start(bf16[512,3072]{1,0:T(8,128)(2,1)} %copy-done.5), calls=%async_computation.6 | async-start | bytes 2097152 | tf_op jit(solution)/shard_map/slice | solution.py:187
  839.4 0.7 copy-start.15
  845.3 4.7 collective-permute-start.3
  847.2 5.0 collective-permute-start.4
  858.2 0.7 copy-start.13
Sparse Core Ops, SparseCore 0:
  10.3 56.5 all-gather.6
  69.7 85.4 all-gather.8
  158.0 68.0 all-gather.10
  228.9 54.8 all-gather.12
  286.5 60.8 all-gather.14
  350.1 54.9 all-gather.16
where the time goes:
time: 873 us; the launch traced here: 867 us
  local copies, waits for them, and re-layouts  455 us (52%)
  matrix products  201 us (23%)
  other arithmetic  106 us (12%)
  waiting for transfers between devices  63.2 us (7%)
  starting transfers between devices  14.7 us (2%)
  between operations  13.8 us (2%)
  loops' own time  12.6 us (1%)
    slice x72, local copies, waits for them, and re-layouts, conv_second(): taken[:, step_f:step_f + 2 * quarter - 1:2]  284 us
    dot_general x72, matrix products, conv_second(): jnp.dot(columns, w_second[offset:offset + channels], preferred_element_ty...  145 us
    convert_element_type x8, other arithmetic, conv_first(): return jnp.maximum(total, 0.0).astype(jnp.bfloat16)  61.5 us
    slice x72, local copies, waits for them, and re-layouts, conv_first(): columns = taken[:, step_f:step_f + bins - 1:2]  57.2 us
    reshape x72, local copies, waits for them, and re-layouts, conv_second(): taken[:, step_f:step_f + 2 * quarter - 1:2]  55.9 us
    all_gather x1, waiting for transfers between devices, on_device(): second_full = lax.all_gather(w_second, ('rec', 'tm'), axis=0, tiled=True)  46.7 us
    dot_general x5, matrix products, add_product(): return jnp.dot(inputs, piece, preferred_element_type=jnp.float32)  31 us
    mul x8, other arithmetic, conv_second(): taken = taken * same_seg[:, None, None]  23.7 us
  transfers between devices with their start and end apart: 11, of which 4 were waited for; matrix products, arithmetic and copies ran while one was open for 87% of the time, Pallas kernels for 0%

commit v1 on v0

v1 whole, which is shorter than its diff:
```python
import functools

import jax
import jax.numpy as jnp
import numpy as np
from jax import lax
from jax.experimental import pallas as pl
from jax.experimental.pallas import tpu as pltpu
from jax.sharding import PartitionSpec as P

WIDTH = 1024
HEADS = 8
HEAD_DIM = 128
KERNEL = 9
WINDOW = 128
CHANNELS = 256
NORM_EPSILON = 1e-05

EDGE = 16
HALO = WINDOW + EDGE
COLS = 256


def segment_of(positions, lengths, limit):
    counted = jnp.zeros(positions.shape, jnp.int32)
    bound = 0
    for k in range(len(lengths) - 1):
        bound = bound + lengths[k]
        counted = counted + (positions >= bound).astype(jnp.int32)
    return jnp.where((positions >= 0) & (positions < limit), counted, -1)


def layer_norm(values, gain):
    row_mean = jnp.mean(values, axis=-1, keepdims=True)
    centred = values - row_mean
    variance = jnp.mean(centred * centred, axis=-1, keepdims=True)
    return centred * lax.rsqrt(variance + NORM_EPSILON) * gain


def exchange(block, axis, distance):
    size = lax.axis_size(axis)
    return lax.ppermute(block, axis, [(i, i ^ distance) for i in range(size)])


def bit_groups():
    groups = []
    for axis, lowest in (("rec", 1), ("tm", 2)):
        bits = []
        bit = lowest
        while bit < lax.axis_size(axis):
            bits.append(bit)
            bit *= 2
        groups += [(axis, bits[k : k + 2]) for k in range(0, len(bits), 2)]
    return groups + [("tm", [1])]


def distances(bits):
    return [0] + [bits[0]] if len(bits) == 1 else [0, bits[0], bits[1], bits[0] + bits[1]]


def can_exchange():
    return all(
        lax.axis_size(axis) & (lax.axis_size(axis) - 1) == 0 and lax.axis_size(axis) > 1
        for axis in ("rec", "tm")
    )


def gather_ordered(block):
    if not can_exchange():
        return lax.all_gather(block, ("rec", "tm"), axis=0, tiled=True)
    groups = bit_groups()
    names = []
    rows = block.shape[0]
    held = block[None]
    for axis, bits in groups:
        got = [held] + [exchange(held, axis, d) for d in distances(bits)[1:]]
        me = lax.axis_index(axis)
        for at, bit in enumerate(bits):
            high = (me & bit) != 0
            got = [
                jnp.where(high, got[k ^ (1 << at)], got[k]) for k in range(len(got))
            ]
        held = jnp.concatenate(got, axis=0)
        names = [(axis, bit) for bit in reversed(bits)] + names
    wanted = []
    for axis in ("rec", "tm"):
        wanted += sorted((n for n in names if n[0] == axis), key=lambda n: -n[1])
    order = [names.index(n) for n in wanted]
    dims = held.reshape((2,) * len(names) + block.shape)
    dims = jnp.transpose(dims, order + [len(names), len(names) + 1])
    return dims.reshape((-1,) + block.shape[1:])


def gather_unordered(block):
    groups = bit_groups()
    held = block[None]
    held_bits = []
    for axis, bits in groups[:-2]:
        got = [held] + [exchange(held, axis, d) for d in distances(bits)[1:]]
        held = jnp.concatenate(got, axis=0)
        held_bits = held_bits + [(axis, bit) for bit in bits]
    axis, bits = groups[-2]
    parts = [(held, [])]
    for d in distances(bits)[1:]:
        parts.append((exchange(held, axis, d), [(axis, d)]))
    axis, bits = groups[-1]
    parts += [(exchange(part, axis, 1), far + [(axis, 1)]) for part, far in parts]
    return parts, held_bits


BINS = 41


def prepare_kernel(limit, info_ref, quads_ref, lane_ref, w_ref, patches_ref, taps_ref):
    base = info_ref[0]
    lengths = [info_ref[1 + k] for k in range(4)]
    tokens = quads_ref.shape[0]
    wide = quads_ref.shape[1]
    source = lax.broadcasted_iota(jnp.int32, (wide, COLS), 0)
    token = lax.broadcasted_iota(jnp.int32, (tokens, COLS), 0)
    own = segment_of(base + 4 * (token - HALO), lengths, limit)
    frame = lane_ref[6:7, :]
    for a in range(3):
        middle = segment_of(base + 4 * (token - HALO) + 2 * a - 2, lengths, limit)
        there = segment_of(base + 4 * (token - HALO) + 2 * a - 3 + frame, lengths, limit)
        same = (middle == own) & (there == middle)
        for h in range(2):
            chosen = (source == lane_ref[2 * a + h : 2 * a + h + 1, :]).astype(jnp.float32)
            made = jnp.dot(
                quads_ref[...], chosen.astype(jnp.bfloat16), preferred_element_type=jnp.float32
            )
            patches_ref[a, h] = jnp.where(same, made, 0.0).astype(jnp.bfloat16)

    row = lax.broadcasted_iota(jnp.int32, (COLS, CHANNELS), 0)
    group = jnp.zeros((COLS, CHANNELS), jnp.int32)
    for k in range(1, 7):
        group = group + (row >= BINS * k).astype(jnp.int32)
    at_bin = row - BINS * group
    spread = []
    for b in range(3):
        total = jnp.zeros((COLS, CHANNELS), jnp.float32)
        for a in range(3):
            tap = w_ref[3 * a + b : 3 * a + b + 1, :]
            high = tap.astype(jnp.bfloat16).astype(jnp.float32)
            total = jnp.where(group == a, high, total)
            total = jnp.where(group == 3 + a, tap - high, total)
        spread.append(total)
    for f in range(20):
        total = jnp.zeros((COLS, CHANNELS), jnp.float32)
        for b in range(3):
            total = jnp.where(at_bin == 2 * f + b, spread[b], total)
        taps_ref[:, f * CHANNELS : (f + 1) * CHANNELS] = total.astype(jnp.bfloat16)


def prepare(info, mel, w_first, tokens, limit):
    bins = mel.shape[1]
    reach = 4 * (HALO + EDGE)
    tm = lax.axis_size("tm")
    forward = [(i, i + 1) for i in range(tm - 1)]
    backward = [(i + 1, i) for i in range(tm - 1)]
    low = lax.ppermute(mel[mel.shape[0] - reach :], "tm", forward)
    high = lax.ppermute(mel[:reach], "tm", backward)
    quads = jnp.concatenate([low, mel, high], axis=0).reshape(-1, 4 * bins)
    count = tokens + 2 * HALO
    quads = jnp.concatenate(
        [quads[EDGE - 1 : EDGE - 1 + count], quads[EDGE : EDGE + count]], axis=1
    )
    lane = np.arange(COLS)
    frame, at_bin = lane // BINS % 3, lane % BINS
    used = lane < 6 * BINS
    picks = np.full((8, COLS), -1, np.int32)
    for a in range(3):
        for h in range(2):
            wanted = at_bin - 1 + 40 * h
            place = bins * (2 * a + frame + 1) + wanted
            picks[2 * a + h] = np.where(used & (wanted >= 0), place, -1)
    picks[6] = frame
    whole = pl.BlockSpec(memory_space=pltpu.VMEM)
    return pl.pallas_call(
        functools.partial(prepare_kernel, limit),
        out_shape=(
            jax.ShapeDtypeStruct((3, 2, count, COLS), jnp.bfloat16),
            jax.ShapeDtypeStruct((COLS, 20 * CHANNELS), jnp.bfloat16),
        ),
        in_specs=[pl.BlockSpec(memory_space=pltpu.SMEM)] + [whole] * 3,
        out_specs=(whole, whole),
        compiler_params=pltpu.CompilerParams(vmem_limit_bytes=24 * 1024 * 1024),
        cost_estimate=pl.CostEstimate(
            flops=12 * count * 768 * COLS, bytes_accessed=6 * 1024 * 1024, transcendentals=0
        ),
        name="prepare",
    )(info, quads, jnp.asarray(picks), w_first.reshape(9, CHANNELS))


def conv_kernel(begin, count, a_ref, b_ref, w_ref, out_ref, first):
    tokens = out_ref.shape[0]
    rows_step = tokens // 2

    @pl.loop(0, 2)
    def _(r):
        rows = pl.ds(pl.multiple_of(r * rows_step, 16), rows_step)
        for a in range(3):
            for i in range(2 * count + 1):
                at = 2 * begin - 1 + i
                place = slice(i * COLS, (i + 1) * COLS)
                if at < 0:
                    first[a, :, place] = jnp.zeros((rows_step, COLS), jnp.bfloat16)
                    continue
                half, col = divmod(at, 20)
                made = jnp.dot(
                    a_ref[a, half, rows, :],
                    b_ref[:, col * COLS : (col + 1) * COLS],
                    preferred_element_type=jnp.float32,
                )
                first[a, :, place] = jnp.maximum(made, 0.0).astype(jnp.bfloat16)
        for t in range(count):
            total = None
            for a in range(3):
                made = jnp.dot(
                    first[a, :, 2 * t * COLS : (2 * t + 3) * COLS],
                    w_ref[a],
                    preferred_element_type=jnp.float32,
                )
                total = made if total is None else total + made
            out_ref[rows, t * COLS : (t + 1) * COLS] = jnp.maximum(total, 0.0).astype(jnp.bfloat16)


def subsample(patches, taps, w_second):
    tokens = patches.shape[2]
    count = 4
    weights = w_second.reshape(3, 3 * COLS, COLS)
    whole = pl.BlockSpec(memory_space=pltpu.VMEM)
    flops = 2 * tokens * COLS * COLS * (3 * (2 * count + 1) + 9 * count)
    pieces = []
    for begin in range(0, 20, count):
        pieces.append(
            pl.pallas_call(
                functools.partial(conv_kernel, begin, count),
                out_shape=jax.ShapeDtypeStruct((tokens, count * CHANNELS), jnp.bfloat16),
                in_specs=[whole] * 3,
                out_specs=whole,
                scratch_shapes=[
                    pltpu.VMEM((3, tokens // 2, (2 * count + 1) * COLS), jnp.bfloat16)
                ],
                compiler_params=pltpu.CompilerParams(vmem_limit_bytes=20 * 1024 * 1024),
                cost_estimate=pl.CostEstimate(
                    flops=flops, bytes_accessed=8 * 1024 * 1024, transcendentals=0
                ),
                name="subsample",
            )(patches, taps, weights)
        )
    return pieces


def project_kernel(places, held_bits, info_ref, gain_ref, *rest):
    subs = rest[:5]
    sources = rest[5 : 5 + len(places)]
    mid_ref, normed_ref, weights, hidden, sem = rest[5 + len(places) :]
    rec, tm, tm_size = info_ref[5], info_ref[6], info_ref[7]

    rows = sources[0].shape[-2]
    if held_bits is None:
        pltpu.make_async_copy(sources[0], weights, sem).start()
    else:
        for source, far in zip(sources, places):
            far_rec = sum(d for axis, d in far if axis == "rec")
            far_tm = sum(d for axis, d in far if axis == "tm")
            for slot in range(1 << len(held_bits)):
                own_rec, own_tm = far_rec, far_tm
                for k, (axis, bit) in enumerate(held_bits):
                    if slot >> k & 1:
                        own_rec += bit if axis == "rec" else 0
                        own_tm += bit if axis == "tm" else 0
                owner = (rec ^ own_rec) * tm_size + (tm ^ own_tm)
                place = pl.ds(pl.multiple_of(owner * rows, 16), rows)
                pltpu.make_async_copy(source.at[slot], weights.at[place, :], sem).start()
    pltpu.make_async_copy(weights, weights, sem).wait()

    depth = weights.shape[0] // len(subs)

    @pl.loop(0, WIDTH // COLS)
    def _(n):
        here = pl.ds(pl.multiple_of(n * COLS, COLS), COLS)
        total = None
        for piece, sub in enumerate(subs):
            made = jnp.dot(
                sub[...],
                weights[piece * depth : (piece + 1) * depth, here],
                preferred_element_type=jnp.float32,
            )
            total = made if total is None else total + made
        hidden[:, here] = total

    gain = gain_ref[...]
    chunk = 160

    @pl.loop(0, hidden.shape[0] // chunk)
    def _(r):
        rows = pl.ds(pl.multiple_of(r * chunk, chunk), chunk)
        normed_ref[rows, :] = layer_norm(hidden[rows, :], gain).astype(jnp.bfloat16)

    mid_ref[...] = hidden[WINDOW : WINDOW + mid_ref.shape[0], :]


def project(info, gain, subs, sources, places, held_bits, tokens):
    rows_all = tokens + 2 * HALO
    rows_mid = tokens + 2 * EDGE
    whole = pl.BlockSpec(memory_space=pltpu.VMEM)
    depth = sum(sub.shape[1] for sub in subs)
    return pl.pallas_call(
        functools.partial(project_kernel, places, held_bits),
        out_shape=(
            jax.ShapeDtypeStruct((rows_mid, WIDTH), jnp.float32),
            jax.ShapeDtypeStruct((rows_all, WIDTH), jnp.bfloat16),
        ),
        in_specs=[pl.BlockSpec(memory_space=pltpu.SMEM)]
        + [whole] * 6
        + [pl.BlockSpec(memory_space=pl.ANY)] * len(sources),
        out_specs=(whole, whole),
        scratch_shapes=[
            pltpu.VMEM((depth, WIDTH), jnp.bfloat16),
            pltpu.VMEM((rows_all, WIDTH), jnp.float32),
            pltpu.SemaphoreType.DMA(()),
        ],
        compiler_params=pltpu.CompilerParams(vmem_limit_bytes=34 * 1024 * 1024),
        cost_estimate=pl.CostEstimate(
            flops=2 * rows_all * depth * WIDTH, bytes_accessed=24 * 1024 * 1024, transcendentals=0
        ),
        name="project",
    )(info, gain, *subs, *sources)


def pack_kernel(pieces, *refs):
    out_ref = refs[-1]
    at = 0
    for source, first in pieces:
        rows = refs[source].shape[0]
        out_ref[at : at + rows, :] = refs[source][:, first : first + WIDTH]
        at += rows


def pack(arrays):
    pieces = [
        (k, first) for k, array in enumerate(arrays) for first in range(0, array.shape[1], WIDTH)
    ]
    if any(array.shape[0] % 16 for array in arrays):
        return jnp.concatenate([arrays[k][:, c : c + WIDTH] for k, c in pieces], axis=0)
    rows = sum(arrays[k].shape[0] for k, _ in pieces)
    whole = pl.BlockSpec(memory_space=pltpu.VMEM)
    return pl.pallas_call(
        functools.partial(pack_kernel, pieces),
        out_shape=jax.ShapeDtypeStruct((rows, WIDTH), jnp.bfloat16),
        in_specs=[whole] * len(arrays),
        out_specs=whole,
        compiler_params=pltpu.CompilerParams(vmem_limit_bytes=4 * 1024 * 1024),
        cost_estimate=pl.CostEstimate(
            flops=0, bytes_accessed=4 * rows * WIDTH, transcendentals=0
        ),
        name="pack",
    )(*arrays)


def block_kernel(
    tokens,
    limit,
    plan,
    count,
    info_ref,
    hidden_ref,
    normed_ref,
    gain_conv_ref,
    depth_ref,
    gain_out_ref,
    *rest,
):
    sources = rest[:count]
    out_ref = rest[count]
    scratch = rest[count + 1 :]
    buffers = scratch[: len(plan)]
    keys, values, queries, context, attended, gated, masks, biases, sems = scratch[len(plan) :]
    rows_mid = tokens + 2 * EDGE
    mid = slice(WINDOW, WINDOW + rows_mid)
    copies = []
    for at, (source, offset, rows) in enumerate(plan):
        copies.append(
            pltpu.make_async_copy(
                sources[source].at[:, pl.ds(offset, rows), :], buffers[at], sems.at[at]
            )
        )
    for copy in copies:
        copy.start()
    base = info_ref[0]
    lengths = [info_ref[1 + k] for k in range(4)]

    def columns(at, n):
        part = buffers[at][:, :, pl.ds(pl.multiple_of(n * COLS, COLS), COLS)]
        return part.reshape(-1, COLS)

    def here(n):
        return pl.ds(pl.multiple_of(n * COLS, COLS), COLS)

    blocks = []
    at_row = 0
    while at_row < rows_mid:
        size = 128 + (EDGE if at_row == 0 or at_row + 128 + EDGE == rows_mid else 0)
        blocks.append((at_row, size))
        at_row += size

    row = lax.broadcasted_iota(jnp.int32, (tokens, HEAD_DIM), 0)
    own = segment_of(base + 4 * row, lengths, limit)
    for k in range(KERNEL):
        there = segment_of(base + 4 * (row + k - KERNEL // 2), lengths, limit)
        masks[k] = (there == own).astype(jnp.float32)
    for at, (start, size) in enumerate(blocks):
        span = size + 2 * WINDOW
        q_row = lax.broadcasted_iota(jnp.int32, (size, 1), 0)
        k_row = lax.broadcasted_iota(jnp.int32, (1, span), 1)
        q_seg = segment_of(base + 4 * (q_row + start - EDGE), lengths, limit)
        k_seg = segment_of(base + 4 * (k_row + start - HALO), lengths, limit)
        apart = k_row - q_row
        allowed = (apart >= 0) & (apart <= 2 * WINDOW) & (q_seg == k_seg)
        biases[at, 0:size, 0:span] = jnp.where(allowed, 0.0, -1e30)
    for head in range(HEADS):
        values[:, (2 * head + 1) * HEAD_DIM : (2 * head + 2) * HEAD_DIM] = jnp.ones(
            (values.shape[0], HEAD_DIM), jnp.bfloat16
        )

    copies[0].wait()

    @pl.loop(0, WIDTH // COLS)
    def _(n):
        queries[:, here(n)] = jnp.dot(
            normed_ref[mid, :], columns(0, n), preferred_element_type=jnp.float32
        ).astype(jnp.bfloat16)

    copies[1].wait()

    @pl.loop(0, WIDTH // COLS)
    def _(n):
        keys[:, here(n)] = jnp.dot(
            normed_ref[...], columns(1, n), preferred_element_type=jnp.float32
        ).astype(jnp.bfloat16)

    copies[2].wait()

    @pl.loop(0, WIDTH // COLS)
    def _(n):
        made = jnp.dot(
            normed_ref[...], columns(2, n), preferred_element_type=jnp.float32
        ).astype(jnp.bfloat16)
        for k in range(COLS // HEAD_DIM):
            lanes = pl.ds(pl.multiple_of(2 * n * COLS + 2 * k * HEAD_DIM, HEAD_DIM), HEAD_DIM)
            values[:, lanes] = made[:, k * HEAD_DIM : (k + 1) * HEAD_DIM]

    scale = HEAD_DIM**-0.5 * 1.4426950408889634

    @pl.loop(0, HEADS)
    def _(head):
        lanes = pl.ds(pl.multiple_of(head * HEAD_DIM, HEAD_DIM), HEAD_DIM)
        wide = pl.ds(pl.multiple_of(head * 2 * HEAD_DIM, 2 * HEAD_DIM), 2 * HEAD_DIM)
        for at, (start, size) in enumerate(blocks):
            span = size + 2 * WINDOW
            scores = lax.dot_general(
                queries[start : start + size, lanes],
                keys[start : start + span, lanes],
                (((1,), (1,)), ((), ())),
                preferred_element_type=jnp.float32,
            )
            scores = scores * scale + biases[at, 0:size, 0:span]
            exped = jnp.exp2(scores - jnp.max(scores, axis=-1, keepdims=True))
            mixed = jnp.dot(
                exped.astype(jnp.bfloat16),
                values[start : start + span, wide],
                preferred_element_type=jnp.float32,
            )
            context[start : start + size, lanes] = (
                mixed[:, :HEAD_DIM] / mixed[:, HEAD_DIM:]
            ).astype(jnp.bfloat16)

    copies[3].wait()

    @pl.loop(0, WIDTH // COLS)
    def _(n):
        attended[:, here(n)] = hidden_ref[:, here(n)] + jnp.dot(
            context[...], columns(3, n), preferred_element_type=jnp.float32
        )

    gain_c = gain_conv_ref[...]
    step_rows = rows_mid // 2

    @pl.loop(0, 2)
    def _(r):
        rows = pl.ds(pl.multiple_of(r * step_rows, 16), step_rows)
        queries[rows, :] = layer_norm(attended[rows, :], gain_c).astype(jnp.bfloat16)

    copies[4].wait()
    copies[5].wait()

    @pl.loop(0, WIDTH // COLS)
    def _(n):
        value = jnp.dot(queries[...], columns(4, n), preferred_element_type=jnp.float32)
        gate = jnp.dot(queries[...], columns(5, n), preferred_element_type=jnp.float32)
        made = (value * jax.nn.sigmoid(gate)).astype(jnp.bfloat16).astype(jnp.float32)
        for k in range(COLS // HEAD_DIM):
            gated[n * (COLS // HEAD_DIM) + k] = made[:, k * HEAD_DIM : (k + 1) * HEAD_DIM]

    @pl.loop(0, WIDTH // HEAD_DIM)
    def _(n):
        lanes = pl.ds(pl.multiple_of(n * HEAD_DIM, HEAD_DIM), HEAD_DIM)
        total = jnp.zeros((tokens, HEAD_DIM), jnp.float32)
        for k in range(KERNEL):
            begin = EDGE - KERNEL // 2 + k
            tap = gated[n, begin : begin + tokens, :] * depth_ref[k : k + 1, lanes]
            total = total + (tap if k == KERNEL // 2 else tap * masks[k])
        context[0:tokens, lanes] = (total * jax.nn.sigmoid(total)).astype(jnp.bfloat16)

    copies[6].wait()

    @pl.loop(0, WIDTH // COLS)
    def _(n):
        attended[EDGE : EDGE + tokens, here(n)] += jnp.dot(
            context[0:tokens, :], columns(6, n), preferred_element_type=jnp.float32
        )

    gain_o = gain_out_ref[...]

    @pl.loop(0, tokens // 128)
    def _(r):
        rows = pl.ds(pl.multiple_of(r * 128, 128), 128)
        taken = attended[pl.ds(pl.multiple_of(EDGE + r * 128, 16), 128), :]
        out_ref[rows, :] = layer_norm(taken, gain_o).astype(jnp.bfloat16)


def conformer_block(info, hidden, normed, sources, plan, gain_conv, w_depth, gain_out, limit):
    rows_all = normed.shape[0]
    rows_mid = hidden.shape[0]
    tokens = rows_mid - 2 * EDGE
    whole = pl.BlockSpec(memory_space=pltpu.VMEM)
    scratch = [
        pltpu.VMEM((sources[source].shape[0], rows, WIDTH), jnp.bfloat16)
        for source, _, rows in plan
    ]
    scratch += [
        pltpu.VMEM((rows_all, WIDTH), jnp.bfloat16),
        pltpu.VMEM((rows_all, 2 * WIDTH), jnp.bfloat16),
        pltpu.VMEM((rows_mid, WIDTH), jnp.bfloat16),
        pltpu.VMEM((rows_mid, WIDTH), jnp.bfloat16),
        pltpu.VMEM((rows_mid, WIDTH), jnp.float32),
        pltpu.VMEM((WIDTH // HEAD_DIM, rows_mid, HEAD_DIM), jnp.float32),
        pltpu.VMEM((KERNEL, tokens, HEAD_DIM), jnp.float32),
        pltpu.VMEM((4, 128 + EDGE, 512), jnp.float32),
        pltpu.SemaphoreType.DMA((len(plan),)),
    ]
    flops = 2 * rows_all * WIDTH * 2 * WIDTH + 2 * rows_mid * WIDTH * WIDTH * 5
    return pl.pallas_call(
        functools.partial(block_kernel, tokens, limit, plan, len(sources)),
        out_shape=jax.ShapeDtypeStruct((tokens, WIDTH), jnp.bfloat16),
        in_specs=[pl.BlockSpec(memory_space=pltpu.SMEM)]
        + [whole] * 5
        + [pl.BlockSpec(memory_space=pl.ANY)] * len(sources),
        out_specs=whole,
        scratch_shapes=scratch,
        compiler_params=pltpu.CompilerParams(vmem_limit_bytes=44 * 1024 * 1024),
        cost_estimate=pl.CostEstimate(
            flops=flops, bytes_accessed=24 * 1024 * 1024, transcendentals=4 * 1024 * 1024
        ),
        name="conformer_block",
    )(info, hidden, normed, gain_conv, w_depth, gain_out, *sources)


def on_device(
    mel_frames,
    lengths,
    w_first,
    w_second,
    w_proj,
    gain_attn,
    w_qkv,
    w_out,
    gain_conv,
    w_point_in,
    w_depth,
    w_point_out,
    gain_out,
):
    tokens = mel_frames.shape[1] // 4
    limit = mel_frames.shape[1] * lax.axis_size("tm")
    base = lax.axis_index("tm") * mel_frames.shape[1]
    info = jnp.concatenate(
        [
            jnp.reshape(base, (1,)),
            lengths[0],
            jnp.stack([lax.axis_index("rec"), lax.axis_index("tm")]),
            jnp.full((1,), lax.axis_size("tm"), jnp.int32),
        ]
    ).astype(jnp.int32)

    packed = pack([w_qkv, w_out, w_point_in, w_point_out])
    gathered = lax.all_gather(packed, ("rec", "tm"), axis=0, tiled=False)

    w_second_all = gather_ordered(w_second)
    if can_exchange() and w_proj.shape[0] % 16 == 0:
        parts, held_bits = gather_unordered(w_proj)
        places = [far for _, far in parts]
        proj_sources = [part for part, _ in parts]
    else:
        proj_sources = [lax.all_gather(w_proj, ("rec", "tm"), axis=0, tiled=True)]
        places, held_bits = [[]], None
    patches, taps = prepare(info, mel_frames[0], w_first, tokens, limit)
    subs = subsample(patches, taps, w_second_all)
    hidden, normed = project(info, gain_attn[None], subs, proj_sources, places, held_bits, tokens)

    share = w_out.shape[0]
    if share % 16 == 0:
        sources = [gathered]
        plan = [(0, k * share, share) for k in range(7)]
    else:
        sources = [
            gathered[:, k * share : (k + 1) * share].reshape(1, -1, WIDTH) for k in range(7)
        ]
        plan = [(k, 0, WIDTH) for k in range(7)]
    encoded = conformer_block(
        info,
        hidden,
        normed,
        sources,
        plan,
        gain_conv[None],
        w_depth,
        gain_out[None],
        limit,
    )
    return encoded[None]


def solution(mesh):
    placed = (
        P("rec", "tm", None),
        P("rec", None),
        P(),
        P(("rec", "tm"), None),
        P(("rec", "tm"), None),
        P(),
        P(("rec", "tm"), None),
        P(("rec", "tm"), None),
        P(),
        P(("rec", "tm"), None),
        P(),
        P(("rec", "tm"), None),
        P(),
    )
    return jax.shard_map(
        on_device, mesh=mesh, in_specs=placed, out_specs=P("rec", "tm", None), check_vma=False
    )
```

time: 873 us -> 233 us (0.27)
  local copies, waits for them, and re-layouts: 455 us -> 7.93 us
  matrix products: 201 us -> 0 us
  other arithmetic: 106 us -> 3.25 us
  Pallas kernels: 0 us -> 85.9 us
  waiting for transfers between devices: 63.2 us -> 91.3 us
  starting transfers between devices: 14.7 us -> 30 us
  loops' own time: 12.6 us -> 0 us
    slice x239 -> x6, local copies, waits for them, and re-layouts: 353 us -> 2.23 us  [the longest x3 1.27 us: prepare(): quads[EDGE - 1:EDGE - 1 + count]]
    dot_general x93 -> x0, matrix products: 201 us -> none  [the longest x72 145 us: conv_second(): jnp.dot(columns, w_second[offset:offset + channels], preferred_element_ty...]
    pallas_call x0 -> x9, Pallas kernels: none -> 85.9 us  [the longest x5 35.4 us: subsample(): pl.pallas_call(functools.partial(conv_kernel, begin, count), out_shape=ja...]
    ppermute x5 -> x19, waiting for transfers between devices: 13.3 us -> 91.3 us  [the longest x17 90 us: exchange(): return lax.ppermute(block, axis, [(i, i ^ distance) for i in range(size)])]
    convert_element_type x27 -> x0, other arithmetic: 62.3 us -> none  [the longest x8 61.5 us: conv_first(): return jnp.maximum(total, 0.0).astype(jnp.bfloat16)]
    reshape x72 -> x2, local copies, waits for them, and re-layouts: 55.9 us -> 0.1 us  [the longest x1 0.09 us: gather_ordered(): dims = held.reshape((2,) * len(names) + block.shape)]
    all_gather x6 -> x1, waiting for transfers between devices: 46.8 us -> 0.02 us  [on_device(): gathered = lax.all_gather(packed, ('rec', 'tm'), axis=0, tiled=False)]
    mul x19 -> x0, other arithmetic: 25.2 us -> none  [the longest x8 23.7 us: conv_second(): taken = taken * same_seg[:, None, None]]
  transfers between devices with their start and end apart: 11 -> 20, of which waited for: 4 -> 6; matrix products, arithmetic and copies ran while one was open for 87% -> 2% of each run, Pallas kernels for 0% -> 24%
where the time goes in v1:
time: 233 us; the launch traced here: 232 us
  waiting for transfers between devices  91.3 us (39%)
  Pallas kernels  85.9 us (37%)
  starting transfers between devices  30 us (13%)
  between operations  13.8 us (6%)
  local copies, waits for them, and re-layouts  7.93 us (3%)
  other arithmetic  3.25 us (1%)
    ppermute x17, waiting for transfers between devices, exchange(): return lax.ppermute(block, axis, [(i, i ^ distance) for i in range(size)])  90 us
    pallas_call x5, Pallas kernels, subsample(): pl.pallas_call(functools.partial(conv_kernel, begin, count), out_shape=ja...  35.4 us
    pallas_call x1, Pallas kernels, conformer_block(): pl.pallas_call(functools.partial(block_kernel, tokens, limit, plan, len(s...  29.8 us
    ppermute x17, starting transfers between devices, exchange(): return lax.ppermute(block, axis, [(i, i ^ distance) for i in range(size)])  18.1 us
    pallas_call x1, Pallas kernels, project(): pl.pallas_call(functools.partial(project_kernel, places, held_bits), out_...  15.9 us
    ppermute x1, starting transfers between devices, prepare(): high = lax.ppermute(mel[:reach], 'tm', backward)  7.13 us
    unnamed x28, local copies, waits for them, and re-layouts  5.51 us
    ppermute x1, starting transfers between devices, prepare(): low = lax.ppermute(mel[mel.shape[0] - reach:], 'tm', forward)  4.79 us
  transfers between devices with their start and end apart: 20, of which 6 were waited for; matrix products, arithmetic and copies ran while one was open for 2% of the time, Pallas kernels for 24%

profile of v1, /device:TPU:1, one launch (start us, length us, event | category | flops | bytes accessed | tf_op | source)
XLA Modules:
  0.0 232.2 jit_solution(16200320264401773409)
XLA Ops:
  6.5 0.9 copy-done
  7.5 0.9 copy-done.1
  8.4 0.8 copy-done.2
  9.2 0.8 copy-done.3
  10.1 0.8 pack.1
  10.9 0.0 all-gather.3.cloned.1.call-update
  10.9 4.2 %collective-permute-start.2 = (bf16[1,72,256]{2,1,0:T(8,128)(2,1)S(1)}, bf16[1,72,256]{2,1,0:T(8,128)(2,1)S(1)}, u32[]{:S(2)}, u32[]{:S(2)}) collective-permute-start(bf16[1,72,256]{2,1,0:T(8,128)(2,1)S(1)} %bitcast.34), channel_id=1, source_target_pairs={{0,24},{8,16},{16,8},{24,0},{1,25},{9,17},{17,9},{25,1},{2,26},{10... | collective-permute-start | bytes 110600 | tf_op jit(solution)/shard_map/ppermute | solution.py:42
  15.1 0.0 collective-permute-start.3
  15.1 0.4 collective-permute-start.4
  15.5 2.0 collective-permute-start.10
  17.5 1.2 collective-permute-start.11
  18.8 0.1 concatenate.21.info_ref
  18.8 4.8 %collective-permute-start = (bf16[640,80]{0,1:T(8,128)(2,1)S(1)}, bf16[640,80]{0,1:T(8,128)(2,1)S(1)}, u32[]{:S(2)}, u32[]{:S(2)}) collective-permute-start(bf16[640,80]{0,1:T(8,128)(2,1)S(1)} %get-tuple-element.20), channel_id=1, source_target_pairs={{0,1},{1,2},{2,3},{3,4},{4,5},{5,6},{6,7},{8,9},{9,10},{10,11},{11... | collective-permute-start | bytes 307208 | tf_op jit(solution)/shard_map/ppermute | solution.py:161
  23.7 7.1 %collective-permute-start.1 = (bf16[640,80]{0,1:T(8,128)(2,1)S(1)}, bf16[640,80]{0,1:T(8,128)(2,1)S(1)}, u32[]{:S(2)}, u32[]{:S(2)}) collective-permute-start(bf16[640,80]{0,1:T(8,128)(2,1)S(1)} %get-tuple-element.21), channel_id=1, source_target_pairs={{1,0},{2,1},{3,2},{4,3},{5,4},{6,5},{7,6},{9,8},{10,9},{11,10},{12... | collective-permute-start | bytes 307208 | tf_op jit(solution)/shard_map/ppermute | solution.py:162
  30.9 2.2 collective-permute-start.5
  33.0 0.0 collective-permute-done
  33.0 0.3 collective-permute-start.6
  33.3 1.3 collective-permute-done.1
  34.6 1.2 collective-permute-start.7
  35.8 2.0 collective-permute-done.5
  37.8 0.0 collective-permute-start.9
  37.9 3.4 %collective-permute-done.6 = bf16[4,72,256]{2,1,0:T(8,128)(2,1)S(1)} collective-permute-done((bf16[4,72,256]{2,1,0:T(8,128)(2,1)S(1)}, bf16[4,72,256]{2,1,0:T(8,128)(2,1)S(1)}, u32[]{:S(2)}, u32[]{:S(2)}) %collective-permute-start.6) | collective-permute-done | bytes 147488 | tf_op jit(solution)/shard_map/ppermute | solution.py:42
  41.3 0.1 broadcast_select_fusion.9
  41.4 0.9 pad_maximum_fusion.3
  42.3 0.6 collective-permute-start.8
  42.9 0.3 fusion
  43.2 0.4 copy.18
  43.6 0.5 slice.29
  44.2 0.4 copy.19
  44.6 0.5 slice.31
  45.1 0.0 copy-start.8
  45.1 0.3 pad_maximum_fusion.2.quads_ref
  45.5 0.3 copy-done.8
  45.8 3.9 %prepare.1 = (bf16[3,2,800,256]{3,2,1,0:T(8,128)(2,1)S(1)}, bf16[256,5120]{1,0:T(8,128)(2,1)S(1)}) custom-call(s32[8]{0:T(128)S(1)} %concatenate.21.info_ref, bf16[800,640]{1,0:T(8,128)(2,1)S(1)} %pad_maximum_fusion.2.quads_ref, s32[8,256]{1,0:T(8,128)S(1)} %copy-done.8, f32[9,256]{1,0:T(8,128)S(1)} %reshape.15.w_ref), custom_call_target="tpu_custom_call" | custom-call | flops 1887436800 | bytes 6291456 | tf_op jit(solution)/shard_map/prepare/pallas_call | solution.py:179
  49.7 0.0 collective-permute-done.10
  49.8 7.4 %collective-permute-done.9 = bf16[1,160,1024]{2,1,0:T(8,128)(2,1)} collective-permute-done((bf16[1,160,1024]{2,1,0:T(8,128)(2,1)}, bf16[1,160,1024]{2,1,0:T(8,128)(2,1)}, u32[]{:S(2)}, u32[]{:S(2)}) %collective-permute-start.9) | collective-permute-done | bytes 327712 | tf_op jit(solution)/shard_map/ppermute | solution.py:42
  57.1 1.6 pad_maximum_fusion.rest_5_
  58.7 1.1 collective-permute-start.12
  59.8 1.2 collective-permute-start.13
  61.1 0.4 collective-permute-start.14
  61.4 1.4 collective-permute-start.15
  62.9 0.0 collective-permute-done.8
  62.9 0.1 broadcast_select_fusion.1
  63.0 0.1 pad_maximum_fusion.1
  63.1 0.1 copy.20
  63.2 7.3 %subsample.9.rest_4_ = bf16[800,1024]{1,0:T(8,128)(2,1)S(1)} custom-call(bf16[3,2,800,256]{3,2,1,0:T(8,128)(2,1)S(1)} %get-tuple-element.9.a_ref, bf16[256,5120]{1,0:T(8,128)(2,1)S(1)} %get-tuple-element.10.b_ref, bf16[3,768,256]{2,1,0:T(8,128)(2,1)S(1)} %bitcast.24), custom_call_target="tpu_custom_call" | custom-call | flops 6606028800 | bytes 8388608 | tf_op jit(solution)/shard_map/subsample/pallas_call | solution.py:237
  70.5 7.1 %subsample.8.rest_3_ = bf16[800,1024]{1,0:T(8,128)(2,1)S(1)} custom-call(bf16[3,2,800,256]{3,2,1,0:T(8,128)(2,1)S(1)} %get-tuple-element.9.a_ref, bf16[256,5120]{1,0:T(8,128)(2,1)S(1)} %get-tuple-element.10.b_ref, bf16[3,768,256]{2,1,0:T(8,128)(2,1)S(1)} %bitcast.25), custom_call_target="tpu_custom_call" | custom-call | flops 6606028800 | bytes 8388608 | tf_op jit(solution)/shard_map/subsample/pallas_call | solution.py:237
  77.5 23.2 %collective-permute-done.12.rest_6_ = bf16[4,160,1024]{2,1,0:T(8,128)(2,1)S(1)} collective-permute-done((bf16[4,160,1024]{2,1,0:T(8,128)(2,1)S(1)}, bf16[4,160,1024]{2,1,0:T(8,128)(2,1)S(1)}, u32[]{:S(2)}, u32[]{:S(2)}) %collective-permute-start.12) | collective-permute-done | bytes 1310752 | tf_op jit(solution)/shard_map/ppermute | solution.py:42
  100.8 1.2 collective-permute-start.16
  101.9 0.0 collective-permute-done.13.rest_7_
  101.9 0.0 collective-permute-start.17
  101.9 54.0 %collective-permute-done.14.rest_8_ = bf16[4,160,1024]{2,1,0:T(8,128)(2,1)S(1)} collective-permute-done((bf16[4,160,1024]{2,1,0:T(8,128)(2,1)S(1)}, bf16[4,160,1024]{2,1,0:T(8,128)(2,1)S(1)}, u32[]{:S(2)}, u32[]{:S(2)}) %collective-permute-start.14) | collective-permute-done | bytes 1310752 | tf_op jit(solution)/shard_map/ppermute | solution.py:42
  156.0 0.7 collective-permute-start.18
  156.7 7.1 %subsample.7.rest_2_ = bf16[800,1024]{1,0:T(8,128)(2,1)S(1)} custom-call(bf16[3,2,800,256]{3,2,1,0:T(8,128)(2,1)S(1)} %get-tuple-element.9.a_ref, bf16[256,5120]{1,0:T(8,128)(2,1)S(1)} %get-tuple-element.10.b_ref, bf16[3,768,256]{2,1,0:T(8,128)(2,1)S(1)} %bitcast.26), custom_call_target="tpu_custom_call" | custom-call | flops 6606028800 | bytes 8388608 | tf_op jit(solution)/shard_map/subsample/pallas_call | solution.py:237
  163.8 7.1 %subsample.6.rest_1_ = bf16[800,1024]{1,0:T(8,128)(2,1)S(1)} custom-call(bf16[3,2,800,256]{3,2,1,0:T(8,128)(2,1)S(1)} %get-tuple-element.9.a_ref, bf16[256,5120]{1,0:T(8,128)(2,1)S(1)} %get-tuple-element.10.b_ref, bf16[3,768,256]{2,1,0:T(8,128)(2,1)S(1)} %bitcast.27), custom_call_target="tpu_custom_call" | custom-call | flops 6606028800 | bytes 8388608 | tf_op jit(solution)/shard_map/subsample/pallas_call | solution.py:237
  170.9 0.0 copy-start.5
  170.9 6.9 %subsample.5.rest_0_ = bf16[800,1024]{1,0:T(8,128)(2,1)S(1)} custom-call(bf16[3,2,800,256]{3,2,1,0:T(8,128)(2,1)S(1)} %get-tuple-element.9.a_ref, bf16[256,5120]{1,0:T(8,128)(2,1)S(1)} %get-tuple-element.10.b_ref, bf16[3,768,256]{2,1,0:T(8,128)(2,1)S(1)} %bitcast.28), custom_call_target="tpu_custom_call" | custom-call | flops 6606028800 | bytes 8388608 | tf_op jit(solution)/shard_map/subsample/pallas_call | solution.py:237
  177.9 0.0 copy-start.4
  177.9 0.0 copy-start.6
  177.9 0.0 copy-start.7
  177.9 15.9 %project.1 = (f32[544,1024]{1,0:T(8,128)}, bf16[800,1024]{1,0:T(8,128)(2,1)S(1)}) custom-call(s32[8]{0:T(128)S(1)} %concatenate.21.info_ref, f32[1,1024]{1,0:T(1,128)S(1)} %bitcast.29, bf16[800,1024]{1,0:T(8,128)(2,1)S(1)} %subsample.5.rest_0_, bf16[800,1024]{1,0:T(8,128)(2,1)S(1)} %subsample.6.rest_1_, bf16[800,1024]{1,0:T(8,128)(2,1)S(1)} %subsample.7.rest_2_, ...), custom_call_target="tpu_custom_call" | custom-call | flops 8388608000 | bytes 25165824 | tf_op jit(solution)/shard_map/project/pallas_call | solution.py:310
  193.8 0.0 all-gather.3.cloned.1.call-done
  193.9 1.6 copy-done.9
  195.5 29.8 %conformer_block.1 = bf16[512,1024]{1,0:T(8,128)(2,1)} custom-call(s32[8]{0:T(128)S(1)} %concatenate.21.info_ref, f32[544,1024]{1,0:T(8,128)S(1)} %copy-done.9, bf16[800,1024]{1,0:T(8,128)(2,1)S(1)} %get-tuple-element.12.normed_ref, f32[1,1024]{1,0:T(1,128)S(1)} %bitcast.30, f32[9,1024]{1,0:T(8,128)S(1)} %copy-done.4, f32[1,1024]{1,0:T(1,128)S(1)} %bitcast.31, ...), custom_call_target="tpu_custom_call" | custom-call | flops 9059696640 | bytes 25165824 | tf_op jit(solution)/shard_map/conformer_block/pallas_call | solution.py:555
  (33 shorter events, 0.2 us)
Async XLA Ops:
  6.5 187.3 %all-gather.3.cloned.1.call-start = ((), (), s32[]{:S(2)}) async-start(), calls=%async_computation | async-start | bytes 15138816 | tf_op jit(solution)/shard_map/all_gather | solution.py:599
  6.5 0.9 copy-start
  7.5 0.9 copy-start.1
  8.4 0.8 copy-start.2
  9.2 0.8 copy-start.3
  10.0 0.9 copy-start.11
  10.1 8.6 %copy-start.10 = (bf16[1,2048,80]{1,2,0:T(8,128)(2,1)S(1)}, bf16[1,2048,80]{1,2,0:T(8,128)(2,1)}, u32[]{:S(2)}) copy-start(bf16[1,2048,80]{1,2,0:T(8,128)(2,1)} %param.14) | copy-start | bytes 983044
  10.1 8.7 %copy-start.12 = (f32[3,3,256]{2,1,0:T(4,128)S(1)}, f32[3,3,256]{2,1,0:T(4,128)}, u32[]{:S(2)}) copy-start(f32[3,3,256]{2,1,0:T(4,128)} %param.16) | copy-start | bytes 27652
  10.1 8.7 %copy-start.13 = (s32[1,4]{1,0:T(1,128)S(1)}, s32[1,4]{1,0:T(1,128)}, u32[]{:S(2)}) copy-start(s32[1,4]{1,0:T(1,128)} %param.15) | copy-start | bytes 52
  10.9 7.9 %collective-permute-start.2 = (bf16[1,72,256]{2,1,0:T(8,128)(2,1)S(1)}, bf16[1,72,256]{2,1,0:T(8,128)(2,1)S(1)}, u32[]{:S(2)}, u32[]{:S(2)}) collective-permute-start(bf16[1,72,256]{2,1,0:T(8,128)(2,1)S(1)} %bitcast.34), channel_id=1, source_target_pairs={{0,24},{8,16},{16,8},{24,0},{1,25},{9,17},{17,9},{25,1},{2,26},{10... | collective-permute-start | bytes 110600 | tf_op jit(solution)/shard_map/ppermute | solution.py:42
  15.1 8.5 %collective-permute-start.3 = (bf16[1,72,256]{2,1,0:T(8,128)(2,1)S(1)}, bf16[1,72,256]{2,1,0:T(8,128)(2,1)S(1)}, u32[]{:S(2)}, u32[]{:S(2)}) collective-permute-start(bf16[1,72,256]{2,1,0:T(8,128)(2,1)S(1)} %bitcast.35), channel_id=1, source_target_pairs={{0,16},{8,24},{16,0},{24,8},{1,17},{9,25},{17,1},{25,9},{2,18},{10... | collective-permute-start | bytes 110600 | tf_op jit(solution)/shard_map/ppermute | solution.py:42
  15.1 15.7 %collective-permute-start.4 = (bf16[1,72,256]{2,1,0:T(8,128)(2,1)S(1)}, bf16[1,72,256]{2,1,0:T(8,128)(2,1)S(1)}, u32[]{:S(2)}, u32[]{:S(2)}) collective-permute-start(bf16[1,72,256]{2,1,0:T(8,128)(2,1)S(1)} %bitcast.36), channel_id=1, source_target_pairs={{0,8},{8,0},{16,24},{24,16},{1,9},{9,1},{17,25},{25,17},{2,10},{10... | collective-permute-start | bytes 110600 | tf_op jit(solution)/shard_map/ppermute | solution.py:42
  15.5 34.2 %collective-permute-start.10 = (bf16[1,160,1024]{2,1,0:T(8,128)(2,1)}, bf16[1,160,1024]{2,1,0:T(8,128)(2,1)}, u32[]{:S(2)}, u32[]{:S(2)}) collective-permute-start(bf16[1,160,1024]{2,1,0:T(8,128)(2,1)} %bitcast.13), channel_id=1, source_target_pairs={{0,16},{8,24},{16,0},{24,8},{1,17},{9,25},{17,1},{25,9},{2,18},{10... | collective-permute-start | bytes 983048 | tf_op jit(solution)/shard_map/ppermute | solution.py:42
  17.5 32.2 %collective-permute-start.11 = (bf16[1,160,1024]{2,1,0:T(8,128)(2,1)}, bf16[1,160,1024]{2,1,0:T(8,128)(2,1)}, u32[]{:S(2)}, u32[]{:S(2)}) collective-permute-start(bf16[1,160,1024]{2,1,0:T(8,128)(2,1)} %bitcast.13), channel_id=1, source_target_pairs={{0,24},{8,16},{16,8},{24,0},{1,25},{9,17},{17,9},{25,1},{2,26},{10... | collective-permute-start | bytes 983048 | tf_op jit(solution)/shard_map/ppermute | solution.py:42
  18.8 14.2 %collective-permute-start = (bf16[640,80]{0,1:T(8,128)(2,1)S(1)}, bf16[640,80]{0,1:T(8,128)(2,1)S(1)}, u32[]{:S(2)}, u32[]{:S(2)}) collective-permute-start(bf16[640,80]{0,1:T(8,128)(2,1)S(1)} %get-tuple-element.20), channel_id=1, source_target_pairs={{0,1},{1,2},{2,3},{3,4},{4,5},{5,6},{6,7},{8,9},{9,10},{10,11},{11... | collective-permute-start | bytes 307208 | tf_op jit(solution)/shard_map/ppermute | solution.py:161
  23.7 10.9 %collective-permute-start.1 = (bf16[640,80]{0,1:T(8,128)(2,1)S(1)}, bf16[640,80]{0,1:T(8,128)(2,1)S(1)}, u32[]{:S(2)}, u32[]{:S(2)}) collective-permute-start(bf16[640,80]{0,1:T(8,128)(2,1)S(1)} %get-tuple-element.21), channel_id=1, source_target_pairs={{1,0},{2,1},{3,2},{4,3},{5,4},{6,5},{7,6},{9,8},{10,9},{11,10},{12... | collective-permute-start | bytes 307208 | tf_op jit(solution)/shard_map/ppermute | solution.py:162
  30.9 7.0 %collective-permute-start.5 = (bf16[4,72,256]{2,1,0:T(8,128)(2,1)S(1)}, bf16[4,72,256]{2,1,0:T(8,128)(2,1)S(1)}, u32[]{:S(2)}, u32[]{:S(2)}) collective-permute-start(bf16[4,72,256]{2,1,0:T(8,128)(2,1)S(1)} %pad_maximum_fusion.5), channel_id=1, source_target_pairs={{0,6},{1,7},{2,4},{3,5},{4,2},{5,3},{6,0},{7,1},{8,14},{9,15},{10,... | collective-permute-start | bytes 442376 | tf_op jit(solution)/shard_map/ppermute | solution.py:42
  33.0 8.2 %collective-permute-start.6 = (bf16[4,72,256]{2,1,0:T(8,128)(2,1)S(1)}, bf16[4,72,256]{2,1,0:T(8,128)(2,1)S(1)}, u32[]{:S(2)}, u32[]{:S(2)}) collective-permute-start(bf16[4,72,256]{2,1,0:T(8,128)(2,1)S(1)} %pad_maximum_fusion.5), channel_id=1, source_target_pairs={{0,4},{1,5},{2,6},{3,7},{4,0},{5,1},{6,2},{7,3},{8,12},{9,13},{10,... | collective-permute-start | bytes 442376 | tf_op jit(solution)/shard_map/ppermute | solution.py:42
  34.6 6.7 %collective-permute-start.7 = (bf16[4,72,256]{2,1,0:T(8,128)(2,1)S(1)}, bf16[4,72,256]{2,1,0:T(8,128)(2,1)S(1)}, u32[]{:S(2)}, u32[]{:S(2)}) collective-permute-start(bf16[4,72,256]{2,1,0:T(8,128)(2,1)S(1)} %pad_maximum_fusion.5), channel_id=1, source_target_pairs={{0,2},{1,3},{2,0},{3,1},{4,6},{5,7},{6,4},{7,5},{8,10},{9,11},{10,... | collective-permute-start | bytes 442376 | tf_op jit(solution)/shard_map/ppermute | solution.py:42
  37.8 19.3 %collective-permute-start.9 = (bf16[1,160,1024]{2,1,0:T(8,128)(2,1)}, bf16[1,160,1024]{2,1,0:T(8,128)(2,1)}, u32[]{:S(2)}, u32[]{:S(2)}) collective-permute-start(bf16[1,160,1024]{2,1,0:T(8,128)(2,1)} %bitcast.13), channel_id=1, source_target_pairs={{0,8},{8,0},{16,24},{24,16},{1,9},{9,1},{17,25},{25,17},{2,10},{10... | collective-permute-start | bytes 983048 | tf_op jit(solution)/shard_map/ppermute | solution.py:42
  42.3 20.6 %collective-permute-start.8 = (bf16[16,72,256]{2,1,0:T(8,128)(2,1)}, bf16[16,72,256]{2,1,0:T(8,128)(2,1)S(1)}, u32[]{:S(2)}, u32[]{:S(2)}) collective-permute-start(bf16[16,72,256]{2,1,0:T(8,128)(2,1)} %pad_maximum_fusion.3), channel_id=1, source_target_pairs={{0,1},{1,0},{2,3},{3,2},{4,5},{5,4},{6,7},{7,6},{8,9},{9,8},{10,11... | collective-permute-start | bytes 1769480 | tf_op jit(solution)/shard_map/ppermute | solution.py:42
  45.1 0.7 copy-start.8
  58.7 42.0 %collective-permute-start.12 = (bf16[4,160,1024]{2,1,0:T(8,128)(2,1)S(1)}, bf16[4,160,1024]{2,1,0:T(8,128)(2,1)S(1)}, u32[]{:S(2)}, u32[]{:S(2)}) collective-permute-start(bf16[4,160,1024]{2,1,0:T(8,128)(2,1)S(1)} %pad_maximum_fusion.rest_5_), channel_id=1, source_target_pairs={{0,2},{1,3},{2,0},{3,1},{4,6},{5,7},{6,4},{7,5},{8,10},{9,11},{10,... | collective-permute-start | bytes 3932168 | tf_op jit(solution)/shard_map/ppermute | solution.py:42
  59.8 42.1 %collective-permute-start.13 = (bf16[4,160,1024]{2,1,0:T(8,128)(2,1)S(1)}, bf16[4,160,1024]{2,1,0:T(8,128)(2,1)S(1)}, u32[]{:S(2)}, u32[]{:S(2)}) collective-permute-start(bf16[4,160,1024]{2,1,0:T(8,128)(2,1)S(1)} %pad_maximum_fusion.rest_5_), channel_id=1, source_target_pairs={{0,4},{1,5},{2,6},{3,7},{4,0},{5,1},{6,2},{7,3},{8,12},{9,13},{10,... | collective-permute-start | bytes 3932168 | tf_op jit(solution)/shard_map/ppermute | solution.py:42
  61.1 94.9 %collective-permute-start.14 = (bf16[4,160,1024]{2,1,0:T(8,128)(2,1)S(1)}, bf16[4,160,1024]{2,1,0:T(8,128)(2,1)S(1)}, u32[]{:S(2)}, u32[]{:S(2)}) collective-permute-start(bf16[4,160,1024]{2,1,0:T(8,128)(2,1)S(1)} %pad_maximum_fusion.rest_5_), channel_id=1, source_target_pairs={{0,6},{1,7},{2,4},{3,5},{4,2},{5,3},{6,0},{7,1},{8,14},{9,15},{10,... | collective-permute-start | bytes 3932168 | tf_op jit(solution)/shard_map/ppermute | solution.py:42
  61.4 116.4 %collective-permute-start.15 = (bf16[4,160,1024]{2,1,0:T(8,128)(2,1)S(1)}, bf16[4,160,1024]{2,1,0:T(8,128)(2,1)S(1)}, u32[]{:S(2)}, u32[]{:S(2)}) collective-permute-start(bf16[4,160,1024]{2,1,0:T(8,128)(2,1)S(1)} %pad_maximum_fusion.rest_5_), channel_id=1, source_target_pairs={{0,1},{1,0},{2,3},{3,2},{4,5},{5,4},{6,7},{7,6},{8,9},{9,8},{10,11... | collective-permute-start | bytes 3932168 | tf_op jit(solution)/shard_map/ppermute | solution.py:42
  100.8 77.1 %collective-permute-start.16 = (bf16[4,160,1024]{2,1,0:T(8,128)(2,1)S(1)}, bf16[4,160,1024]{2,1,0:T(8,128)(2,1)S(1)}, u32[]{:S(2)}, u32[]{:S(2)}) collective-permute-start(bf16[4,160,1024]{2,1,0:T(8,128)(2,1)S(1)} %collective-permute-done.12.rest_6_), channel_id=1, source_target_pairs={{0,1},{1,0},{2,3},{3,2},{4,5},{5,4},{6,7},{7,6},{8,9},{9,8},{10,11... | collective-permute-start | bytes 3932168 | tf_op jit(solution)/shard_map/ppermute | solution.py:42
  101.9 75.9 %collective-permute-start.17 = (bf16[4,160,1024]{2,1,0:T(8,128)(2,1)S(1)}, bf16[4,160,1024]{2,1,0:T(8,128)(2,1)S(1)}, u32[]{:S(2)}, u32[]{:S(2)}) collective-permute-start(bf16[4,160,1024]{2,1,0:T(8,128)(2,1)S(1)} %collective-permute-done.13.rest_7_), channel_id=1, source_target_pairs={{0,1},{1,0},{2,3},{3,2},{4,5},{5,4},{6,7},{7,6},{8,9},{9,8},{10,11... | collective-permute-start | bytes 3932168 | tf_op jit(solution)/shard_map/ppermute | solution.py:42
  156.0 21.9 %collective-permute-start.18 = (bf16[4,160,1024]{2,1,0:T(8,128)(2,1)S(1)}, bf16[4,160,1024]{2,1,0:T(8,128)(2,1)S(1)}, u32[]{:S(2)}, u32[]{:S(2)}) collective-permute-start(bf16[4,160,1024]{2,1,0:T(8,128)(2,1)S(1)} %collective-permute-done.14.rest_8_), channel_id=1, source_target_pairs={{0,1},{1,0},{2,3},{3,2},{4,5},{5,4},{6,7},{7,6},{8,9},{9,8},{10,11... | collective-permute-start | bytes 3932168 | tf_op jit(solution)/shard_map/ppermute | solution.py:42
  170.9 7.0 %copy-start.5 = (f32[1024]{0:T(1024)S(1)}, f32[1024]{0:T(1024)}, u32[]{:S(2)}) copy-start(f32[1024]{0:T(1024)} %param.19) | copy-start | bytes 12292
  177.9 16.0 %copy-start.4 = (f32[9,1024]{1,0:T(8,128)S(1)}, f32[9,1024]{1,0:T(8,128)}, u32[]{:S(2)}) copy-start(f32[9,1024]{1,0:T(8,128)} %depth_ref.1) | copy-start | bytes 110596
  177.9 16.0 %copy-start.6 = (f32[1024]{0:T(1024)S(1)}, f32[1024]{0:T(1024)}, u32[]{:S(2)}) copy-start(f32[1024]{0:T(1024)} %param.22) | copy-start | bytes 12292
  177.9 16.0 %copy-start.7 = (f32[1024]{0:T(1024)S(1)}, f32[1024]{0:T(1024)}, u32[]{:S(2)}) copy-start(f32[1024]{0:T(1024)} %param.26) | copy-start | bytes 12292
  193.9 1.6 copy-start.9
Sparse Core Ops, SparseCore 0:
  11.0 162.7 all-gather.2

commit v2 on v1

--- a/solution.py
+++ b/solution.py
@@ -91,21 +91,38 @@
     return dims.reshape((-1,) + block.shape[1:])
 
 
-def gather_unordered(block):
-    groups = bit_groups()
-    held = block[None]
-    held_bits = []
-    for axis, bits in groups[:-2]:
-        got = [held] + [exchange(held, axis, d) for d in distances(bits)[1:]]
-        held = jnp.concatenate(got, axis=0)
-        held_bits = held_bits + [(axis, bit) for bit in bits]
-    axis, bits = groups[-2]
-    parts = [(held, [])]
-    for d in distances(bits)[1:]:
-        parts.append((exchange(held, axis, d), [(axis, d)]))
-    axis, bits = groups[-1]
-    parts += [(exchange(part, axis, 1), far + [(axis, 1)]) for part, far in parts]
-    return parts, held_bits
+def gather_relayed(block, whole_rec, after):
+    if whole_rec:
+        held = lax.all_gather(block, "rec", axis=0, tiled=True)
+    else:
+        held = jnp.concatenate([block] + [exchange(block, "rec", d) for d in (1, 2, 3)], axis=0)
+    if after:
+        held = lax.optimization_barrier((held, *after))[0]
+    half = held.shape[0] // 2
+    beside = exchange(held, "tm", 2)
+    above = exchange(held, "tm", 4)
+    low = exchange(beside[:half], "tm", 4)
+    high = exchange(above[half:], "tm", 2)
+    pieces = [(held, 0, 0, 4), (beside, 2, 0, 4), (above, 4, 0, 4), (low, 6, 0, 2), (high, 6, 2, 2)]
+    pieces += [(exchange(p, "tm", 1), far ^ 1, slot, n) for p, far, slot, n in pieces]
+    return [p[0] for p in pieces], [p[1:] + (whole_rec,) for p in pieces], [low, high]
+
+
+def copies_in(info_ref, sources, places, target, sem):
+    if places is None:
+        pltpu.make_async_copy(sources[0], target, sem).start()
+        return
+    rec, tm, tm_size = info_ref[5], info_ref[6], info_ref[7]
+    for source, (far, first, number, indices) in zip(sources, places):
+        rows = source.shape[0] // number
+        for slot in range(number):
+            owner_rec = first + slot if indices else rec ^ (first + slot)
+            owner = owner_rec * tm_size + (tm ^ far)
+            if len(target.shape) == 3:
+                place = target.at[owner]
+            else:
+                place = target.at[pl.ds(pl.multiple_of(owner * rows, 16), rows), :]
+            pltpu.make_async_copy(source.at[pl.ds(slot * rows, rows), :], place, sem).start()
 
 
 BINS = 41
@@ -252,28 +269,11 @@
     return pieces
 
 
-def project_kernel(places, held_bits, info_ref, gain_ref, *rest):
+def project_kernel(places, info_ref, gain_ref, *rest):
     subs = rest[:5]
-    sources = rest[5 : 5 + len(places)]
-    mid_ref, normed_ref, weights, hidden, sem = rest[5 + len(places) :]
-    rec, tm, tm_size = info_ref[5], info_ref[6], info_ref[7]
-
-    rows = sources[0].shape[-2]
-    if held_bits is None:
-        pltpu.make_async_copy(sources[0], weights, sem).start()
-    else:
-        for source, far in zip(sources, places):
-            far_rec = sum(d for axis, d in far if axis == "rec")
-            far_tm = sum(d for axis, d in far if axis == "tm")
-            for slot in range(1 << len(held_bits)):
-                own_rec, own_tm = far_rec, far_tm
-                for k, (axis, bit) in enumerate(held_bits):
-                    if slot >> k & 1:
-                        own_rec += bit if axis == "rec" else 0
-                        own_tm += bit if axis == "tm" else 0
-                owner = (rec ^ own_rec) * tm_size + (tm ^ own_tm)
-                place = pl.ds(pl.multiple_of(owner * rows, 16), rows)
-                pltpu.make_async_copy(source.at[slot], weights.at[place, :], sem).start()
+    sources = rest[5:-5]
+    mid_ref, normed_ref, weights, hidden, sem = rest[-5:]
+    copies_in(info_ref, sources, places, weights, sem)
     pltpu.make_async_copy(weights, weights, sem).wait()
 
     depth = weights.shape[0] // len(subs)
@@ -302,13 +302,13 @@
     mid_ref[...] = hidden[WINDOW : WINDOW + mid_ref.shape[0], :]
 
 
-def project(info, gain, subs, sources, places, held_bits, tokens):
+def project(info, gain, subs, sources, places, tokens):
     rows_all = tokens + 2 * HALO
     rows_mid = tokens + 2 * EDGE
     whole = pl.BlockSpec(memory_space=pltpu.VMEM)
     depth = sum(sub.shape[1] for sub in subs)
     return pl.pallas_call(
-        functools.partial(project_kernel, places, held_bits),
+        functools.partial(project_kernel, places),
         out_shape=(
             jax.ShapeDtypeStruct((rows_mid, WIDTH), jnp.float32),
             jax.ShapeDtypeStruct((rows_all, WIDTH), jnp.bfloat16),
@@ -360,44 +360,19 @@
     )(*arrays)
 
 
-def block_kernel(
-    tokens,
-    limit,
-    plan,
-    count,
-    info_ref,
-    hidden_ref,
-    normed_ref,
-    gain_conv_ref,
-    depth_ref,
-    gain_out_ref,
-    *rest,
-):
-    sources = rest[:count]
-    out_ref = rest[count]
-    scratch = rest[count + 1 :]
-    buffers = scratch[: len(plan)]
-    keys, values, queries, context, attended, gated, masks, biases, sems = scratch[len(plan) :]
+def columns(weights, part, parts, n):
+    rows = weights.shape[1] // parts
+    here = pl.ds(pl.multiple_of(n * COLS, COLS), COLS)
+    return weights[:, part * rows : (part + 1) * rows, here].reshape(-1, COLS)
+
+
+def attention_kernel(tokens, limit, places, info_ref, normed_ref, *rest):
+    sources = rest[:-7]
+    context_ref, weights, keys, values, queries, biases, sem = rest[-7:]
     rows_mid = tokens + 2 * EDGE
-    mid = slice(WINDOW, WINDOW + rows_mid)
-    copies = []
-    for at, (source, offset, rows) in enumerate(plan):
-        copies.append(
-            pltpu.make_async_copy(
-                sources[source].at[:, pl.ds(offset, rows), :], buffers[at], sems.at[at]
-            )
-        )
-    for copy in copies:
-        copy.start()
+    copies_in(info_ref, sources, places, weights, sem)
     base = info_ref[0]
     lengths = [info_ref[1 + k] for k in range(4)]
-
-    def columns(at, n):
-        part = buffers[at][:, :, pl.ds(pl.multiple_of(n * COLS, COLS), COLS)]
-        return part.reshape(-1, COLS)
-
-    def here(n):
-        return pl.ds(pl.multiple_of(n * COLS, COLS), COLS)
 
     blocks = []
     at_row = 0
@@ -406,11 +381,6 @@
         blocks.append((at_row, size))
         at_row += size
 
-    row = lax.broadcasted_iota(jnp.int32, (tokens, HEAD_DIM), 0)
-    own = segment_of(base + 4 * row, lengths, limit)
-    for k in range(KERNEL):
-        there = segment_of(base + 4 * (row + k - KERNEL // 2), lengths, limit)
-        masks[k] = (there == own).astype(jnp.float32)
     for at, (start, size) in enumerate(blocks):
         span = size + 2 * WINDOW
         q_row = lax.broadcasted_iota(jnp.int32, (size, 1), 0)
@@ -425,28 +395,21 @@
             (values.shape[0], HEAD_DIM), jnp.bfloat16
         )
 
-    copies[0].wait()
+    pltpu.make_async_copy(weights, weights, sem).wait()
 
     @pl.loop(0, WIDTH // COLS)
     def _(n):
-        queries[:, here(n)] = jnp.dot(
-            normed_ref[mid, :], columns(0, n), preferred_element_type=jnp.float32
+        here = pl.ds(pl.multiple_of(n * COLS, COLS), COLS)
+        queries[:, here] = jnp.dot(
+            normed_ref[WINDOW : WINDOW + rows_mid, :],
+            columns(weights, 0, 3, n),
+            preferred_element_type=jnp.float32,
         ).astype(jnp.bfloat16)
-
-    copies[1].wait()
-
-    @pl.loop(0, WIDTH // COLS)
-    def _(n):
-        keys[:, here(n)] = jnp.dot(
-            normed_ref[...], columns(1, n), preferred_element_type=jnp.float32
+        keys[:, here] = jnp.dot(
+            normed_ref[...], columns(weights, 1, 3, n), preferred_element_type=jnp.float32
         ).astype(jnp.bfloat16)
-
-    copies[2].wait()
-
-    @pl.loop(0, WIDTH // COLS)
-    def _(n):
         made = jnp.dot(
-            normed_ref[...], columns(2, n), preferred_element_type=jnp.float32
+            normed_ref[...], columns(weights, 2, 3, n), preferred_element_type=jnp.float32
         ).astype(jnp.bfloat16)
         for k in range(COLS // HEAD_DIM):
             lanes = pl.ds(pl.multiple_of(2 * n * COLS + 2 * k * HEAD_DIM, HEAD_DIM), HEAD_DIM)
@@ -473,16 +436,71 @@
                 values[start : start + span, wide],
                 preferred_element_type=jnp.float32,
             )
-            context[start : start + size, lanes] = (
+            context_ref[start : start + size, lanes] = (
                 mixed[:, :HEAD_DIM] / mixed[:, HEAD_DIM:]
             ).astype(jnp.bfloat16)
 
-    copies[3].wait()
+
+def attend(info, normed, sources, places, limit):
+    rows_all = normed.shape[0]
+    tokens = rows_all - 2 * HALO
+    rows_mid = tokens + 2 * EDGE
+    whole = pl.BlockSpec(memory_space=pltpu.VMEM)
+    flops = 2 * WIDTH * (rows_all * 2 * WIDTH + rows_mid * WIDTH + 3 * rows_mid * 400)
+    return pl.pallas_call(
+        functools.partial(attention_kernel, tokens, limit, places),
+        out_shape=jax.ShapeDtypeStruct((rows_mid, WIDTH), jnp.bfloat16),
+        in_specs=[pl.BlockSpec(memory_space=pltpu.SMEM), whole]
+        + [pl.BlockSpec(memory_space=pl.ANY)] * len(sources),
+        out_specs=whole,
+        scratch_shapes=[
+            pltpu.VMEM((32, 3 * WIDTH // 32, WIDTH), jnp.bfloat16),
+            pltpu.VMEM((rows_all, WIDTH), jnp.bfloat16),
+            pltpu.VMEM((rows_all, 2 * WIDTH), jnp.bfloat16),
+            pltpu.VMEM((rows_mid, WIDTH), jnp.bfloat16),
+            pltpu.VMEM((4, 128 + EDGE, 512), jnp.float32),
+            pltpu.SemaphoreType.DMA(()),
+        ],
+        compiler_params=pltpu.CompilerParams(vmem_limit_bytes=26 * 1024 * 1024),
+        cost_estimate=pl.CostEstimate(
+            flops=flops, bytes_accessed=10 * 1024 * 1024, transcendentals=2 * 1024 * 1024
+        ),
+        name="attend",
+    )(info, normed, *sources)
+
+
+def final_kernel(
+    tokens,
+    limit,
+    places,
+    info_ref,
+    hidden_ref,
+    context_ref,
+    gain_conv_ref,
+    depth_ref,
+    gain_out_ref,
+    *rest,
+):
+    sources = rest[:-8]
+    out_ref, weights, attended, normed, gated, acted, masks, sem = rest[-8:]
+    rows_mid = tokens + 2 * EDGE
+    copies_in(info_ref, sources, places, weights, sem)
+    base = info_ref[0]
+    lengths = [info_ref[1 + k] for k in range(4)]
+
+    row = lax.broadcasted_iota(jnp.int32, (tokens, HEAD_DIM), 0)
+    own = segment_of(base + 4 * row, lengths, limit)
+    for k in range(KERNEL):
+        there = segment_of(base + 4 * (row + k - KERNEL // 2), lengths, limit)
+        masks[k] = (there == own).astype(jnp.float32)
+
+    pltpu.make_async_copy(weights, weights, sem).wait()
 
     @pl.loop(0, WIDTH // COLS)
     def _(n):
-        attended[:, here(n)] = hidden_ref[:, here(n)] + jnp.dot(
-            context[...], columns(3, n), preferred_element_type=jnp.float32
+        here = pl.ds(pl.multiple_of(n * COLS, COLS), COLS)
+        attended[:, here] = hidden_ref[:, here] + jnp.dot(
+            context_ref[...], columns(weights, 0, 4, n), preferred_element_type=jnp.float32
         )
 
     gain_c = gain_conv_ref[...]
@@ -491,35 +509,28 @@
     @pl.loop(0, 2)
     def _(r):
         rows = pl.ds(pl.multiple_of(r * step_rows, 16), step_rows)
-        queries[rows, :] = layer_norm(attended[rows, :], gain_c).astype(jnp.bfloat16)
-
-    copies[4].wait()
-    copies[5].wait()
+        normed[rows, :] = layer_norm(attended[rows, :], gain_c).astype(jnp.bfloat16)
 
     @pl.loop(0, WIDTH // COLS)
     def _(n):
-        value = jnp.dot(queries[...], columns(4, n), preferred_element_type=jnp.float32)
-        gate = jnp.dot(queries[...], columns(5, n), preferred_element_type=jnp.float32)
+        value = jnp.dot(normed[...], columns(weights, 1, 4, n), preferred_element_type=jnp.float32)
+        gate = jnp.dot(normed[...], columns(weights, 2, 4, n), preferred_element_type=jnp.float32)
         made = (value * jax.nn.sigmoid(gate)).astype(jnp.bfloat16).astype(jnp.float32)
-        for k in range(COLS // HEAD_DIM):
-            gated[n * (COLS // HEAD_DIM) + k] = made[:, k * HEAD_DIM : (k + 1) * HEAD_DIM]
-
-    @pl.loop(0, WIDTH // HEAD_DIM)
-    def _(n):
-        lanes = pl.ds(pl.multiple_of(n * HEAD_DIM, HEAD_DIM), HEAD_DIM)
-        total = jnp.zeros((tokens, HEAD_DIM), jnp.float32)
-        for k in range(KERNEL):
-            begin = EDGE - KERNEL // 2 + k
-            tap = gated[n, begin : begin + tokens, :] * depth_ref[k : k + 1, lanes]
-            total = total + (tap if k == KERNEL // 2 else tap * masks[k])
-        context[0:tokens, lanes] = (total * jax.nn.sigmoid(total)).astype(jnp.bfloat16)
-
-    copies[6].wait()
+        for j in range(COLS // HEAD_DIM):
+            gated[...] = made[:, j * HEAD_DIM : (j + 1) * HEAD_DIM]
+            lanes = pl.ds(pl.multiple_of(n * COLS + j * HEAD_DIM, HEAD_DIM), HEAD_DIM)
+            total = jnp.zeros((tokens, HEAD_DIM), jnp.float32)
+            for k in range(KERNEL):
+                begin = EDGE - KERNEL // 2 + k
+                tap = gated[begin : begin + tokens, :] * depth_ref[k : k + 1, lanes]
+                total = total + (tap if k == KERNEL // 2 else tap * masks[k])
+            acted[:, lanes] = (total * jax.nn.sigmoid(total)).astype(jnp.bfloat16)
 
     @pl.loop(0, WIDTH // COLS)
     def _(n):
-        attended[EDGE : EDGE + tokens, here(n)] += jnp.dot(
-            context[0:tokens, :], columns(6, n), preferred_element_type=jnp.float32
+        here = pl.ds(pl.multiple_of(n * COLS, COLS), COLS)
+        attended[EDGE : EDGE + tokens, here] += jnp.dot(
+            acted[...], columns(weights, 3, 4, n), preferred_element_type=jnp.float32
         )
 
     gain_o = gain_out_ref[...]
@@ -531,41 +542,34 @@
         out_ref[rows, :] = layer_norm(taken, gain_o).astype(jnp.bfloat16)
 
 
-def conformer_block(info, hidden, normed, sources, plan, gain_conv, w_depth, gain_out, limit):
-    rows_all = normed.shape[0]
+def finish(info, hidden, context, sources, places, gain_conv, w_depth, gain_out, limit):
     rows_mid = hidden.shape[0]
     tokens = rows_mid - 2 * EDGE
     whole = pl.BlockSpec(memory_space=pltpu.VMEM)
-    scratch = [
-        pltpu.VMEM((sources[source].shape[0], rows, WIDTH), jnp.bfloat16)
-        for source, _, rows in plan
-    ]
-    scratch += [
-        pltpu.VMEM((rows_all, WIDTH), jnp.bfloat16),
-        pltpu.VMEM((rows_all, 2 * WIDTH), jnp.bfloat16),
-        pltpu.VMEM((rows_mid, WIDTH), jnp.bfloat16),
-        pltpu.VMEM((rows_mid, WIDTH), jnp.bfloat16),
-        pltpu.VMEM((rows_mid, WIDTH), jnp.float32),
-        pltpu.VMEM((WIDTH // HEAD_DIM, rows_mid, HEAD_DIM), jnp.float32),
-        pltpu.VMEM((KERNEL, tokens, HEAD_DIM), jnp.float32),
-        pltpu.VMEM((4, 128 + EDGE, 512), jnp.float32),
-        pltpu.SemaphoreType.DMA((len(plan),)),
-    ]
-    flops = 2 * rows_all * WIDTH * 2 * WIDTH + 2 * rows_mid * WIDTH * WIDTH * 5
     return pl.pallas_call(
-        functools.partial(block_kernel, tokens, limit, plan, len(sources)),
+        functools.partial(final_kernel, tokens, limit, places),
         out_shape=jax.ShapeDtypeStruct((tokens, WIDTH), jnp.bfloat16),
         in_specs=[pl.BlockSpec(memory_space=pltpu.SMEM)]
         + [whole] * 5
         + [pl.BlockSpec(memory_space=pl.ANY)] * len(sources),
         out_specs=whole,
-        scratch_shapes=scratch,
-        compiler_params=pltpu.CompilerParams(vmem_limit_bytes=44 * 1024 * 1024),
+        scratch_shapes=[
+            pltpu.VMEM((32, 4 * WIDTH // 32, WIDTH), jnp.bfloat16),
+            pltpu.VMEM((rows_mid, WIDTH), jnp.float32),
+            pltpu.VMEM((rows_mid, WIDTH), jnp.bfloat16),
+            pltpu.VMEM((rows_mid, HEAD_DIM), jnp.float32),
+            pltpu.VMEM((tokens, WIDTH), jnp.bfloat16),
+            pltpu.VMEM((KERNEL, tokens, HEAD_DIM), jnp.float32),
+            pltpu.SemaphoreType.DMA(()),
+        ],
+        compiler_params=pltpu.CompilerParams(vmem_limit_bytes=30 * 1024 * 1024),
         cost_estimate=pl.CostEstimate(
-            flops=flops, bytes_accessed=24 * 1024 * 1024, transcendentals=4 * 1024 * 1024
+            flops=8 * rows_mid * WIDTH * WIDTH,
+            bytes_accessed=14 * 1024 * 1024,
+            transcendentals=2 * 1024 * 1024,
         ),
-        name="conformer_block",
-    )(info, hidden, normed, gain_conv, w_depth, gain_out, *sources)
+        name="finish",
+    )(info, hidden, context, gain_conv, w_depth, gain_out, *sources)
 
 
 def on_device(
@@ -595,36 +599,33 @@
         ]
     ).astype(jnp.int32)
 
-    packed = pack([w_qkv, w_out, w_point_in, w_point_out])
-    gathered = lax.all_gather(packed, ("rec", "tm"), axis=0, tiled=False)
-
     w_second_all = gather_ordered(w_second)
-    if can_exchange() and w_proj.shape[0] % 16 == 0:
-        parts, held_bits = gather_unordered(w_proj)
-        places = [far for _, far in parts]
-        proj_sources = [part for part, _ in parts]
+    rest = [w_qkv], [w_out, w_point_in, w_point_out]
+    relayed = lax.axis_size("rec") == 4 and lax.axis_size("tm") == 8
+    if relayed:
+        gathered = [gather_relayed(w_proj, False, [])]
+        for arrays in rest:
+            gathered.append(gather_relayed(pack(arrays), True, gathered[-1][2]))
     else:
-        proj_sources = [lax.all_gather(w_proj, ("rec", "tm"), axis=0, tiled=True)]
-        places, held_bits = [[]], None
+        full = lax.all_gather(w_proj, ("rec", "tm"), axis=0, tiled=True)
+        gathered = [([full], None)]
+        for arrays in rest:
+            packed = pack(arrays)
+            parts = packed.shape[0] // w_out.shape[0]
+            full = lax.all_gather(packed, ("rec", "tm"), axis=0, tiled=False)
+            full = full.reshape(full.shape[0], parts, -1, WIDTH).transpose(1, 0, 2, 3)
+            full = full.reshape(parts, 32, -1, WIDTH).transpose(1, 0, 2, 3)
+            gathered.append(([full.reshape(32, -1, WIDTH)], None))
+
     patches, taps = prepare(info, mel_frames[0], w_first, tokens, limit)
     subs = subsample(patches, taps, w_second_all)
-    hidden, normed = project(info, gain_attn[None], subs, proj_sources, places, held_bits, tokens)
-
-    share = w_out.shape[0]
-    if share % 16 == 0:
-        sources = [gathered]
-        plan = [(0, k * share, share) for k in range(7)]
-    else:
-        sources = [
-            gathered[:, k * share : (k + 1) * share].reshape(1, -1, WIDTH) for k in range(7)
-        ]
-        plan = [(k, 0, WIDTH) for k in range(7)]
-    encoded = conformer_block(
+    hidden, normed = project(info, gain_attn[None], subs, *gathered[0][:2], tokens)
+    context = attend(info, normed, *gathered[1][:2], limit)
+    encoded = finish(
         info,
         hidden,
-        normed,
-        sources,
-        plan,
+        context,
+        *gathered[2][:2],
         gain_conv[None],
         w_depth,
         gain_out[None],

time: 233 us -> 254 us (1.090)
  waiting for transfers between devices: 91.3 us -> 43.3 us
  local copies, waits for them, and re-layouts: 7.93 us -> 30.2 us
  blocking collectives: 0 us -> 20.4 us
  starting transfers between devices: 30 us -> 48 us
  Pallas kernels: 85.9 us -> 92.6 us
    ppermute x17 -> x37, waiting for transfers between devices: 90 us -> 42.3 us  [exchange(): return lax.ppermute(block, axis, [(i, i ^ distance) for i in range(size)])]
    all_gather x0 -> x1, blocking collectives: none -> 20.4 us  [gather_relayed(): held = lax.all_gather(block, 'rec', axis=0, tiled=True)]
    ppermute x17 -> x37, starting transfers between devices: 18.1 us -> 37.7 us  [exchange(): return lax.ppermute(block, axis, [(i, i ^ distance) for i in range(size)])]
    unnamed x28 -> x81, local copies, waits for them, and re-layouts: 5.51 us -> 16.5 us
    pallas_call x2 -> x3, Pallas kernels: 45.8 us -> 52.7 us  [the longest x1 21.8 us: attend(): pl.pallas_call(functools.partial(attention_kernel, tokens, limit, places)...]
    ppermute x1, starting transfers between devices: 7.13 us -> 2.07 us  [prepare(): high = lax.ppermute(mel[:reach], 'tm', backward)]
    slice x0 -> x6, local copies, waits for them, and re-layouts: none -> 3.89 us  [the longest x3 2.98 us: gather_relayed(): high = exchange(above[half:], 'tm', 2)]
    slice x2, local copies, waits for them, and re-layouts: 0.94 us -> 4.68 us  [prepare(): quads[EDGE:EDGE + count]]
  transfers between devices with their start and end apart: 20 -> 40, of which waited for: 6 -> 9; matrix products, arithmetic and copies ran while one was open for 2% -> 8% of each run, Pallas kernels for 24% -> 31%
where the time goes in v2:
time: 254 us; the launch traced here: 253 us
  Pallas kernels  92.6 us (36%)
  starting transfers between devices  48 us (19%)
  waiting for transfers between devices  43.3 us (17%)
  local copies, waits for them, and re-layouts  30.2 us (12%)
  blocking collectives  20.4 us (8%)
  between operations  14 us (6%)
  other arithmetic  4.04 us (2%)
    ppermute x37, waiting for transfers between devices, exchange(): return lax.ppermute(block, axis, [(i, i ^ distance) for i in range(size)])  42.3 us
    ppermute x37, starting transfers between devices, exchange(): return lax.ppermute(block, axis, [(i, i ^ distance) for i in range(size)])  37.7 us
    pallas_call x5, Pallas kernels, subsample(): pl.pallas_call(functools.partial(conv_kernel, begin, count), out_shape=ja...  35.2 us
    pallas_call x1, Pallas kernels, attend(): pl.pallas_call(functools.partial(attention_kernel, tokens, limit, places)...  21.8 us
    all_gather x1, blocking collectives, gather_relayed(): held = lax.all_gather(block, 'rec', axis=0, tiled=True)  20.4 us
    unnamed x81, local copies, waits for them, and re-layouts  16.5 us
    pallas_call x1, Pallas kernels, project(): pl.pallas_call(functools.partial(project_kernel, places), out_shape=(jax....  16.3 us
    pallas_call x1, Pallas kernels, finish(): pl.pallas_call(functools.partial(final_kernel, tokens, limit, places), ou...  14.6 us
  transfers between devices with their start and end apart: 40, of which 9 were waited for; matrix products, arithmetic and copies ran while one was open for 8% of the time, Pallas kernels for 31%

profile of v2, /device:TPU:1, one launch (start us, length us, event | category | flops | bytes accessed | tf_op | source)
XLA Modules:
  0.0 252.6 jit_solution(7453084562967538205)
XLA Ops:
  6.6 2.2 collective-permute-start.9
  8.8 2.3 collective-permute-start.10
  11.1 1.8 constant_dynamic-update-slice_fusion.3
  12.9 9.8 %collective-permute-done.9 = bf16[160,1024]{1,0:T(8,128)(2,1)S(1)} collective-permute-done((bf16[160,1024]{1,0:T(8,128)(2,1)}, bf16[160,1024]{1,0:T(8,128)(2,1)S(1)}, u32[]{:S(2)}, u32[]{:S(2)}) %collective-permute-start.9) | collective-permute-done | bytes 327712 | tf_op jit(solution)/shard_map/ppermute | solution.py:42
  22.7 0.8 constant_dynamic-update-slice_fusion.2
  23.4 0.8 constant_dynamic-update-slice_fusion.1
  24.2 8.2 %collective-permute-done.11 = bf16[160,1024]{1,0:T(8,128)(2,1)S(1)} collective-permute-done((bf16[160,1024]{1,0:T(8,128)(2,1)}, bf16[160,1024]{1,0:T(8,128)(2,1)S(1)}, u32[]{:S(2)}, u32[]{:S(2)}) %collective-permute-start.11) | collective-permute-done | bytes 327712 | tf_op jit(solution)/shard_map/ppermute | solution.py:42
  32.4 0.7 constant_dynamic-update-slice_fusion.rest_5_
  33.1 1.2 collective-permute-start.12
  34.3 1.2 collective-permute-start.13
  35.6 1.1 collective-permute-start.2
  36.7 7.7 %collective-permute-start.3 = (bf16[1,72,256]{2,1,0:T(8,128)(2,1)S(1)}, bf16[1,72,256]{2,1,0:T(8,128)(2,1)S(1)}, u32[]{:S(2)}, u32[]{:S(2)}) collective-permute-start(bf16[1,72,256]{2,1,0:T(8,128)(2,1)S(1)} %bitcast.33), channel_id=1, source_target_pairs={{0,16},{8,24},{16,0},{24,8},{1,17},{9,25},{17,1},{25,9},{2,18},{10... | collective-permute-start | bytes 110600 | tf_op jit(solution)/shard_map/ppermute | solution.py:42
  44.5 0.7 pack.3
  45.3 20.4 %all_gather.6.rest_0_ = bf16[384,1024]{1,0:T(8,128)(2,1)S(1)} all-gather(bf16[96,1024]{1,0:T(8,128)(2,1)S(1)} %pack.2), channel_id=1, replica_groups=mesh['rec'=4,'tm'=8] {'rec'}, dimensions={0}, use_global_device_ids=true | all-gather | bytes 983040 | tf_op jit(solution)/shard_map/all_gather | solution.py:96
  65.9 8.2 %collective-permute-start = (bf16[640,80]{0,1:T(8,128)(2,1)S(1)}, bf16[640,80]{0,1:T(8,128)(2,1)S(1)}, u32[]{:S(2)}, u32[]{:S(2)}) collective-permute-start(bf16[640,80]{0,1:T(8,128)(2,1)S(1)} %get-tuple-element.24), channel_id=1, source_target_pairs={{0,1},{1,2},{2,3},{3,4},{4,5},{5,6},{6,7},{8,9},{9,10},{10,11},{11... | collective-permute-start | bytes 307208 | tf_op jit(solution)/shard_map/ppermute | solution.py:178
  74.1 2.1 collective-permute-start.1
  76.3 2.1 collective-permute-start.6
  79.1 1.1 slice.59
  80.3 1.0 collective-permute-done.1
  81.3 1.9 collective-permute-start.15
  83.2 2.6 %collective-permute-done.6 = bf16[4,72,256]{2,1,0:T(8,128)(2,1)S(1)} collective-permute-done((bf16[4,72,256]{2,1,0:T(8,128)(2,1)S(1)}, bf16[4,72,256]{2,1,0:T(8,128)(2,1)S(1)}, u32[]{:S(2)}, u32[]{:S(2)}) %collective-permute-start.6) | collective-permute-done | bytes 147488 | tf_op jit(solution)/shard_map/ppermute | solution.py:42
  86.0 1.0 pad_maximum_fusion.2
  87.0 2.1 collective-permute-start.8
  89.1 10.8 %collective-permute-done.14.rest_8_ = bf16[320,1024]{1,0:T(8,128)(2,1)} collective-permute-done((bf16[320,1024]{1,0:T(8,128)(2,1)S(1)}, bf16[320,1024]{1,0:T(8,128)(2,1)}, u32[]{:S(2)}, u32[]{:S(2)}) %collective-permute-start.14) | collective-permute-done | bytes 655392 | tf_op jit(solution)/shard_map/ppermute | solution.py:42
  100.0 1.0 collective-permute-start.21
  101.3 1.1 fusion
  102.5 1.2 copy.18
  103.7 1.8 slice.47
  105.5 2.2 copy.19
  107.7 2.4 slice.49
  110.2 1.4 pad_maximum_fusion.1.quads_ref
  111.6 3.9 %prepare.1 = (bf16[3,2,800,256]{3,2,1,0:T(8,128)(2,1)S(1)}, bf16[256,5120]{1,0:T(8,128)(2,1)S(1)}) custom-call(s32[8]{0:T(128)S(1)} %concatenate.21.info_ref, bf16[800,640]{1,0:T(8,128)(2,1)S(1)} %pad_maximum_fusion.1.quads_ref, s32[8,256]{1,0:T(8,128)S(1)} %copy-done.17, f32[9,256]{1,0:T(8,128)S(1)} %reshape.15.w_ref), custom_call_target="tpu_custom_call" | custom-call | flops 1887436800 | bytes 6291456 | tf_op jit(solution)/shard_map/prepare/pallas_call | solution.py:196
  115.6 2.4 collective-permute-start.16
  118.7 1.3 broadcast_select_fusion.1
  120.3 1.6 collective-permute-start.17
  122.4 1.0 slice.61
  123.4 4.6 %collective-permute-done.23.rest_3_ = bf16[192,1024]{1,0:T(8,128)(2,1)} collective-permute-done((bf16[192,1024]{1,0:T(8,128)(2,1)S(1)}, bf16[192,1024]{1,0:T(8,128)(2,1)}, u32[]{:S(2)}, u32[]{:S(2)}) %collective-permute-start.23) | collective-permute-done | bytes 393248 | tf_op jit(solution)/shard_map/ppermute | solution.py:42
  128.0 7.1 %subsample.9.rest_4_ = bf16[800,1024]{1,0:T(8,128)(2,1)S(1)} custom-call(bf16[3,2,800,256]{3,2,1,0:T(8,128)(2,1)S(1)} %get-tuple-element.11.a_ref, bf16[256,5120]{1,0:T(8,128)(2,1)S(1)} %get-tuple-element.12.b_ref, bf16[3,768,256]{2,1,0:T(8,128)(2,1)S(1)} %bitcast.22), custom_call_target="tpu_custom_call" | custom-call | flops 6606028800 | bytes 8388608 | tf_op jit(solution)/shard_map/subsample/pallas_call | solution.py:254
  135.2 1.2 copy-done.23
  136.5 3.2 %collective-permute-start.20 = (bf16[320,1024]{1,0:T(8,128)(2,1)}, bf16[320,1024]{1,0:T(8,128)(2,1)}, u32[]{:S(2)}, u32[]{:S(2)}) collective-permute-start(bf16[320,1024]{1,0:T(8,128)(2,1)} %collective-permute-done.15.rest_9_), channel_id=1, source_target_pairs={{0,1},{1,0},{2,3},{3,2},{4,5},{5,4},{6,7},{7,6},{8,9},{9,8},{10,11... | collective-permute-start | bytes 1966088 | tf_op jit(solution)/shard_map/ppermute | solution.py:42
  139.7 7.1 %subsample.8.rest_3_ = bf16[800,1024]{1,0:T(8,128)(2,1)S(1)} custom-call(bf16[3,2,800,256]{3,2,1,0:T(8,128)(2,1)S(1)} %get-tuple-element.11.a_ref, bf16[256,5120]{1,0:T(8,128)(2,1)S(1)} %get-tuple-element.12.b_ref, bf16[3,768,256]{2,1,0:T(8,128)(2,1)S(1)} %bitcast.23), custom_call_target="tpu_custom_call" | custom-call | flops 6606028800 | bytes 8388608 | tf_op jit(solution)/shard_map/subsample/pallas_call | solution.py:254
  146.8 1.4 copy-done.19
  148.2 1.4 copy-done.21
  149.7 1.3 copy-done.25
  151.0 0.7 collective-permute-start.30
  151.7 1.7 copy-done.20
  153.4 1.7 copy-done.22
  155.1 7.1 %subsample.7.rest_2_ = bf16[800,1024]{1,0:T(8,128)(2,1)S(1)} custom-call(bf16[3,2,800,256]{3,2,1,0:T(8,128)(2,1)S(1)} %copy-done.22, bf16[256,5120]{1,0:T(8,128)(2,1)S(1)} %copy-done.20, bf16[3,768,256]{2,1,0:T(8,128)(2,1)S(1)} %bitcast.24), custom_call_target="tpu_custom_call" | custom-call | flops 6606028800 | bytes 8388608 | tf_op jit(solution)/shard_map/subsample/pallas_call | solution.py:254
  163.4 7.1 %subsample.6.rest_1_ = bf16[800,1024]{1,0:T(8,128)(2,1)S(1)} custom-call(bf16[3,2,800,256]{3,2,1,0:T(8,128)(2,1)S(1)} %copy-done.22, bf16[256,5120]{1,0:T(8,128)(2,1)S(1)} %copy-done.20, bf16[3,768,256]{2,1,0:T(8,128)(2,1)S(1)} %bitcast.25), custom_call_target="tpu_custom_call" | custom-call | flops 6606028800 | bytes 8388608 | tf_op jit(solution)/shard_map/subsample/pallas_call | solution.py:254
  170.5 5.5 %collective-permute-done.30.rest_1_ = bf16[512,1024]{1,0:T(8,128)(2,1)S(1)} collective-permute-done((bf16[512,1024]{1,0:T(8,128)(2,1)}, bf16[512,1024]{1,0:T(8,128)(2,1)S(1)}, u32[]{:S(2)}, u32[]{:S(2)}) %collective-permute-start.30) | collective-permute-done | bytes 1048608 | tf_op jit(solution)/shard_map/ppermute | solution.py:42
  175.9 0.8 collective-permute-start.28
  177.4 6.8 %subsample.5.rest_0_ = bf16[800,1024]{1,0:T(8,128)(2,1)S(1)} custom-call(bf16[3,2,800,256]{3,2,1,0:T(8,128)(2,1)S(1)} %copy-done.22, bf16[256,5120]{1,0:T(8,128)(2,1)S(1)} %copy-done.20, bf16[3,768,256]{2,1,0:T(8,128)(2,1)S(1)} %bitcast.26), custom_call_target="tpu_custom_call" | custom-call | flops 6606028800 | bytes 8388608 | tf_op jit(solution)/shard_map/subsample/pallas_call | solution.py:254
  184.2 0.8 slice.62
  185.1 0.8 slice.63
  186.0 0.9 copy-done.7
  186.9 0.8 collective-permute-start.33
  187.7 0.7 copy-done.9
  188.4 1.0 collective-permute-start.35
  189.4 0.8 copy-done.11
  190.2 16.3 %project.1 = (f32[544,1024]{1,0:T(8,128)}, bf16[800,1024]{1,0:T(8,128)(2,1)S(1)}) custom-call(s32[8]{0:T(128)S(1)} %concatenate.21.info_ref, f32[1,1024]{1,0:T(1,128)S(1)} %bitcast.27, bf16[800,1024]{1,0:T(8,128)(2,1)S(1)} %subsample.5.rest_0_, bf16[800,1024]{1,0:T(8,128)(2,1)S(1)} %subsample.6.rest_1_, bf16[800,1024]{1,0:T(8,128)(2,1)S(1)} %subsample.7.rest_2_, ...), custom_call_target="tpu_custom_call" | custom-call | flops 8388608000 | bytes 25165824 | tf_op jit(solution)/shard_map/project/pallas_call | solution.py:310
  207.2 1.0 copy-done.10
  208.2 1.0 copy-done.12
  209.2 21.8 %attend.1.context_ref = bf16[544,1024]{1,0:T(8,128)(2,1)S(1)} custom-call(s32[8]{0:T(128)S(1)} %concatenate.21.info_ref, bf16[800,1024]{1,0:T(8,128)(2,1)S(1)} %get-tuple-element.14.normed_ref, bf16[384,1024]{1,0:T(8,128)(2,1)S(1)} %all_gather.6.rest_0_, bf16[384,1024]{1,0:T(8,128)(2,1)S(1)} %copy-done.1, bf16[384,1024]{1,0:T(8,128)(2,1)} %collective-permute-done.22.rest_2_, ...), custom_call_target="tpu_custom_call" | custom-call | flops 5833228288 | bytes 10485760 | tf_op jit(solution)/shard_map/attend/pallas_call | solution.py:450
  231.1 14.6 %finish.1 = bf16[512,1024]{1,0:T(8,128)(2,1)} custom-call(s32[8]{0:T(128)S(1)} %concatenate.21.info_ref, f32[544,1024]{1,0:T(8,128)S(1)} %copy-done.18, bf16[544,1024]{1,0:T(8,128)(2,1)S(1)} %attend.1.context_ref, f32[1,1024]{1,0:T(1,128)S(1)} %bitcast.28, f32[9,1024]{1,0:T(8,128)S(1)} %copy-done.13, f32[1,1024]{1,0:T(1,128)S(1)} %bitcast.29, ...), custom_call_target="tpu_custom_call" | custom-call | flops 4563402752 | bytes 14680064 | tf_op jit(solution)/shard_map/finish/pallas_call | solution.py:549
  (135 shorter events, 5.9 us)
Async XLA Ops:
  6.5 29.1 %copy-start.36 = (bf16[72,256]{1,0:T(8,128)(2,1)S(1)}, bf16[72,256]{1,0:T(8,128)(2,1)}, u32[]{:S(2)}) copy-start(bf16[72,256]{1,0:T(8,128)(2,1)} %param.17) | copy-start | bytes 110596
  6.5 37.9 %copy-start.4 = (bf16[32,1024]{1,0:T(8,128)(2,1)S(1)}, bf16[32,1024]{1,0:T(8,128)(2,1)}, u32[]{:S(2)}) copy-start(bf16[32,1024]{1,0:T(8,128)(2,1)} %refs_0_.3) | copy-start | bytes 196612
  6.5 37.9 %copy-start.3 = (bf16[32,2048]{1,0:T(8,128)(2,1)S(1)}, bf16[32,2048]{1,0:T(8,128)(2,1)}, u32[]{:S(2)}) copy-start(bf16[32,2048]{1,0:T(8,128)(2,1)} %refs_1_.1) | copy-start | bytes 393220
  6.5 37.9 %copy-start.5 = (bf16[32,1024]{1,0:T(8,128)(2,1)S(1)}, bf16[32,1024]{1,0:T(8,128)(2,1)}, u32[]{:S(2)}) copy-start(bf16[32,1024]{1,0:T(8,128)(2,1)} %refs_2_.1) | copy-start | bytes 196612
  6.5 144.4 %all-gather.2.cloned.1.call-start = ((), (), s32[]{:S(2)}) async-start(), calls=%async_computation | async-start | bytes 1310720 | tf_op jit(solution)/shard_map/all_gather | solution.py:96
  6.6 16.1 %collective-permute-start.9 = (bf16[160,1024]{1,0:T(8,128)(2,1)}, bf16[160,1024]{1,0:T(8,128)(2,1)S(1)}, u32[]{:S(2)}, u32[]{:S(2)}) collective-permute-start(bf16[160,1024]{1,0:T(8,128)(2,1)} %param.18), channel_id=1, source_target_pairs={{0,8},{8,0},{16,24},{24,16},{1,9},{9,1},{17,25},{25,17},{2,10},{10... | collective-permute-start | bytes 983048 | tf_op jit(solution)/shard_map/ppermute | solution.py:42
  8.8 14.7 %collective-permute-start.10 = (bf16[160,1024]{1,0:T(8,128)(2,1)}, bf16[160,1024]{1,0:T(8,128)(2,1)S(1)}, u32[]{:S(2)}, u32[]{:S(2)}) collective-permute-start(bf16[160,1024]{1,0:T(8,128)(2,1)} %param.18), channel_id=1, source_target_pairs={{0,16},{8,24},{16,0},{24,8},{1,17},{9,25},{17,1},{25,9},{2,18},{10... | collective-permute-start | bytes 983048 | tf_op jit(solution)/shard_map/ppermute | solution.py:42
  11.1 21.3 %collective-permute-start.11 = (bf16[160,1024]{1,0:T(8,128)(2,1)}, bf16[160,1024]{1,0:T(8,128)(2,1)S(1)}, u32[]{:S(2)}, u32[]{:S(2)}) collective-permute-start(bf16[160,1024]{1,0:T(8,128)(2,1)} %param.18), channel_id=1, source_target_pairs={{0,24},{8,16},{16,8},{24,0},{1,25},{9,17},{17,9},{25,1},{2,26},{10... | collective-permute-start | bytes 983048 | tf_op jit(solution)/shard_map/ppermute | solution.py:42
  12.9 32.4 %copy-start.2 = (bf16[32,3072]{1,0:T(8,128)(2,1)S(1)}, bf16[32,3072]{1,0:T(8,128)(2,1)}, u32[]{:S(2)}) copy-start(bf16[32,3072]{1,0:T(8,128)(2,1)} %refs_0_.2) | copy-start | bytes 589828
  24.2 41.5 %copy-start.35 = (bf16[1,2048,80]{1,2,0:T(8,128)(2,1)S(1)}, bf16[1,2048,80]{1,2,0:T(8,128)(2,1)}, u32[]{:S(2)}) copy-start(bf16[1,2048,80]{1,2,0:T(8,128)(2,1)} %param.14) | copy-start | bytes 983044
  33.1 32.6 %copy-start.37 = (f32[3,3,256]{2,1,0:T(4,128)S(1)}, f32[3,3,256]{2,1,0:T(4,128)}, u32[]{:S(2)}) copy-start(f32[3,3,256]{2,1,0:T(4,128)} %param.16) | copy-start | bytes 27652
  33.1 43.2 %collective-permute-start.12 = (bf16[640,1024]{1,0:T(8,128)(2,1)}, bf16[640,1024]{1,0:T(8,128)(2,1)S(1)}, u32[]{:S(2)}, u32[]{:S(2)}) collective-permute-start(bf16[640,1024]{1,0:T(8,128)(2,1)} %constant_dynamic-update-slice_fusion.rest_5_), channel_id=1, source_target_pairs={{0,2},{1,3},{2,0},{3,1},{4,6},{5,7},{6,4},{7,5},{8,10},{9,11},{10,... | collective-permute-start | bytes 3932168 | tf_op jit(solution)/shard_map/ppermute | solution.py:42
  34.3 44.1 %collective-permute-start.13 = (bf16[640,1024]{1,0:T(8,128)(2,1)}, bf16[640,1024]{1,0:T(8,128)(2,1)}, u32[]{:S(2)}, u32[]{:S(2)}) collective-permute-start(bf16[640,1024]{1,0:T(8,128)(2,1)} %constant_dynamic-update-slice_fusion.rest_5_), channel_id=1, source_target_pairs={{0,4},{1,5},{2,6},{3,7},{4,0},{5,1},{6,2},{7,3},{8,12},{9,13},{10,... | collective-permute-start | bytes 3932168 | tf_op jit(solution)/shard_map/ppermute | solution.py:42
  35.6 30.2 %copy-start.38 = (s32[1,4]{1,0:T(1,128)S(1)}, s32[1,4]{1,0:T(1,128)}, u32[]{:S(2)}) copy-start(s32[1,4]{1,0:T(1,128)} %param.15) | copy-start | bytes 52
  35.6 30.3 %collective-permute-start.2 = (bf16[1,72,256]{2,1,0:T(8,128)(2,1)S(1)}, bf16[1,72,256]{2,1,0:T(8,128)(2,1)S(1)}, u32[]{:S(2)}, u32[]{:S(2)}) collective-permute-start(bf16[1,72,256]{2,1,0:T(8,128)(2,1)S(1)} %bitcast.32), channel_id=1, source_target_pairs={{0,24},{8,16},{16,8},{24,0},{1,25},{9,17},{17,9},{25,1},{2,26},{10... | collective-permute-start | bytes 110600 | tf_op jit(solution)/shard_map/ppermute | solution.py:42
  36.7 37.4 %collective-permute-start.3 = (bf16[1,72,256]{2,1,0:T(8,128)(2,1)S(1)}, bf16[1,72,256]{2,1,0:T(8,128)(2,1)S(1)}, u32[]{:S(2)}, u32[]{:S(2)}) collective-permute-start(bf16[1,72,256]{2,1,0:T(8,128)(2,1)S(1)} %bitcast.33), channel_id=1, source_target_pairs={{0,16},{8,24},{16,0},{24,8},{1,17},{9,25},{17,1},{25,9},{2,18},{10... | collective-permute-start | bytes 110600 | tf_op jit(solution)/shard_map/ppermute | solution.py:42
  44.4 31.8 %collective-permute-start.4 = (bf16[1,72,256]{2,1,0:T(8,128)(2,1)S(1)}, bf16[1,72,256]{2,1,0:T(8,128)(2,1)S(1)}, u32[]{:S(2)}, u32[]{:S(2)}) collective-permute-start(bf16[1,72,256]{2,1,0:T(8,128)(2,1)S(1)} %bitcast.34), channel_id=1, source_target_pairs={{0,8},{8,0},{16,24},{24,16},{1,9},{9,1},{17,25},{25,17},{2,10},{10... | collective-permute-start | bytes 110600 | tf_op jit(solution)/shard_map/ppermute | solution.py:42
  65.9 14.3 %collective-permute-start = (bf16[640,80]{0,1:T(8,128)(2,1)S(1)}, bf16[640,80]{0,1:T(8,128)(2,1)S(1)}, u32[]{:S(2)}, u32[]{:S(2)}) collective-permute-start(bf16[640,80]{0,1:T(8,128)(2,1)S(1)} %get-tuple-element.24), channel_id=1, source_target_pairs={{0,1},{1,2},{2,3},{3,4},{4,5},{5,6},{6,7},{8,9},{9,10},{10,11},{11... | collective-permute-start | bytes 307208 | tf_op jit(solution)/shard_map/ppermute | solution.py:178
  74.1 7.2 %collective-permute-start.1 = (bf16[640,80]{0,1:T(8,128)(2,1)S(1)}, bf16[640,80]{0,1:T(8,128)(2,1)S(1)}, u32[]{:S(2)}, u32[]{:S(2)}) collective-permute-start(bf16[640,80]{0,1:T(8,128)(2,1)S(1)} %get-tuple-element.25), channel_id=1, source_target_pairs={{1,0},{2,1},{3,2},{4,3},{5,4},{6,5},{7,6},{9,8},{10,9},{11,10},{12... | collective-permute-start | bytes 307208 | tf_op jit(solution)/shard_map/ppermute | solution.py:179
  76.2 7.0 %collective-permute-start.5 = (bf16[4,72,256]{2,1,0:T(8,128)(2,1)S(1)}, bf16[4,72,256]{2,1,0:T(8,128)(2,1)S(1)}, u32[]{:S(2)}, u32[]{:S(2)}) collective-permute-start(bf16[4,72,256]{2,1,0:T(8,128)(2,1)S(1)} %pad_maximum_fusion.4), channel_id=1, source_target_pairs={{0,6},{1,7},{2,4},{3,5},{4,2},{5,3},{6,0},{7,1},{8,14},{9,15},{10,... | collective-permute-start | bytes 442376 | tf_op jit(solution)/shard_map/ppermute | solution.py:42
  76.3 9.5 %collective-permute-start.6 = (bf16[4,72,256]{2,1,0:T(8,128)(2,1)S(1)}, bf16[4,72,256]{2,1,0:T(8,128)(2,1)S(1)}, u32[]{:S(2)}, u32[]{:S(2)}) collective-permute-start(bf16[4,72,256]{2,1,0:T(8,128)(2,1)S(1)} %pad_maximum_fusion.4), channel_id=1, source_target_pairs={{0,4},{1,5},{2,6},{3,7},{4,0},{5,1},{6,2},{7,3},{8,12},{9,13},{10,... | collective-permute-start | bytes 442376 | tf_op jit(solution)/shard_map/ppermute | solution.py:42
  78.5 7.3 %collective-permute-start.7 = (bf16[4,72,256]{2,1,0:T(8,128)(2,1)S(1)}, bf16[4,72,256]{2,1,0:T(8,128)(2,1)S(1)}, u32[]{:S(2)}, u32[]{:S(2)}) collective-permute-start(bf16[4,72,256]{2,1,0:T(8,128)(2,1)S(1)} %pad_maximum_fusion.4), channel_id=1, source_target_pairs={{0,2},{1,3},{2,0},{3,1},{4,6},{5,7},{6,4},{7,5},{8,10},{9,11},{10,... | collective-permute-start | bytes 442376 | tf_op jit(solution)/shard_map/ppermute | solution.py:42
  80.2 19.7 %collective-permute-start.14 = (bf16[320,1024]{1,0:T(8,128)(2,1)S(1)}, bf16[320,1024]{1,0:T(8,128)(2,1)}, u32[]{:S(2)}, u32[]{:S(2)}) collective-permute-start(bf16[320,1024]{1,0:T(8,128)(2,1)S(1)} %slice.58), channel_id=1, source_target_pairs={{0,4},{1,5},{2,6},{3,7},{4,0},{5,1},{6,2},{7,3},{8,12},{9,13},{10,... | collective-permute-start | bytes 1966088 | tf_op jit(solution)/shard_map/ppermute | solution.py:42
  81.3 18.7 %collective-permute-start.15 = (bf16[320,1024]{1,0:T(8,128)(2,1)S(1)}, bf16[320,1024]{1,0:T(8,128)(2,1)}, u32[]{:S(2)}, u32[]{:S(2)}) collective-permute-start(bf16[320,1024]{1,0:T(8,128)(2,1)S(1)} %slice.59), channel_id=1, source_target_pairs={{0,2},{1,3},{2,0},{3,1},{4,6},{5,7},{6,4},{7,5},{8,10},{9,11},{10,... | collective-permute-start | bytes 1966088 | tf_op jit(solution)/shard_map/ppermute | solution.py:42
  85.9 16.6 %copy-start.33 = (bf16[4,72,256]{2,1,0:T(8,128)(2,1)}, bf16[4,72,256]{2,1,0:T(8,128)(2,1)S(1)}, u32[]{:S(2)}) copy-start(bf16[4,72,256]{2,1,0:T(8,128)(2,1)S(1)} %broadcast_select_fusion.6) | copy-start | bytes 442372
  85.9 16.5 %copy-start.27 = (bf16[4,72,256]{2,1,0:T(8,128)(2,1)}, bf16[4,72,256]{2,1,0:T(8,128)(2,1)S(1)}, u32[]{:S(2)}) copy-start(bf16[4,72,256]{2,1,0:T(8,128)(2,1)S(1)} %get-tuple-element.19) | copy-start | bytes 442372
  85.9 16.5 %copy-start.29 = (bf16[4,72,256]{2,1,0:T(8,128)(2,1)}, bf16[4,72,256]{2,1,0:T(8,128)(2,1)S(1)}, u32[]{:S(2)}) copy-start(bf16[4,72,256]{2,1,0:T(8,128)(2,1)S(1)} %get-tuple-element.20) | copy-start | bytes 442372
  86.0 16.5 %copy-start.31 = (bf16[4,72,256]{2,1,0:T(8,128)(2,1)}, bf16[4,72,256]{2,1,0:T(8,128)(2,1)S(1)}, u32[]{:S(2)}) copy-start(bf16[4,72,256]{2,1,0:T(8,128)(2,1)S(1)} %get-tuple-element.21) | copy-start | bytes 442372
  87.0 31.7 %collective-permute-start.8 = (bf16[16,72,256]{2,1,0:T(8,128)(2,1)}, bf16[16,72,256]{2,1,0:T(8,128)(2,1)}, u32[]{:S(2)}, u32[]{:S(2)}) collective-permute-start(bf16[16,72,256]{2,1,0:T(8,128)(2,1)} %pad_maximum_fusion.2), channel_id=1, source_target_pairs={{0,1},{1,0},{2,3},{3,2},{4,5},{5,4},{6,7},{7,6},{8,9},{9,8},{10,11... | collective-permute-start | bytes 1769480 | tf_op jit(solution)/shard_map/ppermute | solution.py:42
  100.0 18.6 %collective-permute-start.21 = (bf16[384,1024]{1,0:T(8,128)(2,1)S(1)}, bf16[384,1024]{1,0:T(8,128)(2,1)S(1)}, u32[]{:S(2)}, u32[]{:S(2)}) collective-permute-start(bf16[384,1024]{1,0:T(8,128)(2,1)S(1)} %all_gather.6.rest_0_), channel_id=1, source_target_pairs={{0,2},{1,3},{2,0},{3,1},{4,6},{5,7},{6,4},{7,5},{8,10},{9,11},{10,... | collective-permute-start | bytes 2359304 | tf_op jit(solution)/shard_map/ppermute | solution.py:42
  100.9 21.0 %collective-permute-start.22 = (bf16[384,1024]{1,0:T(8,128)(2,1)S(1)}, bf16[384,1024]{1,0:T(8,128)(2,1)}, u32[]{:S(2)}, u32[]{:S(2)}) collective-permute-start(bf16[384,1024]{1,0:T(8,128)(2,1)S(1)} %all_gather.6.rest_0_), channel_id=1, source_target_pairs={{0,4},{1,5},{2,6},{3,7},{4,0},{5,1},{6,2},{7,3},{8,12},{9,13},{10,... | collective-permute-start | bytes 2359304 | tf_op jit(solution)/shard_map/ppermute | solution.py:42
  111.6 7.1 %copy-start.28 = (bf16[4,72,256]{2,1,0:T(8,128)(2,1)S(1)}, bf16[4,72,256]{2,1,0:T(8,128)(2,1)}, u32[]{:S(2)}) copy-start(bf16[4,72,256]{2,1,0:T(8,128)(2,1)} %copy-done.27) | copy-start | bytes 442372
  111.6 7.1 %copy-start.30 = (bf16[4,72,256]{2,1,0:T(8,128)(2,1)S(1)}, bf16[4,72,256]{2,1,0:T(8,128)(2,1)}, u32[]{:S(2)}) copy-start(bf16[4,72,256]{2,1,0:T(8,128)(2,1)} %copy-done.29) | copy-start | bytes 442372
  111.6 7.1 %copy-start.32 = (bf16[4,72,256]{2,1,0:T(8,128)(2,1)S(1)}, bf16[4,72,256]{2,1,0:T(8,128)(2,1)}, u32[]{:S(2)}) copy-start(bf16[4,72,256]{2,1,0:T(8,128)(2,1)} %copy-done.31) | copy-start | bytes 442372
  111.6 7.1 %copy-start.34 = (bf16[4,72,256]{2,1,0:T(8,128)(2,1)S(1)}, bf16[4,72,256]{2,1,0:T(8,128)(2,1)}, u32[]{:S(2)}) copy-start(bf16[4,72,256]{2,1,0:T(8,128)(2,1)} %copy-done.33) | copy-start | bytes 442372
  115.6 35.4 %collective-permute-start.16 = (bf16[640,1024]{1,0:T(8,128)(2,1)}, bf16[640,1024]{1,0:T(8,128)(2,1)}, u32[]{:S(2)}, u32[]{:S(2)}) collective-permute-start(bf16[640,1024]{1,0:T(8,128)(2,1)} %constant_dynamic-update-slice_fusion.rest_5_), channel_id=1, source_target_pairs={{0,1},{1,0},{2,3},{3,2},{4,5},{5,4},{6,7},{7,6},{8,9},{9,8},{10,11... | collective-permute-start | bytes 3932168 | tf_op jit(solution)/shard_map/ppermute | solution.py:42
  118.6 9.4 %collective-permute-start.23 = (bf16[192,1024]{1,0:T(8,128)(2,1)S(1)}, bf16[192,1024]{1,0:T(8,128)(2,1)}, u32[]{:S(2)}, u32[]{:S(2)}) collective-permute-start(bf16[192,1024]{1,0:T(8,128)(2,1)S(1)} %slice.60), channel_id=1, source_target_pairs={{0,4},{1,5},{2,6},{3,7},{4,0},{5,1},{6,2},{7,3},{8,12},{9,13},{10,... | collective-permute-start | bytes 1179656 | tf_op jit(solution)/shard_map/ppermute | solution.py:42
  120.3 42.6 %collective-permute-start.17 = (bf16[640,1024]{1,0:T(8,128)(2,1)S(1)}, bf16[640,1024]{1,0:T(8,128)(2,1)}, u32[]{:S(2)}, u32[]{:S(2)}) collective-permute-start(bf16[640,1024]{1,0:T(8,128)(2,1)S(1)} %collective-permute-done.12.rest_6_), channel_id=1, source_target_pairs={{0,1},{1,0},{2,3},{3,2},{4,5},{5,4},{6,7},{7,6},{8,9},{9,8},{10,11... | collective-permute-start | bytes 3932168 | tf_op jit(solution)/shard_map/ppermute | solution.py:42
  121.8 41.1 %collective-permute-start.18 = (bf16[640,1024]{1,0:T(8,128)(2,1)}, bf16[640,1024]{1,0:T(8,128)(2,1)}, u32[]{:S(2)}, u32[]{:S(2)}) collective-permute-start(bf16[640,1024]{1,0:T(8,128)(2,1)} %collective-permute-done.13.rest_7_), channel_id=1, source_target_pairs={{0,1},{1,0},{2,3},{3,2},{4,5},{5,4},{6,7},{7,6},{8,9},{9,8},{10,11... | collective-permute-start | bytes 3932168 | tf_op jit(solution)/shard_map/ppermute | solution.py:42
  121.9 29.7 %collective-permute-start.19 = (bf16[320,1024]{1,0:T(8,128)(2,1)}, bf16[320,1024]{1,0:T(8,128)(2,1)}, u32[]{:S(2)}, u32[]{:S(2)}) collective-permute-start(bf16[320,1024]{1,0:T(8,128)(2,1)} %collective-permute-done.14.rest_8_), channel_id=1, source_target_pairs={{0,1},{1,0},{2,3},{3,2},{4,5},{5,4},{6,7},{7,6},{8,9},{9,8},{10,11... | collective-permute-start | bytes 1966088 | tf_op jit(solution)/shard_map/ppermute | solution.py:42
  128.0 8.4 %collective-permute-start.24 = (bf16[192,1024]{1,0:T(8,128)(2,1)S(1)}, bf16[192,1024]{1,0:T(8,128)(2,1)}, u32[]{:S(2)}, u32[]{:S(2)}) collective-permute-start(bf16[192,1024]{1,0:T(8,128)(2,1)S(1)} %slice.61), channel_id=1, source_target_pairs={{0,2},{1,3},{2,0},{3,1},{4,6},{5,7},{6,4},{7,5},{8,10},{9,11},{10,... | collective-permute-start | bytes 1179656 | tf_op jit(solution)/shard_map/ppermute | solution.py:42
  136.5 25.8 %collective-permute-start.20 = (bf16[320,1024]{1,0:T(8,128)(2,1)}, bf16[320,1024]{1,0:T(8,128)(2,1)}, u32[]{:S(2)}, u32[]{:S(2)}) collective-permute-start(bf16[320,1024]{1,0:T(8,128)(2,1)} %collective-permute-done.15.rest_9_), channel_id=1, source_target_pairs={{0,1},{1,0},{2,3},{3,2},{4,5},{5,4},{6,7},{7,6},{8,9},{9,8},{10,11... | collective-permute-start | bytes 1966088 | tf_op jit(solution)/shard_map/ppermute | solution.py:42
  150.9 11.9 %copy-start.1 = (bf16[384,1024]{1,0:T(8,128)(2,1)S(1)}, bf16[384,1024]{1,0:T(8,128)(2,1)}, u32[]{:S(2)}) copy-start(bf16[384,1024]{1,0:T(8,128)(2,1)} %copy-done) | copy-start | bytes 2359300
  151.0 25.0 %collective-permute-start.30 = (bf16[512,1024]{1,0:T(8,128)(2,1)}, bf16[512,1024]{1,0:T(8,128)(2,1)S(1)}, u32[]{:S(2)}, u32[]{:S(2)}) collective-permute-start(bf16[512,1024]{1,0:T(8,128)(2,1)} %all-gather.2.cloned.1.call-done.rest_0_), channel_id=1, source_target_pairs={{0,2},{1,3},{2,0},{3,1},{4,6},{5,7},{6,4},{7,5},{8,10},{9,11},{10,... | collective-permute-start | bytes 3145736 | tf_op jit(solution)/shard_map/ppermute | solution.py:42
  151.6 25.1 %collective-permute-start.31 = (bf16[512,1024]{1,0:T(8,128)(2,1)}, bf16[512,1024]{1,0:T(8,128)(2,1)S(1)}, u32[]{:S(2)}, u32[]{:S(2)}) collective-permute-start(bf16[512,1024]{1,0:T(8,128)(2,1)} %all-gather.2.cloned.1.call-done.rest_0_), channel_id=1, source_target_pairs={{0,4},{1,5},{2,6},{3,7},{4,0},{5,1},{6,2},{7,3},{8,12},{9,13},{10,... | collective-permute-start | bytes 3145736 | tf_op jit(solution)/shard_map/ppermute | solution.py:42
  162.2 23.7 %collective-permute-start.25 = (bf16[384,1024]{1,0:T(8,128)(2,1)S(1)}, bf16[384,1024]{1,0:T(8,128)(2,1)S(1)}, u32[]{:S(2)}, u32[]{:S(2)}) collective-permute-start(bf16[384,1024]{1,0:T(8,128)(2,1)S(1)} %all_gather.6.rest_0_), channel_id=1, source_target_pairs={{0,1},{1,0},{2,3},{3,2},{4,5},{5,4},{6,7},{7,6},{8,9},{9,8},{10,11... | collective-permute-start | bytes 2359304 | tf_op jit(solution)/shard_map/ppermute | solution.py:42
  162.9 23.1 %collective-permute-start.26 = (bf16[384,1024]{1,0:T(8,128)(2,1)S(1)}, bf16[384,1024]{1,0:T(8,128)(2,1)S(1)}, u32[]{:S(2)}, u32[]{:S(2)}) collective-permute-start(bf16[384,1024]{1,0:T(8,128)(2,1)S(1)} %copy-done.1), channel_id=1, source_target_pairs={{0,1},{1,0},{2,3},{3,2},{4,5},{5,4},{6,7},{7,6},{8,9},{9,8},{10,11... | collective-permute-start | bytes 2359304 | tf_op jit(solution)/shard_map/ppermute | solution.py:42
  162.9 23.1 %collective-permute-start.27 = (bf16[384,1024]{1,0:T(8,128)(2,1)}, bf16[384,1024]{1,0:T(8,128)(2,1)S(1)}, u32[]{:S(2)}, u32[]{:S(2)}) collective-permute-start(bf16[384,1024]{1,0:T(8,128)(2,1)} %collective-permute-done.22.rest_2_), channel_id=1, source_target_pairs={{0,1},{1,0},{2,3},{3,2},{4,5},{5,4},{6,7},{7,6},{8,9},{9,8},{10,11... | collective-permute-start | bytes 2359304 | tf_op jit(solution)/shard_map/ppermute | solution.py:42
  175.9 11.7 %collective-permute-start.28 = (bf16[192,1024]{1,0:T(8,128)(2,1)}, bf16[192,1024]{1,0:T(8,128)(2,1)S(1)}, u32[]{:S(2)}, u32[]{:S(2)}) collective-permute-start(bf16[192,1024]{1,0:T(8,128)(2,1)} %collective-permute-done.23.rest_3_), channel_id=1, source_target_pairs={{0,1},{1,0},{2,3},{3,2},{4,5},{5,4},{6,7},{7,6},{8,9},{9,8},{10,11... | collective-permute-start | bytes 1179656 | tf_op jit(solution)/shard_map/ppermute | solution.py:42
  176.7 12.7 %collective-permute-start.29 = (bf16[192,1024]{1,0:T(8,128)(2,1)}, bf16[192,1024]{1,0:T(8,128)(2,1)S(1)}, u32[]{:S(2)}, u32[]{:S(2)}) collective-permute-start(bf16[192,1024]{1,0:T(8,128)(2,1)} %collective-permute-done.24.rest_4_), channel_id=1, source_target_pairs={{0,1},{1,0},{2,3},{3,2},{4,5},{5,4},{6,7},{7,6},{8,9},{9,8},{10,11... | collective-permute-start | bytes 1179656 | tf_op jit(solution)/shard_map/ppermute | solution.py:42
  177.4 12.8 %copy-start.24 = (bf16[800,1024]{1,0:T(8,128)(2,1)S(1)}, bf16[800,1024]{1,0:T(8,128)(2,1)}, u32[]{:S(2)}) copy-start(bf16[800,1024]{1,0:T(8,128)(2,1)} %copy-done.23) | copy-start | bytes 4915204
  177.4 12.8 %copy-start.26 = (bf16[800,1024]{1,0:T(8,128)(2,1)S(1)}, bf16[800,1024]{1,0:T(8,128)(2,1)}, u32[]{:S(2)}) copy-start(bf16[800,1024]{1,0:T(8,128)(2,1)} %copy-done.25) | copy-start | bytes 4915204
  185.9 45.1 %collective-permute-start.34 = (bf16[512,1024]{1,0:T(8,128)(2,1)S(1)}, bf16[512,1024]{1,0:T(8,128)(2,1)S(1)}, u32[]{:S(2)}, u32[]{:S(2)}) collective-permute-start(bf16[512,1024]{1,0:T(8,128)(2,1)S(1)} %copy-done.6), channel_id=1, source_target_pairs={{0,1},{1,0},{2,3},{3,2},{4,5},{5,4},{6,7},{7,6},{8,9},{9,8},{10,11... | collective-permute-start | bytes 3145736 | tf_op jit(solution)/shard_map/ppermute | solution.py:42
  185.9 20.6 %collective-permute-start.32 = (bf16[256,1024]{1,0:T(8,128)(2,1)}, bf16[256,1024]{1,0:T(8,128)(2,1)S(1)}, u32[]{:S(2)}, u32[]{:S(2)}) collective-permute-start(bf16[256,1024]{1,0:T(8,128)(2,1)} %slice.62), channel_id=1, source_target_pairs={{0,4},{1,5},{2,6},{3,7},{4,0},{5,1},{6,2},{7,3},{8,12},{9,13},{10,... | collective-permute-start | bytes 1572872 | tf_op jit(solution)/shard_map/ppermute | solution.py:42
  186.9 20.2 %collective-permute-start.33 = (bf16[256,1024]{1,0:T(8,128)(2,1)}, bf16[256,1024]{1,0:T(8,128)(2,1)}, u32[]{:S(2)}, u32[]{:S(2)}) collective-permute-start(bf16[256,1024]{1,0:T(8,128)(2,1)} %slice.63), channel_id=1, source_target_pairs={{0,2},{1,3},{2,0},{3,1},{4,6},{5,7},{6,4},{7,5},{8,10},{9,11},{10,... | collective-permute-start | bytes 1572872 | tf_op jit(solution)/shard_map/ppermute | solution.py:42
  188.4 42.6 %collective-permute-start.35 = (bf16[512,1024]{1,0:T(8,128)(2,1)S(1)}, bf16[512,1024]{1,0:T(8,128)(2,1)S(1)}, u32[]{:S(2)}, u32[]{:S(2)}) collective-permute-start(bf16[512,1024]{1,0:T(8,128)(2,1)S(1)} %collective-permute-done.30.rest_1_), channel_id=1, source_target_pairs={{0,1},{1,0},{2,3},{3,2},{4,5},{5,4},{6,7},{7,6},{8,9},{9,8},{10,11... | collective-permute-start | bytes 3145736 | tf_op jit(solution)/shard_map/ppermute | solution.py:42
  190.2 40.9 %collective-permute-start.36 = (bf16[512,1024]{1,0:T(8,128)(2,1)S(1)}, bf16[512,1024]{1,0:T(8,128)(2,1)S(1)}, u32[]{:S(2)}, u32[]{:S(2)}) collective-permute-start(bf16[512,1024]{1,0:T(8,128)(2,1)S(1)} %collective-permute-done.31.rest_2_), channel_id=1, source_target_pairs={{0,1},{1,0},{2,3},{3,2},{4,5},{5,4},{6,7},{7,6},{8,9},{9,8},{10,11... | collective-permute-start | bytes 3145736 | tf_op jit(solution)/shard_map/ppermute | solution.py:42
  190.2 17.0 %copy-start.8 = (bf16[384,1024]{1,0:T(8,128)(2,1)S(1)}, bf16[384,1024]{1,0:T(8,128)(2,1)}, u32[]{:S(2)}) copy-start(bf16[384,1024]{1,0:T(8,128)(2,1)} %copy-done.7) | copy-start | bytes 2359300
  206.5 24.5 %collective-permute-start.37 = (bf16[256,1024]{1,0:T(8,128)(2,1)S(1)}, bf16[256,1024]{1,0:T(8,128)(2,1)S(1)}, u32[]{:S(2)}, u32[]{:S(2)}) collective-permute-start(bf16[256,1024]{1,0:T(8,128)(2,1)S(1)} %collective-permute-done.32.rest_3_), channel_id=1, source_target_pairs={{0,1},{1,0},{2,3},{3,2},{4,5},{5,4},{6,7},{7,6},{8,9},{9,8},{10,11... | collective-permute-start | bytes 1572872 | tf_op jit(solution)/shard_map/ppermute | solution.py:42
  207.1 23.9 %collective-permute-start.38 = (bf16[256,1024]{1,0:T(8,128)(2,1)}, bf16[256,1024]{1,0:T(8,128)(2,1)S(1)}, u32[]{:S(2)}, u32[]{:S(2)}) collective-permute-start(bf16[256,1024]{1,0:T(8,128)(2,1)} %collective-permute-done.33.rest_4_), channel_id=1, source_target_pairs={{0,1},{1,0},{2,3},{3,2},{4,5},{5,4},{6,7},{7,6},{8,9},{9,8},{10,11... | collective-permute-start | bytes 1572872 | tf_op jit(solution)/shard_map/ppermute | solution.py:42
  209.2 21.9 %copy-start.13 = (f32[9,1024]{1,0:T(8,128)S(1)}, f32[9,1024]{1,0:T(8,128)}, u32[]{:S(2)}) copy-start(f32[9,1024]{1,0:T(8,128)} %depth_ref.1) | copy-start | bytes 110596
  209.2 21.9 %copy-start.15 = (f32[1024]{0:T(1024)S(1)}, f32[1024]{0:T(1024)}, u32[]{:S(2)}) copy-start(f32[1024]{0:T(1024)} %param.22) | copy-start | bytes 12292
  209.2 21.9 %copy-start.16 = (f32[1024]{0:T(1024)S(1)}, f32[1024]{0:T(1024)}, u32[]{:S(2)}) copy-start(f32[1024]{0:T(1024)} %param.26) | copy-start | bytes 12292
  209.2 21.9 %copy-start.18 = (f32[544,1024]{1,0:T(8,128)S(1)}, f32[544,1024]{1,0:T(8,128)}, u32[]{:S(2)}) copy-start(f32[544,1024]{1,0:T(8,128)} %get-tuple-element.13.hidden_ref) | copy-start | bytes 6684676
  (15 other events, 23.7 us)
Sparse Core Ops, SparseCore 0:
  45.4 35.3 all-gather.1

commit v3 on v2

--- a/solution.py
+++ b/solution.py
@@ -65,21 +65,23 @@
     )
 
 
+def behind(value, *others):
+    return lax.optimization_barrier((value, *others))[0]
+
+
 def gather_ordered(block):
     if not can_exchange():
-        return lax.all_gather(block, ("rec", "tm"), axis=0, tiled=True)
-    groups = bit_groups()
+        return lax.all_gather(block, ("rec", "tm"), axis=0, tiled=True), []
     names = []
-    rows = block.shape[0]
     held = block[None]
-    for axis, bits in groups:
+    rounds = []
+    for axis, bits in bit_groups():
         got = [held] + [exchange(held, axis, d) for d in distances(bits)[1:]]
+        rounds.append(got[1:])
         me = lax.axis_index(axis)
         for at, bit in enumerate(bits):
             high = (me & bit) != 0
-            got = [
-                jnp.where(high, got[k ^ (1 << at)], got[k]) for k in range(len(got))
-            ]
+            got = [jnp.where(high, got[k ^ (1 << at)], got[k]) for k in range(len(got))]
         held = jnp.concatenate(got, axis=0)
         names = [(axis, bit) for bit in reversed(bits)] + names
     wanted = []
@@ -88,24 +90,26 @@
     order = [names.index(n) for n in wanted]
     dims = held.reshape((2,) * len(names) + block.shape)
     dims = jnp.transpose(dims, order + [len(names), len(names) + 1])
-    return dims.reshape((-1,) + block.shape[1:])
-
-
-def gather_relayed(block, whole_rec, after):
-    if whole_rec:
-        held = lax.all_gather(block, "rec", axis=0, tiled=True)
-    else:
-        held = jnp.concatenate([block] + [exchange(block, "rec", d) for d in (1, 2, 3)], axis=0)
-    if after:
-        held = lax.optimization_barrier((held, *after))[0]
+    return dims.reshape((-1,) + block.shape[1:]), rounds
+
+
+def along_rec(block):
+    return [block] + [exchange(block, "rec", d) for d in (1, 2, 3)]
+
+
+def to_neighbours(held):
+    return held, exchange(held, "tm", 2), exchange(held, "tm", 4)
+
+
+def relayed(held, beside, above):
     half = held.shape[0] // 2
-    beside = exchange(held, "tm", 2)
-    above = exchange(held, "tm", 4)
-    low = exchange(beside[:half], "tm", 4)
-    high = exchange(above[half:], "tm", 2)
+    return exchange(beside[:half], "tm", 4), exchange(above[half:], "tm", 2)
+
+
+def to_other_core(held, beside, above, low, high):
     pieces = [(held, 0, 0, 4), (beside, 2, 0, 4), (above, 4, 0, 4), (low, 6, 0, 2), (high, 6, 2, 2)]
     pieces += [(exchange(p, "tm", 1), far ^ 1, slot, n) for p, far, slot, n in pieces]
-    return [p[0] for p in pieces], [p[1:] + (whole_rec,) for p in pieces], [low, high]
+    return [p[0] for p in pieces], [p[1:] for p in pieces]
 
 
 def copies_in(info_ref, sources, places, target, sem):
@@ -113,11 +117,10 @@
         pltpu.make_async_copy(sources[0], target, sem).start()
         return
     rec, tm, tm_size = info_ref[5], info_ref[6], info_ref[7]
-    for source, (far, first, number, indices) in zip(sources, places):
+    for source, (far, first, number) in zip(sources, places):
         rows = source.shape[0] // number
         for slot in range(number):
-            owner_rec = first + slot if indices else rec ^ (first + slot)
-            owner = owner_rec * tm_size + (tm ^ far)
+            owner = (rec ^ (first + slot)) * tm_size + (tm ^ far)
             if len(target.shape) == 3:
                 place = target.at[owner]
             else:
@@ -366,13 +369,35 @@
     return weights[:, part * rows : (part + 1) * rows, here].reshape(-1, COLS)
 
 
-def attention_kernel(tokens, limit, places, info_ref, normed_ref, *rest):
-    sources = rest[:-7]
-    context_ref, weights, keys, values, queries, biases, sem = rest[-7:]
+def block_kernel(
+    tokens,
+    limit,
+    info_ref,
+    hidden_ref,
+    normed_ref,
+    gain_conv_ref,
+    depth_ref,
+    gain_out_ref,
+    *rest,
+):
+    late, out_ref, early_w, late_w, keys, values, queries, context, attended, gated, masks = rest[
+        :11
+    ]
+    biases, sems = rest[11:]
     rows_mid = tokens + 2 * EDGE
-    copies_in(info_ref, sources, places, weights, sem)
+    mid = slice(WINDOW, WINDOW + rows_mid)
+    early_rows, late_rows = early_w.shape[1], late_w.shape[1]
+    early_copy = pltpu.make_async_copy(late.at[:, pl.ds(0, early_rows), :], early_w, sems.at[0])
+    late_copy = pltpu.make_async_copy(
+        late.at[:, pl.ds(early_rows, late_rows), :], late_w, sems.at[1]
+    )
+    early_copy.start()
+    late_copy.start()
     base = info_ref[0]
     lengths = [info_ref[1 + k] for k in range(4)]
+
+    def here(n):
+        return pl.ds(pl.multiple_of(n * COLS, COLS), COLS)
 
     blocks = []
     at_row = 0
@@ -381,6 +406,11 @@
         blocks.append((at_row, size))
         at_row += size
 
+    row = lax.broadcasted_iota(jnp.int32, (tokens, HEAD_DIM), 0)
+    own = segment_of(base + 4 * row, lengths, limit)
+    for k in range(KERNEL):
+        there = segment_of(base + 4 * (row + k - KERNEL // 2), lengths, limit)
+        masks[k] = (there == own).astype(jnp.float32)
     for at, (start, size) in enumerate(blocks):
         span = size + 2 * WINDOW
         q_row = lax.broadcasted_iota(jnp.int32, (size, 1), 0)
@@ -395,21 +425,18 @@
             (values.shape[0], HEAD_DIM), jnp.bfloat16
         )
 
-    pltpu.make_async_copy(weights, weights, sem).wait()
+    early_copy.wait()
 
     @pl.loop(0, WIDTH // COLS)
     def _(n):
-        here = pl.ds(pl.multiple_of(n * COLS, COLS), COLS)
-        queries[:, here] = jnp.dot(
-            normed_ref[WINDOW : WINDOW + rows_mid, :],
-            columns(weights, 0, 3, n),
-            preferred_element_type=jnp.float32,
+        queries[:, here(n)] = jnp.dot(
+            normed_ref[mid, :], columns(early_w, 0, 3, n), preferred_element_type=jnp.float32
         ).astype(jnp.bfloat16)
-        keys[:, here] = jnp.dot(
-            normed_ref[...], columns(weights, 1, 3, n), preferred_element_type=jnp.float32
+        keys[:, here(n)] = jnp.dot(
+            normed_ref[...], columns(early_w, 1, 3, n), preferred_element_type=jnp.float32
         ).astype(jnp.bfloat16)
         made = jnp.dot(
-            normed_ref[...], columns(weights, 2, 3, n), preferred_element_type=jnp.float32
+            normed_ref[...], columns(early_w, 2, 3, n), preferred_element_type=jnp.float32
         ).astype(jnp.bfloat16)
         for k in range(COLS // HEAD_DIM):
             lanes = pl.ds(pl.multiple_of(2 * n * COLS + 2 * k * HEAD_DIM, HEAD_DIM), HEAD_DIM)
@@ -436,71 +463,16 @@
                 values[start : start + span, wide],
                 preferred_element_type=jnp.float32,
             )
-            context_ref[start : start + size, lanes] = (
+            context[start : start + size, lanes] = (
                 mixed[:, :HEAD_DIM] / mixed[:, HEAD_DIM:]
             ).astype(jnp.bfloat16)
 
-
-def attend(info, normed, sources, places, limit):
-    rows_all = normed.shape[0]
-    tokens = rows_all - 2 * HALO
-    rows_mid = tokens + 2 * EDGE
-    whole = pl.BlockSpec(memory_space=pltpu.VMEM)
-    flops = 2 * WIDTH * (rows_all * 2 * WIDTH + rows_mid * WIDTH + 3 * rows_mid * 400)
-    return pl.pallas_call(
-        functools.partial(attention_kernel, tokens, limit, places),
-        out_shape=jax.ShapeDtypeStruct((rows_mid, WIDTH), jnp.bfloat16),
-        in_specs=[pl.BlockSpec(memory_space=pltpu.SMEM), whole]
-        + [pl.BlockSpec(memory_space=pl.ANY)] * len(sources),
-        out_specs=whole,
-        scratch_shapes=[
-            pltpu.VMEM((32, 3 * WIDTH // 32, WIDTH), jnp.bfloat16),
-            pltpu.VMEM((rows_all, WIDTH), jnp.bfloat16),
-            pltpu.VMEM((rows_all, 2 * WIDTH), jnp.bfloat16),
-            pltpu.VMEM((rows_mid, WIDTH), jnp.bfloat16),
-            pltpu.VMEM((4, 128 + EDGE, 512), jnp.float32),
-            pltpu.SemaphoreType.DMA(()),
-        ],
-        compiler_params=pltpu.CompilerParams(vmem_limit_bytes=26 * 1024 * 1024),
-        cost_estimate=pl.CostEstimate(
-            flops=flops, bytes_accessed=10 * 1024 * 1024, transcendentals=2 * 1024 * 1024
-        ),
-        name="attend",
-    )(info, normed, *sources)
-
-
-def final_kernel(
-    tokens,
-    limit,
-    places,
-    info_ref,
-    hidden_ref,
-    context_ref,
-    gain_conv_ref,
-    depth_ref,
-    gain_out_ref,
-    *rest,
-):
-    sources = rest[:-8]
-    out_ref, weights, attended, normed, gated, acted, masks, sem = rest[-8:]
-    rows_mid = tokens + 2 * EDGE
-    copies_in(info_ref, sources, places, weights, sem)
-    base = info_ref[0]
-    lengths = [info_ref[1 + k] for k in range(4)]
-
-    row = lax.broadcasted_iota(jnp.int32, (tokens, HEAD_DIM), 0)
-    own = segment_of(base + 4 * row, lengths, limit)
-    for k in range(KERNEL):
-        there = segment_of(base + 4 * (row + k - KERNEL // 2), lengths, limit)
-        masks[k] = (there == own).astype(jnp.float32)
-
-    pltpu.make_async_copy(weights, weights, sem).wait()
+    late_copy.wait()
 
     @pl.loop(0, WIDTH // COLS)
     def _(n):
-        here = pl.ds(pl.multiple_of(n * COLS, COLS), COLS)
-        attended[:, here] = hidden_ref[:, here] + jnp.dot(
-            context_ref[...], columns(weights, 0, 4, n), preferred_element_type=jnp.float32
+        attended[:, here(n)] = hidden_ref[:, here(n)] + jnp.dot(
+            context[...], columns(late_w, 0, 4, n), preferred_element_type=jnp.float32
         )
 
     gain_c = gain_conv_ref[...]
@@ -509,12 +481,13 @@
     @pl.loop(0, 2)
     def _(r):
         rows = pl.ds(pl.multiple_of(r * step_rows, 16), step_rows)
-        normed[rows, :] = layer_norm(attended[rows, :], gain_c).astype(jnp.bfloat16)
+        queries[rows, :] = layer_norm(attended[rows, :], gain_c).astype(jnp.bfloat16)
+
 
     @pl.loop(0, WIDTH // COLS)
     def _(n):
-        value = jnp.dot(normed[...], columns(weights, 1, 4, n), preferred_element_type=jnp.float32)
-        gate = jnp.dot(normed[...], columns(weights, 2, 4, n), preferred_element_type=jnp.float32)
+        value = jnp.dot(queries[...], columns(late_w, 1, 4, n), preferred_element_type=jnp.float32)
+        gate = jnp.dot(queries[...], columns(late_w, 2, 4, n), preferred_element_type=jnp.float32)
         made = (value * jax.nn.sigmoid(gate)).astype(jnp.bfloat16).astype(jnp.float32)
         for j in range(COLS // HEAD_DIM):
             gated[...] = made[:, j * HEAD_DIM : (j + 1) * HEAD_DIM]
@@ -524,13 +497,12 @@
                 begin = EDGE - KERNEL // 2 + k
                 tap = gated[begin : begin + tokens, :] * depth_ref[k : k + 1, lanes]
                 total = total + (tap if k == KERNEL // 2 else tap * masks[k])
-            acted[:, lanes] = (total * jax.nn.sigmoid(total)).astype(jnp.bfloat16)
+            context[0:tokens, lanes] = (total * jax.nn.sigmoid(total)).astype(jnp.bfloat16)
 
     @pl.loop(0, WIDTH // COLS)
     def _(n):
-        here = pl.ds(pl.multiple_of(n * COLS, COLS), COLS)
-        attended[EDGE : EDGE + tokens, here] += jnp.dot(
-            acted[...], columns(weights, 3, 4, n), preferred_element_type=jnp.float32
+        attended[EDGE : EDGE + tokens, here(n)] += jnp.dot(
+            context[0:tokens, :], columns(late_w, 3, 4, n), preferred_element_type=jnp.float32
         )
 
     gain_o = gain_out_ref[...]
@@ -542,34 +514,38 @@
         out_ref[rows, :] = layer_norm(taken, gain_o).astype(jnp.bfloat16)
 
 
-def finish(info, hidden, context, sources, places, gain_conv, w_depth, gain_out, limit):
+def conformer_block(info, hidden, normed, late, gain_conv, w_depth, gain_out, limit):
+    rows_all = normed.shape[0]
     rows_mid = hidden.shape[0]
     tokens = rows_mid - 2 * EDGE
     whole = pl.BlockSpec(memory_space=pltpu.VMEM)
+    flops = 2 * rows_all * WIDTH * 2 * WIDTH + 2 * rows_mid * WIDTH * WIDTH * 5
     return pl.pallas_call(
-        functools.partial(final_kernel, tokens, limit, places),
+        functools.partial(block_kernel, tokens, limit),
         out_shape=jax.ShapeDtypeStruct((tokens, WIDTH), jnp.bfloat16),
         in_specs=[pl.BlockSpec(memory_space=pltpu.SMEM)]
         + [whole] * 5
-        + [pl.BlockSpec(memory_space=pl.ANY)] * len(sources),
+        + [pl.BlockSpec(memory_space=pl.ANY)],
         out_specs=whole,
         scratch_shapes=[
+            pltpu.VMEM((32, 3 * WIDTH // 32, WIDTH), jnp.bfloat16),
             pltpu.VMEM((32, 4 * WIDTH // 32, WIDTH), jnp.bfloat16),
+            pltpu.VMEM((rows_all, WIDTH), jnp.bfloat16),
+            pltpu.VMEM((rows_all, 2 * WIDTH), jnp.bfloat16),
+            pltpu.VMEM((rows_mid, WIDTH), jnp.bfloat16),
+            pltpu.VMEM((rows_mid, WIDTH), jnp.bfloat16),
             pltpu.VMEM((rows_mid, WIDTH), jnp.float32),
-            pltpu.VMEM((rows_mid, WIDTH), jnp.bfloat16),
             pltpu.VMEM((rows_mid, HEAD_DIM), jnp.float32),
-            pltpu.VMEM((tokens, WIDTH), jnp.bfloat16),
             pltpu.VMEM((KERNEL, tokens, HEAD_DIM), jnp.float32),
-            pltpu.SemaphoreType.DMA(()),
+            pltpu.VMEM((4, 128 + EDGE, 512), jnp.float32),
+            pltpu.SemaphoreType.DMA((2,)),
         ],
-        compiler_params=pltpu.CompilerParams(vmem_limit_bytes=30 * 1024 * 1024),
+        compiler_params=pltpu.CompilerParams(vmem_limit_bytes=44 * 1024 * 1024),
         cost_estimate=pl.CostEstimate(
-            flops=8 * rows_mid * WIDTH * WIDTH,
-            bytes_accessed=14 * 1024 * 1024,
-            transcendentals=2 * 1024 * 1024,
+            flops=flops, bytes_accessed=24 * 1024 * 1024, transcendentals=4 * 1024 * 1024
         ),
-        name="finish",
-    )(info, hidden, context, gain_conv, w_depth, gain_out, *sources)
+        name="conformer_block",
+    )(info, hidden, normed, gain_conv, w_depth, gain_out, late)
 
 
 def on_device(
@@ -599,33 +575,34 @@
         ]
     ).astype(jnp.int32)
 
-    w_second_all = gather_ordered(w_second)
-    rest = [w_qkv], [w_out, w_point_in, w_point_out]
-    relayed = lax.axis_size("rec") == 4 and lax.axis_size("tm") == 8
-    if relayed:
-        gathered = [gather_relayed(w_proj, False, [])]
-        for arrays in rest:
-            gathered.append(gather_relayed(pack(arrays), True, gathered[-1][2]))
-    else:
-        full = lax.all_gather(w_proj, ("rec", "tm"), axis=0, tiled=True)
-        gathered = [([full], None)]
-        for arrays in rest:
-            packed = pack(arrays)
-            parts = packed.shape[0] // w_out.shape[0]
-            full = lax.all_gather(packed, ("rec", "tm"), axis=0, tiled=False)
-            full = full.reshape(full.shape[0], parts, -1, WIDTH).transpose(1, 0, 2, 3)
-            full = full.reshape(parts, 32, -1, WIDTH).transpose(1, 0, 2, 3)
-            gathered.append(([full.reshape(32, -1, WIDTH)], None))
-
+    def gather_packed(arrays):
+        packed = pack(arrays)
+        full = lax.all_gather(packed, ("rec", "tm"), axis=0, tiled=False)
+        if full.shape[0] == 32:
+            return full
+        parts = packed.shape[0] // w_out.shape[0]
+        full = full.reshape(full.shape[0], parts, -1, WIDTH).transpose(1, 0, 2, 3)
+        full = full.reshape(parts, 32, -1, WIDTH).transpose(1, 0, 2, 3)
+        return full.reshape(32, -1, WIDTH)
+
+    late = gather_packed([w_qkv, w_out, w_point_in, w_point_out])
+    w_second_all, rounds = gather_ordered(w_second)
     patches, taps = prepare(info, mel_frames[0], w_first, tokens, limit)
     subs = subsample(patches, taps, w_second_all)
-    hidden, normed = project(info, gain_attn[None], subs, *gathered[0][:2], tokens)
-    context = attend(info, normed, *gathered[1][:2], limit)
-    encoded = finish(
+    if lax.axis_size("rec") == 4 and lax.axis_size("tm") == 8:
+        proj = along_rec(behind(w_proj, *rounds[0]))
+        proj = behind(tuple(proj), patches, *rounds[1], *subs[:2])
+        proj = to_neighbours(jnp.concatenate(proj, axis=0))
+        proj_late = relayed(*behind(proj, *subs))
+        proj, places = to_other_core(*proj, *proj_late)
+    else:
+        proj, places = [lax.all_gather(w_proj, ("rec", "tm"), axis=0, tiled=True)], None
+    hidden, normed = project(info, gain_attn[None], subs, proj, places, tokens)
+    encoded = conformer_block(
         info,
         hidden,
-        context,
-        *gathered[2][:2],
+        normed,
+        late,
         gain_conv[None],
         w_depth,
         gain_out[None],

time: 254 us -> 206 us (0.81)
  blocking collectives: 20.4 us -> 0 us
  local copies, waits for them, and re-layouts: 30.2 us -> 12 us
  waiting for transfers between devices: 43.3 us -> 60.7 us
  starting transfers between devices: 48 us -> 31.4 us
  Pallas kernels: 92.6 us -> 85.8 us
    all_gather x1 -> x0, blocking collectives: 20.4 us -> none  [gather_relayed(): held = lax.all_gather(block, 'rec', axis=0, tiled=True)]
    ppermute x37 -> x19, starting transfers between devices: 37.7 us -> 25.1 us  [exchange(): return lax.ppermute(block, axis, [(i, i ^ distance) for i in range(size)])]
    all_gather x1, waiting for transfers between devices: 0.01 us -> 10 us  [gather_packed(): full = lax.all_gather(packed, ('rec', 'tm'), axis=0, tiled=False)]
    unnamed x81 -> x31, local copies, waits for them, and re-layouts: 16.5 us -> 8.5 us
    pallas_call x2 -> x1, Pallas kernels: 36.5 us -> 29.7 us  [conformer_block(): pl.pallas_call(functools.partial(block_kernel, tokens, limit), out_shape=...]
    ppermute x37 -> x19, waiting for transfers between devices: 42.3 us -> 48.1 us  [exchange(): return lax.ppermute(block, axis, [(i, i ^ distance) for i in range(size)])]
    slice x6 -> x2, local copies, waits for them, and re-layouts: 3.89 us -> 0.09 us  [relayed(): return (exchange(beside[:half], 'tm', 4), exchange(above[half:], 'tm', 2))]
    ppermute x1, starting transfers between devices: 8.18 us -> 4.38 us  [prepare(): low = lax.ppermute(mel[mel.shape[0] - reach:], 'tm', forward)]
  transfers between devices with their start and end apart: 40 -> 22, of which waited for: 9 -> 9; matrix products, arithmetic and copies ran while one was open for 8% -> 4% of each run, Pallas kernels for 31% -> 27%
where the time goes in v3:
time: 206 us; the launch traced here: 205 us
  Pallas kernels  85.8 us (42%)
  waiting for transfers between devices  60.7 us (29%)
  starting transfers between devices  31.4 us (15%)
  between operations  13.7 us (7%)
  local copies, waits for them, and re-layouts  12 us (6%)
    ppermute x19, waiting for transfers between devices, exchange(): return lax.ppermute(block, axis, [(i, i ^ distance) for i in range(size)])  48.1 us
    pallas_call x5, Pallas kernels, subsample(): pl.pallas_call(functools.partial(conv_kernel, begin, count), out_shape=ja...  35.4 us
    pallas_call x1, Pallas kernels, conformer_block(): pl.pallas_call(functools.partial(block_kernel, tokens, limit), out_shape=...  29.7 us
    ppermute x19, starting transfers between devices, exchange(): return lax.ppermute(block, axis, [(i, i ^ distance) for i in range(size)])  25.1 us
    pallas_call x1, Pallas kernels, project(): pl.pallas_call(functools.partial(project_kernel, places), out_shape=(jax....  16 us
    all_gather x1, waiting for transfers between devices, gather_packed(): full = lax.all_gather(packed, ('rec', 'tm'), axis=0, tiled=False)  10 us
    unnamed x31, local copies, waits for them, and re-layouts  8.5 us
    ppermute x1, starting transfers between devices, prepare(): low = lax.ppermute(mel[mel.shape[0] - reach:], 'tm', forward)  4.38 us
  transfers between devices with their start and end apart: 22, of which 9 were waited for; matrix products, arithmetic and copies ran while one was open for 4% of the time, Pallas kernels for 27%

profile of v3, /device:TPU:1, one launch (start us, length us, event | category | flops | bytes accessed | tf_op | source)
XLA Modules:
  0.0 205.3 jit_solution(11019178229310626670)
XLA Ops:
  6.5 0.9 copy-done
  7.5 0.9 copy-done.1
  8.4 0.8 copy-done.2
  9.2 0.8 copy-done.3
  10.1 0.8 pack.1
  10.9 0.0 all-gather.3.cloned.1.call-update
  10.9 4.2 %collective-permute-start.2 = (bf16[1,72,256]{2,1,0:T(8,128)(2,1)S(1)}, bf16[1,72,256]{2,1,0:T(8,128)(2,1)S(1)}, u32[]{:S(2)}, u32[]{:S(2)}) collective-permute-start(bf16[1,72,256]{2,1,0:T(8,128)(2,1)S(1)} %bitcast.33), channel_id=1, source_target_pairs={{0,24},{8,16},{16,8},{24,0},{1,25},{9,17},{17,9},{25,1},{2,26},{10... | collective-permute-start | bytes 110600 | tf_op jit(solution)/shard_map/ppermute | solution.py:42
  15.1 0.4 collective-permute-start.4
  15.5 4.4 %collective-permute-start = (bf16[640,80]{0,1:T(8,128)(2,1)S(1)}, bf16[640,80]{0,1:T(8,128)(2,1)S(1)}, u32[]{:S(2)}, u32[]{:S(2)}) collective-permute-start(bf16[640,80]{0,1:T(8,128)(2,1)S(1)} %get-tuple-element.34), channel_id=1, source_target_pairs={{0,1},{1,2},{2,3},{3,4},{4,5},{5,6},{6,7},{8,9},{9,10},{10,11},{11... | collective-permute-start | bytes 307208 | tf_op jit(solution)/shard_map/ppermute | solution.py:181
  19.9 1.9 collective-permute-start.1
  21.9 0.1 concatenate.21.info_ref
  22.0 1.1 collective-permute-start.5
  23.2 1.3 collective-permute-start.6
  24.5 0.3 collective-permute-start.7
  24.8 1.9 collective-permute-start.10
  26.6 2.6 %collective-permute-done.1 = bf16[640,80]{0,1:T(8,128)(2,1)S(1)} collective-permute-done((bf16[640,80]{0,1:T(8,128)(2,1)S(1)}, bf16[640,80]{0,1:T(8,128)(2,1)S(1)}, u32[]{:S(2)}, u32[]{:S(2)}) %collective-permute-start.1) | collective-permute-done | bytes 102432 | tf_op jit(solution)/shard_map/ppermute | solution.py:182
  29.2 3.0 %collective-permute-start.11 = (bf16[160,1024]{1,0:T(8,128)(2,1)}, bf16[160,1024]{1,0:T(8,128)(2,1)}, u32[]{:S(2)}, u32[]{:S(2)}) collective-permute-start(bf16[160,1024]{1,0:T(8,128)(2,1)} %param.18), channel_id=1, source_target_pairs={{0,24},{8,16},{16,8},{24,0},{1,25},{9,17},{17,9},{25,1},{2,26},{10... | collective-permute-start | bytes 983048 | tf_op jit(solution)/shard_map/ppermute | solution.py:42
  32.3 0.5 collective-permute-start.9
  32.7 0.6 collective-permute-done.6
  33.3 1.2 collective-permute-done.7
  34.6 0.1 broadcast_select_fusion.9
  34.7 0.9 pad_maximum_fusion.2
  35.6 1.6 collective-permute-start.8
  37.1 0.3 fusion
  37.5 0.4 copy.18
  37.9 0.5 slice.35
  38.4 0.4 copy.19
  38.9 0.5 slice.37
  39.4 0.0 copy-start.8
  39.4 0.3 pad_maximum_fusion.1.quads_ref
  39.7 0.3 copy-done.8
  40.1 3.9 %prepare.1 = (bf16[3,2,800,256]{3,2,1,0:T(8,128)(2,1)S(1)}, bf16[256,5120]{1,0:T(8,128)(2,1)S(1)}) custom-call(s32[8]{0:T(128)S(1)} %concatenate.21.info_ref, bf16[800,640]{1,0:T(8,128)(2,1)S(1)} %pad_maximum_fusion.1.quads_ref, s32[8,256]{1,0:T(8,128)S(1)} %copy-done.8, f32[9,256]{1,0:T(8,128)S(1)} %reshape.15.w_ref), custom_call_target="tpu_custom_call" | custom-call | flops 1887436800 | bytes 6291456 | tf_op jit(solution)/shard_map/prepare/pallas_call | solution.py:199
  44.0 0.1 broadcast_select_fusion.1
  44.1 0.1 pad_maximum_fusion
  44.3 0.1 copy.20
  44.4 7.3 %subsample.6.rest_1_ = bf16[800,1024]{1,0:T(8,128)(2,1)S(1)} custom-call(bf16[3,2,800,256]{3,2,1,0:T(8,128)(2,1)S(1)} %get-tuple-element.16.a_ref, bf16[256,5120]{1,0:T(8,128)(2,1)S(1)} %get-tuple-element.17.b_ref, bf16[3,768,256]{2,1,0:T(8,128)(2,1)S(1)} %bitcast.23), custom_call_target="tpu_custom_call" | custom-call | flops 6606028800 | bytes 8388608 | tf_op jit(solution)/shard_map/subsample/pallas_call | solution.py:257
  51.6 6.7 %subsample.5.rest_0_ = bf16[800,1024]{1,0:T(8,128)(2,1)S(1)} custom-call(bf16[3,2,800,256]{3,2,1,0:T(8,128)(2,1)S(1)} %get-tuple-element.16.a_ref, bf16[256,5120]{1,0:T(8,128)(2,1)S(1)} %get-tuple-element.17.b_ref, bf16[3,768,256]{2,1,0:T(8,128)(2,1)S(1)} %bitcast.24), custom_call_target="tpu_custom_call" | custom-call | flops 6606028800 | bytes 8388608 | tf_op jit(solution)/shard_map/subsample/pallas_call | solution.py:257
  58.4 0.1 collective-permute-done.9
  58.5 1.0 constant_dynamic-update-slice_fusion.3
  59.5 1.0 constant_dynamic-update-slice_fusion.2
  60.5 1.0 constant_dynamic-update-slice_fusion.1
  61.5 1.0 constant_dynamic-update-slice_fusion.rest_5_
  62.5 3.7 %collective-permute-start.12 = (bf16[640,1024]{1,0:T(8,128)(2,1)S(1)}, bf16[640,1024]{1,0:T(8,128)(2,1)S(1)}, u32[]{:S(2)}, u32[]{:S(2)}) collective-permute-start(bf16[640,1024]{1,0:T(8,128)(2,1)S(1)} %constant_dynamic-update-slice_fusion.rest_5_), channel_id=1, source_target_pairs={{0,2},{1,3},{2,0},{3,1},{4,6},{5,7},{6,4},{7,5},{8,10},{9,11},{10,... | collective-permute-start | bytes 3932168 | tf_op jit(solution)/shard_map/ppermute | solution.py:42
  66.1 7.1 %subsample.9.rest_4_ = bf16[800,1024]{1,0:T(8,128)(2,1)S(1)} custom-call(bf16[3,2,800,256]{3,2,1,0:T(8,128)(2,1)S(1)} %get-tuple-element.16.a_ref, bf16[256,5120]{1,0:T(8,128)(2,1)S(1)} %get-tuple-element.17.b_ref, bf16[3,768,256]{2,1,0:T(8,128)(2,1)S(1)} %bitcast.25), custom_call_target="tpu_custom_call" | custom-call | flops 6606028800 | bytes 8388608 | tf_op jit(solution)/shard_map/subsample/pallas_call | solution.py:257
  73.2 1.2 collective-permute-start.16
  74.4 7.1 %subsample.8.rest_3_ = bf16[800,1024]{1,0:T(8,128)(2,1)S(1)} custom-call(bf16[3,2,800,256]{3,2,1,0:T(8,128)(2,1)S(1)} %get-tuple-element.16.a_ref, bf16[256,5120]{1,0:T(8,128)(2,1)S(1)} %get-tuple-element.17.b_ref, bf16[3,768,256]{2,1,0:T(8,128)(2,1)S(1)} %bitcast.26), custom_call_target="tpu_custom_call" | custom-call | flops 6606028800 | bytes 8388608 | tf_op jit(solution)/shard_map/subsample/pallas_call | solution.py:257
  81.5 7.3 %subsample.7.rest_2_ = bf16[800,1024]{1,0:T(8,128)(2,1)S(1)} custom-call(bf16[3,2,800,256]{3,2,1,0:T(8,128)(2,1)S(1)} %get-tuple-element.16.a_ref, bf16[256,5120]{1,0:T(8,128)(2,1)S(1)} %get-tuple-element.17.b_ref, bf16[3,768,256]{2,1,0:T(8,128)(2,1)S(1)} %bitcast.27), custom_call_target="tpu_custom_call" | custom-call | flops 6606028800 | bytes 8388608 | tf_op jit(solution)/shard_map/subsample/pallas_call | solution.py:257
  88.8 0.0 copy-start.5
  88.8 17.1 %collective-permute-done.12.rest_6_ = bf16[640,1024]{1,0:T(8,128)(2,1)S(1)} collective-permute-done((bf16[640,1024]{1,0:T(8,128)(2,1)S(1)}, bf16[640,1024]{1,0:T(8,128)(2,1)S(1)}, u32[]{:S(2)}, u32[]{:S(2)}) %collective-permute-start.12) | collective-permute-done | bytes 1310752 | tf_op jit(solution)/shard_map/ppermute | solution.py:42
  105.9 1.1 collective-permute-start.14
  107.1 0.3 collective-permute-start.15
  107.4 1.5 collective-permute-start.17
  108.9 27.3 %collective-permute-done.14.rest_8_ = bf16[320,1024]{1,0:T(8,128)(2,1)S(1)} collective-permute-done((bf16[320,1024]{1,0:T(8,128)(2,1)S(1)}, bf16[320,1024]{1,0:T(8,128)(2,1)S(1)}, u32[]{:S(2)}, u32[]{:S(2)}) %collective-permute-start.14) | collective-permute-done | bytes 655392 | tf_op jit(solution)/shard_map/ppermute | solution.py:42
  136.2 1.7 collective-permute-start.19
  137.9 1.5 collective-permute-start.20
  139.4 0.2 collective-permute-done.19.rest_13_
  139.6 1.5 collective-permute-done.20.rest_14_
  141.1 0.0 copy-start.4
  141.1 0.0 copy-start.6
  141.1 0.0 copy-start.7
  141.1 16.0 %project.1 = (f32[544,1024]{1,0:T(8,128)}, bf16[800,1024]{1,0:T(8,128)(2,1)S(1)}) custom-call(s32[8]{0:T(128)S(1)} %concatenate.21.info_ref, f32[1,1024]{1,0:T(1,128)S(1)} %bitcast.28, bf16[800,1024]{1,0:T(8,128)(2,1)S(1)} %subsample.5.rest_0_, bf16[800,1024]{1,0:T(8,128)(2,1)S(1)} %subsample.6.rest_1_, bf16[800,1024]{1,0:T(8,128)(2,1)S(1)} %subsample.7.rest_2_, ...), custom_call_target="tpu_custom_call" | custom-call | flops 8388608000 | bytes 25165824 | tf_op jit(solution)/shard_map/project/pallas_call | solution.py:313
  157.2 10.0 %all-gather.3.cloned.1.call-done = bf16[7168,1024]{1,0:T(8,128)(2,1)} async-done(((bf16[224,1024]{1,0:T(8,128)(2,1)}), bf16[7168,1024]{1,0:T(8,128)(2,1)}) %all-gather.3.cloned.1.call-update) | async-done | bytes 14680080 | tf_op jit(solution)/shard_map/all_gather | solution.py:580
  167.2 1.6 copy-done.9
  168.8 29.7 %conformer_block.1 = bf16[512,1024]{1,0:T(8,128)(2,1)} custom-call(s32[8]{0:T(128)S(1)} %concatenate.21.info_ref, f32[544,1024]{1,0:T(8,128)S(1)} %copy-done.9, bf16[800,1024]{1,0:T(8,128)(2,1)S(1)} %get-tuple-element.26.normed_ref, f32[1,1024]{1,0:T(1,128)S(1)} %bitcast.29, f32[9,1024]{1,0:T(8,128)S(1)} %copy-done.4, f32[1,1024]{1,0:T(1,128)S(1)} %bitcast.30, ...), custom_call_target="tpu_custom_call" | custom-call | flops 9059696640 | bytes 25165824 | tf_op jit(solution)/shard_map/conformer_block/pallas_call | solution.py:523
  (42 shorter events, 0.3 us)
Async XLA Ops:
  6.5 160.6 %all-gather.3.cloned.1.call-start = ((), (), s32[]{:S(2)}) async-start(), calls=%async_computation | async-start | bytes 15138816 | tf_op jit(solution)/shard_map/all_gather | solution.py:580
  6.5 0.9 copy-start
  7.5 0.9 copy-start.1
  8.4 0.8 copy-start.2
  9.2 0.8 copy-start.3
  10.0 0.8 copy-start.11
  10.1 5.4 %copy-start.10 = (bf16[1,2048,80]{1,2,0:T(8,128)(2,1)S(1)}, bf16[1,2048,80]{1,2,0:T(8,128)(2,1)}, u32[]{:S(2)}) copy-start(bf16[1,2048,80]{1,2,0:T(8,128)(2,1)} %param.14) | copy-start | bytes 983044
  10.1 11.8 %copy-start.12 = (f32[3,3,256]{2,1,0:T(4,128)S(1)}, f32[3,3,256]{2,1,0:T(4,128)}, u32[]{:S(2)}) copy-start(f32[3,3,256]{2,1,0:T(4,128)} %param.16) | copy-start | bytes 27652
  10.1 11.8 %copy-start.13 = (s32[1,4]{1,0:T(1,128)S(1)}, s32[1,4]{1,0:T(1,128)}, u32[]{:S(2)}) copy-start(s32[1,4]{1,0:T(1,128)} %param.15) | copy-start | bytes 52
  10.9 11.1 %collective-permute-start.2 = (bf16[1,72,256]{2,1,0:T(8,128)(2,1)S(1)}, bf16[1,72,256]{2,1,0:T(8,128)(2,1)S(1)}, u32[]{:S(2)}, u32[]{:S(2)}) collective-permute-start(bf16[1,72,256]{2,1,0:T(8,128)(2,1)S(1)} %bitcast.33), channel_id=1, source_target_pairs={{0,24},{8,16},{16,8},{24,0},{1,25},{9,17},{17,9},{25,1},{2,26},{10... | collective-permute-start | bytes 110600 | tf_op jit(solution)/shard_map/ppermute | solution.py:42
  15.1 6.8 %collective-permute-start.3 = (bf16[1,72,256]{2,1,0:T(8,128)(2,1)S(1)}, bf16[1,72,256]{2,1,0:T(8,128)(2,1)S(1)}, u32[]{:S(2)}, u32[]{:S(2)}) collective-permute-start(bf16[1,72,256]{2,1,0:T(8,128)(2,1)S(1)} %bitcast.34), channel_id=1, source_target_pairs={{0,16},{8,24},{16,0},{24,8},{1,17},{9,25},{17,1},{25,9},{2,18},{10... | collective-permute-start | bytes 110600 | tf_op jit(solution)/shard_map/ppermute | solution.py:42
  15.1 6.8 %collective-permute-start.4 = (bf16[1,72,256]{2,1,0:T(8,128)(2,1)S(1)}, bf16[1,72,256]{2,1,0:T(8,128)(2,1)S(1)}, u32[]{:S(2)}, u32[]{:S(2)}) collective-permute-start(bf16[1,72,256]{2,1,0:T(8,128)(2,1)S(1)} %bitcast.35), channel_id=1, source_target_pairs={{0,8},{8,0},{16,24},{24,16},{1,9},{9,1},{17,25},{25,17},{2,10},{10... | collective-permute-start | bytes 110600 | tf_op jit(solution)/shard_map/ppermute | solution.py:42
  15.5 9.3 %collective-permute-start = (bf16[640,80]{0,1:T(8,128)(2,1)S(1)}, bf16[640,80]{0,1:T(8,128)(2,1)S(1)}, u32[]{:S(2)}, u32[]{:S(2)}) collective-permute-start(bf16[640,80]{0,1:T(8,128)(2,1)S(1)} %get-tuple-element.34), channel_id=1, source_target_pairs={{0,1},{1,2},{2,3},{3,4},{4,5},{5,6},{6,7},{8,9},{9,10},{10,11},{11... | collective-permute-start | bytes 307208 | tf_op jit(solution)/shard_map/ppermute | solution.py:181
  19.9 9.3 %collective-permute-start.1 = (bf16[640,80]{0,1:T(8,128)(2,1)S(1)}, bf16[640,80]{0,1:T(8,128)(2,1)S(1)}, u32[]{:S(2)}, u32[]{:S(2)}) collective-permute-start(bf16[640,80]{0,1:T(8,128)(2,1)S(1)} %get-tuple-element.35), channel_id=1, source_target_pairs={{1,0},{2,1},{3,2},{4,3},{5,4},{6,5},{7,6},{9,8},{10,9},{11,10},{12... | collective-permute-start | bytes 307208 | tf_op jit(solution)/shard_map/ppermute | solution.py:182
  22.0 10.2 %collective-permute-start.5 = (bf16[4,72,256]{2,1,0:T(8,128)(2,1)S(1)}, bf16[4,72,256]{2,1,0:T(8,128)(2,1)S(1)}, u32[]{:S(2)}, u32[]{:S(2)}) collective-permute-start(bf16[4,72,256]{2,1,0:T(8,128)(2,1)S(1)} %pad_maximum_fusion.4), channel_id=1, source_target_pairs={{0,6},{1,7},{2,4},{3,5},{4,2},{5,3},{6,0},{7,1},{8,14},{9,15},{10,... | collective-permute-start | bytes 442376 | tf_op jit(solution)/shard_map/ppermute | solution.py:42
  23.2 10.1 %collective-permute-start.6 = (bf16[4,72,256]{2,1,0:T(8,128)(2,1)S(1)}, bf16[4,72,256]{2,1,0:T(8,128)(2,1)S(1)}, u32[]{:S(2)}, u32[]{:S(2)}) collective-permute-start(bf16[4,72,256]{2,1,0:T(8,128)(2,1)S(1)} %pad_maximum_fusion.4), channel_id=1, source_target_pairs={{0,4},{1,5},{2,6},{3,7},{4,0},{5,1},{6,2},{7,3},{8,12},{9,13},{10,... | collective-permute-start | bytes 442376 | tf_op jit(solution)/shard_map/ppermute | solution.py:42
  24.5 10.0 %collective-permute-start.7 = (bf16[4,72,256]{2,1,0:T(8,128)(2,1)S(1)}, bf16[4,72,256]{2,1,0:T(8,128)(2,1)S(1)}, u32[]{:S(2)}, u32[]{:S(2)}) collective-permute-start(bf16[4,72,256]{2,1,0:T(8,128)(2,1)S(1)} %pad_maximum_fusion.4), channel_id=1, source_target_pairs={{0,2},{1,3},{2,0},{3,1},{4,6},{5,7},{6,4},{7,5},{8,10},{9,11},{10,... | collective-permute-start | bytes 442376 | tf_op jit(solution)/shard_map/ppermute | solution.py:42
  24.8 33.6 %collective-permute-start.10 = (bf16[160,1024]{1,0:T(8,128)(2,1)}, bf16[160,1024]{1,0:T(8,128)(2,1)}, u32[]{:S(2)}, u32[]{:S(2)}) collective-permute-start(bf16[160,1024]{1,0:T(8,128)(2,1)} %param.18), channel_id=1, source_target_pairs={{0,16},{8,24},{16,0},{24,8},{1,17},{9,25},{17,1},{25,9},{2,18},{10... | collective-permute-start | bytes 983048 | tf_op jit(solution)/shard_map/ppermute | solution.py:42
  29.2 29.1 %collective-permute-start.11 = (bf16[160,1024]{1,0:T(8,128)(2,1)}, bf16[160,1024]{1,0:T(8,128)(2,1)}, u32[]{:S(2)}, u32[]{:S(2)}) collective-permute-start(bf16[160,1024]{1,0:T(8,128)(2,1)} %param.18), channel_id=1, source_target_pairs={{0,24},{8,16},{16,8},{24,0},{1,25},{9,17},{17,9},{25,1},{2,26},{10... | collective-permute-start | bytes 983048 | tf_op jit(solution)/shard_map/ppermute | solution.py:42
  32.3 26.2 %collective-permute-start.9 = (bf16[160,1024]{1,0:T(8,128)(2,1)}, bf16[160,1024]{1,0:T(8,128)(2,1)}, u32[]{:S(2)}, u32[]{:S(2)}) collective-permute-start(bf16[160,1024]{1,0:T(8,128)(2,1)} %param.18), channel_id=1, source_target_pairs={{0,8},{8,0},{16,24},{24,16},{1,9},{9,1},{17,25},{25,17},{2,10},{10... | collective-permute-start | bytes 983048 | tf_op jit(solution)/shard_map/ppermute | solution.py:42
  35.6 8.5 %collective-permute-start.8 = (bf16[16,72,256]{2,1,0:T(8,128)(2,1)}, bf16[16,72,256]{2,1,0:T(8,128)(2,1)S(1)}, u32[]{:S(2)}, u32[]{:S(2)}) collective-permute-start(bf16[16,72,256]{2,1,0:T(8,128)(2,1)} %pad_maximum_fusion.2), channel_id=1, source_target_pairs={{0,1},{1,0},{2,3},{3,2},{4,5},{5,4},{6,7},{7,6},{8,9},{9,8},{10,11... | collective-permute-start | bytes 1769480 | tf_op jit(solution)/shard_map/ppermute | solution.py:42
  39.4 0.7 copy-start.8
  62.5 43.4 %collective-permute-start.12 = (bf16[640,1024]{1,0:T(8,128)(2,1)S(1)}, bf16[640,1024]{1,0:T(8,128)(2,1)S(1)}, u32[]{:S(2)}, u32[]{:S(2)}) collective-permute-start(bf16[640,1024]{1,0:T(8,128)(2,1)S(1)} %constant_dynamic-update-slice_fusion.rest_5_), channel_id=1, source_target_pairs={{0,2},{1,3},{2,0},{3,1},{4,6},{5,7},{6,4},{7,5},{8,10},{9,11},{10,... | collective-permute-start | bytes 3932168 | tf_op jit(solution)/shard_map/ppermute | solution.py:42
  66.1 39.8 %collective-permute-start.13 = (bf16[640,1024]{1,0:T(8,128)(2,1)S(1)}, bf16[640,1024]{1,0:T(8,128)(2,1)S(1)}, u32[]{:S(2)}, u32[]{:S(2)}) collective-permute-start(bf16[640,1024]{1,0:T(8,128)(2,1)S(1)} %constant_dynamic-update-slice_fusion.rest_5_), channel_id=1, source_target_pairs={{0,4},{1,5},{2,6},{3,7},{4,0},{5,1},{6,2},{7,3},{8,12},{9,13},{10,... | collective-permute-start | bytes 3932168 | tf_op jit(solution)/shard_map/ppermute | solution.py:42
  73.2 66.2 %collective-permute-start.16 = (bf16[640,1024]{1,0:T(8,128)(2,1)S(1)}, bf16[640,1024]{1,0:T(8,128)(2,1)S(1)}, u32[]{:S(2)}, u32[]{:S(2)}) collective-permute-start(bf16[640,1024]{1,0:T(8,128)(2,1)S(1)} %constant_dynamic-update-slice_fusion.rest_5_), channel_id=1, source_target_pairs={{0,1},{1,0},{2,3},{3,2},{4,5},{5,4},{6,7},{7,6},{8,9},{9,8},{10,11... | collective-permute-start | bytes 3932168 | tf_op jit(solution)/shard_map/ppermute | solution.py:42
  88.8 52.3 %copy-start.5 = (f32[1024]{0:T(1024)S(1)}, f32[1024]{0:T(1024)}, u32[]{:S(2)}) copy-start(f32[1024]{0:T(1024)} %param.19) | copy-start | bytes 12292
  105.9 30.2 %collective-permute-start.14 = (bf16[320,1024]{1,0:T(8,128)(2,1)S(1)}, bf16[320,1024]{1,0:T(8,128)(2,1)S(1)}, u32[]{:S(2)}, u32[]{:S(2)}) collective-permute-start(bf16[320,1024]{1,0:T(8,128)(2,1)S(1)} %slice.38), channel_id=1, source_target_pairs={{0,4},{1,5},{2,6},{3,7},{4,0},{5,1},{6,2},{7,3},{8,12},{9,13},{10,... | collective-permute-start | bytes 1966088 | tf_op jit(solution)/shard_map/ppermute | solution.py:42
  107.1 30.8 %collective-permute-start.15 = (bf16[320,1024]{1,0:T(8,128)(2,1)S(1)}, bf16[320,1024]{1,0:T(8,128)(2,1)S(1)}, u32[]{:S(2)}, u32[]{:S(2)}) collective-permute-start(bf16[320,1024]{1,0:T(8,128)(2,1)S(1)} %slice.39), channel_id=1, source_target_pairs={{0,2},{1,3},{2,0},{3,1},{4,6},{5,7},{6,4},{7,5},{8,10},{9,11},{10,... | collective-permute-start | bytes 1966088 | tf_op jit(solution)/shard_map/ppermute | solution.py:42
  107.4 33.7 %collective-permute-start.17 = (bf16[640,1024]{1,0:T(8,128)(2,1)S(1)}, bf16[640,1024]{1,0:T(8,128)(2,1)S(1)}, u32[]{:S(2)}, u32[]{:S(2)}) collective-permute-start(bf16[640,1024]{1,0:T(8,128)(2,1)S(1)} %collective-permute-done.12.rest_6_), channel_id=1, source_target_pairs={{0,1},{1,0},{2,3},{3,2},{4,5},{5,4},{6,7},{7,6},{8,9},{9,8},{10,11... | collective-permute-start | bytes 3932168 | tf_op jit(solution)/shard_map/ppermute | solution.py:42
  108.9 32.2 %collective-permute-start.18 = (bf16[640,1024]{1,0:T(8,128)(2,1)S(1)}, bf16[640,1024]{1,0:T(8,128)(2,1)S(1)}, u32[]{:S(2)}, u32[]{:S(2)}) collective-permute-start(bf16[640,1024]{1,0:T(8,128)(2,1)S(1)} %collective-permute-done.13.rest_7_), channel_id=1, source_target_pairs={{0,1},{1,0},{2,3},{3,2},{4,5},{5,4},{6,7},{7,6},{8,9},{9,8},{10,11... | collective-permute-start | bytes 3932168 | tf_op jit(solution)/shard_map/ppermute | solution.py:42
  136.2 3.4 %collective-permute-start.19 = (bf16[320,1024]{1,0:T(8,128)(2,1)S(1)}, bf16[320,1024]{1,0:T(8,128)(2,1)S(1)}, u32[]{:S(2)}, u32[]{:S(2)}) collective-permute-start(bf16[320,1024]{1,0:T(8,128)(2,1)S(1)} %collective-permute-done.14.rest_8_), channel_id=1, source_target_pairs={{0,1},{1,0},{2,3},{3,2},{4,5},{5,4},{6,7},{7,6},{8,9},{9,8},{10,11... | collective-permute-start | bytes 1966088 | tf_op jit(solution)/shard_map/ppermute | solution.py:42
  137.9 3.2 %collective-permute-start.20 = (bf16[320,1024]{1,0:T(8,128)(2,1)S(1)}, bf16[320,1024]{1,0:T(8,128)(2,1)S(1)}, u32[]{:S(2)}, u32[]{:S(2)}) collective-permute-start(bf16[320,1024]{1,0:T(8,128)(2,1)S(1)} %collective-permute-done.15.rest_9_), channel_id=1, source_target_pairs={{0,1},{1,0},{2,3},{3,2},{4,5},{5,4},{6,7},{7,6},{8,9},{9,8},{10,11... | collective-permute-start | bytes 1966088 | tf_op jit(solution)/shard_map/ppermute | solution.py:42
  141.1 26.0 %copy-start.4 = (f32[9,1024]{1,0:T(8,128)S(1)}, f32[9,1024]{1,0:T(8,128)}, u32[]{:S(2)}) copy-start(f32[9,1024]{1,0:T(8,128)} %depth_ref.1) | copy-start | bytes 110596
  141.1 26.0 %copy-start.6 = (f32[1024]{0:T(1024)S(1)}, f32[1024]{0:T(1024)}, u32[]{:S(2)}) copy-start(f32[1024]{0:T(1024)} %param.22) | copy-start | bytes 12292
  141.1 26.0 %copy-start.7 = (f32[1024]{0:T(1024)S(1)}, f32[1024]{0:T(1024)}, u32[]{:S(2)}) copy-start(f32[1024]{0:T(1024)} %param.26) | copy-start | bytes 12292
  167.2 1.6 copy-start.9
Sparse Core Ops, SparseCore 0:
  11.0 156.0 all-gather.2
